TPU v7x, 32 devices: a whole 2x2x4 slice. The times are simulated.
32 devices in a mesh: lon: 8 (over z, y), lat: 2 (over x), lev: 2 (over core).
Axes of the slice: x: 2, y: 2, z: 4, core: 2. Of those that a mesh axis runs over, the one named last changes fastest.
Arguments:
- adjoint_in: float32 [9, 16, 32, 1024], P(None, 'lev', 'lat', 'lon'), may hold values from -6 to 6
- trajectory: bfloat16 [3, 9, 16, 32, 1024], P(None, None, 'lev', 'lat', 'lon'), may hold values from 0.5 to 2
- courant: float32 [2, 16, 32, 1024], P(None, 'lev', 'lat', 'lon'), may hold values from -0.4 to 0.4
- mixing: float32 [16, 32, 1024], P('lev', 'lat', 'lon'), may hold values from 0.02 to 0.2
- coag_rates: float32 [6, 16], replicated, may hold values from 0.02 to 0.2
- settle_speed: float32 [8, 9], replicated, may hold values from 0.01 to 0.2
- settle_class: int32 [16], replicated, may hold values from 0 to 7
- emis_profile: float32 [16], replicated, may hold values from 0.1 to 1
- emis_coef: float32 [9], replicated, may hold values from 0.5 to 2
- land_mask: int32 [32, 1024], P('lat', 'lon'), may hold values 0 or 1
- source_mask: int32 [32, 1024], P('lat', 'lon'), may hold values 0 or 1
Outputs:
- adjoint_out: float32 [9, 16, 32, 1024], P(None, 'lev', 'lat', 'lon')
- emis_grad: float32 [3, 32, 1024], P(None, 'lat', 'lon')
All inputs are finite; a program needn't handle non-finite values. No bound on the sum of `land_mask` or of `source_mask` on one device may be relied on, other than what follows from the above.
Results may differ from a plain program's by a relative error of at most 0.0003.
Values may be sent and summed in bfloat16 or wider, within the bound.
No kernel may reach another device: no remote copies, remote signals or barrier semaphores. Data moves between devices by JAX's collectives and lax.ppermute only.
A program may use at most 64 MiB of HBM per device.

v0:
```python
import jax
import jax.numpy as jnp
from jax import lax
from jax.sharding import PartitionSpec as P


def with_halo(cells, sides, width, closed):
    for axis, dim in sides:
        count = lax.axis_size(axis)
        ends = count if closed else count - 1
        head = lax.slice_in_dim(cells, 0, width, axis=dim)
        tail = lax.slice_in_dim(cells, cells.shape[dim] - width, cells.shape[dim], axis=dim)
        cells = jnp.concatenate(
            [
                lax.ppermute(tail, axis, [(i, (i + 1) % count) for i in range(ends)]),
                cells,
                lax.ppermute(head, axis, [((i + 1) % count, i) for i in range(ends)]),
            ],
            axis=dim,
        )
    return cells


def slab(field, axis, start, length):
    return lax.slice_in_dim(field, start, start + length, axis=axis)


def transport(padded, courant_pad, axis, length):
    courant_wide = courant_pad[None]
    diff_face = slab(padded, axis, 0, length + 3) - slab(padded, axis, 1, length + 3)
    face_speed = slab(courant_wide, axis, 0, length + 3)
    forward_part = jnp.maximum(face_speed, 0.0) * diff_face
    backward_part = jnp.minimum(face_speed, 0.0) * diff_face
    return (
        -1.5 * slab(forward_part, axis, 2, length)
        + 0.5 * slab(forward_part, axis, 3, length)
        - 1.5 * slab(backward_part, axis, 1, length)
        + 0.5 * slab(backward_part, axis, 0, length)
    )


def vertical(padded, mixing_pad, speeds, deposit):
    depth_count = padded.shape[1] - 2
    mixing_below = mixing_pad[:depth_count]
    mixing_above = mixing_pad[1 : depth_count + 1]
    speed_level = speeds[:, :, None, None]
    centre = padded[:, 1 : depth_count + 1]
    return (
        centre * (1.0 - mixing_above - mixing_below - speed_level - deposit)
        + padded[:, :depth_count] * (mixing_below + speed_level)
        + padded[:, 2:] * mixing_above
    )


def coag_increment(state, rates):
    rate_grid = rates[:, :, None, None]
    number = [state[0], state[3], state[6]]
    volume = [state[1], state[4], state[7]]
    moment_six = [state[2], state[5], state[8]]
    pair_rate = {(0, 1): rate_grid[3], (0, 2): rate_grid[4], (1, 2): rate_grid[5]}
    outputs = []
    for mode_index in range(3):
        d_number = -rate_grid[mode_index] * number[mode_index] * number[mode_index]
        d_volume = jnp.zeros_like(number[mode_index])
        d_moment = rate_grid[mode_index] * volume[mode_index] * volume[mode_index]
        for other_mode in range(3):
            if other_mode > mode_index:
                pair = pair_rate[mode_index, other_mode]
                d_number = d_number - pair * number[mode_index] * number[other_mode]
                d_volume = d_volume - pair * volume[mode_index] * number[other_mode]
                d_moment = d_moment - pair * moment_six[mode_index] * number[other_mode]
            if other_mode < mode_index:
                pair = pair_rate[other_mode, mode_index]
                d_volume = d_volume + pair * volume[other_mode] * number[mode_index]
                d_moment = d_moment + pair * (
                    moment_six[other_mode] * number[mode_index]
                    + 2.0 * volume[other_mode] * volume[mode_index]
                )
        outputs.extend([d_number, d_volume, d_moment])
    return jnp.stack(outputs)


def coag_adjoint(adjoint, state, rates):
    primal_out, pullback = jax.vjp(lambda value: coag_increment(value, rates), state)
    return adjoint + pullback(adjoint)[0]


def emission_part(adjoint, profile, emis_coef, source):
    weighted = adjoint * (emis_coef[:, None, None, None] * profile[None, :, None, None])
    per_tracer = jnp.sum(weighted, axis=1)
    per_mode = jnp.sum(per_tracer.reshape(3, 3, per_tracer.shape[1], per_tracer.shape[2]), axis=1)
    return per_mode * source


def sides(field, lat_index, row_count, lat_count):
    lon_pad = with_halo(field, (("lon", 3),), 2, True)
    lat_pad = with_halo(field, (("lat", 2),), 2, False)
    return (lon_pad, lat_pad)


def planes(field):
    return with_halo(field, (("lev", 1),), 1, False)


def run_split(
    adjoint_in,
    trajectory,
    winds,
    mixing_top,
    coag_rates,
    speeds_all,
    emis_profile,
    emis_coef,
    dep_rows,
    source,
):
    depth_count = adjoint_in.shape[1]
    row_count = adjoint_in.shape[2]
    col_count = adjoint_in.shape[3]
    lev_index = lax.axis_index("lev")
    lat_index = lax.axis_index("lat")
    lat_count = lax.axis_size("lat")
    level_global = lev_index * depth_count + jnp.arange(depth_count, dtype=jnp.int32)
    level_start = lev_index * depth_count
    rates_own = lax.dynamic_slice_in_dim(coag_rates, level_start, depth_count, 1)
    profile_own = lax.dynamic_slice_in_dim(emis_profile, level_start, depth_count, 0)
    wind_lon, wind_lat = sides(winds, lat_index, row_count, lat_count)
    east_pad = wind_lon[0]
    north_pad = wind_lat[1]
    mixing_pad = planes(mixing_top[None])[0]
    speeds_used = lax.dynamic_slice_in_dim(speeds_all, level_start, depth_count, 1)
    surface = (level_global == 0).astype(jnp.float32)
    deposit = dep_rows[None] * surface[:, None, None]
    adjoint = adjoint_in
    emis_grad = jnp.zeros((3, row_count, col_count), jnp.float32)
    for step_index in range(trajectory.shape[0] - 1, -1, -1):
        emis_grad = emis_grad + emission_part(adjoint, profile_own, emis_coef, source)
        adjoint = coag_adjoint(adjoint, trajectory[step_index].astype(jnp.float32), rates_own)
        adjoint = vertical(planes(adjoint), mixing_pad, speeds_used, deposit)
        lon_pad, lat_pad = sides(adjoint, lat_index, row_count, lat_count)
        adjoint = (
            adjoint
            + transport(lon_pad, east_pad, 3, col_count)
            + transport(lat_pad, north_pad, 2, row_count)
        )
    emis_grad = lax.psum(emis_grad, "lev")
    return (adjoint, emis_grad)


def shards(
    adjoint_in,
    trajectory,
    courant,
    mixing,
    coag_rates,
    settle_speed,
    settle_class,
    emis_profile,
    emis_coef,
    land_mask,
    source_mask,
):
    depth_count = adjoint_in.shape[1]
    row_count = adjoint_in.shape[2]
    lev_index = lax.axis_index("lev")
    lat_index = lax.axis_index("lat")
    lat_count = lax.axis_size("lat")
    level_total = settle_class.shape[0]
    row_global = lat_index * row_count + jnp.arange(row_count, dtype=jnp.int32)
    top_row = (row_global == row_count * lat_count - 1)[None, :, None]
    winds = jnp.stack([courant[0], jnp.where(top_row, 0.0, courant[1])])
    level_global = lev_index * depth_count + jnp.arange(depth_count, dtype=jnp.int32)
    mixing_top = jnp.where((level_global == level_total - 1)[:, None, None], 0.0, mixing)
    choose = (
        settle_class[:, None] == jnp.arange(settle_speed.shape[0], dtype=jnp.int32)[None, :]
    ).astype(jnp.float32)
    speeds_all = jnp.dot(choose, settle_speed, precision=lax.Precision.HIGHEST).T
    dep_rows = 0.1 + 0.3 * land_mask.astype(jnp.float32)
    source = source_mask.astype(jnp.float32)
    return run_split(
        adjoint_in,
        trajectory,
        winds,
        mixing_top,
        coag_rates,
        speeds_all,
        emis_profile,
        emis_coef,
        dep_rows,
        source,
    )


def solution(mesh):
    return jax.shard_map(
        shards,
        mesh=mesh,
        in_specs=(
            P(None, "lev", "lat", "lon"),
            P(None, None, "lev", "lat", "lon"),
            P(None, "lev", "lat", "lon"),
            P("lev", "lat", "lon"),
            P(),
            P(),
            P(),
            P(),
            P(),
            P("lat", "lon"),
            P("lat", "lon"),
        ),
        out_specs=(P(None, "lev", "lat", "lon"), P(None, "lat", "lon")),
        check_vma=False,
    )
```

profile of v0, /device:TPU:0, one launch (start us, length us, event | category | flops | bytes accessed | tf_op | source)
XLA Modules:
  0.0 121.9 jit_solution(9505242472145461022)
XLA Ops:
  0.7 0.8 constant_dynamic-slice_fusion
  1.5 1.4 %slice_convert_fusion = (f32[1,9,8,16,128]{4,3,2,1,0:T(8,128)S(1)}, f32[1,9,8,16,128]{4,3,2,1,0:T(8,128)S(1)}, f32[1,9,8,16,128]{4,3,2,1,0:T(8,128)S(1)}) fusion(bf16[3,9,8,16,128]{4,3,2,1,0:T(8,128)(2,1)} %param.12), kind=kLoop, calls=%fused_computation.97 | loop fusion | flops 442368 | bytes 2654208 | tf_op jit(solution)/shard_map/convert_element_type | solution.py:138
  3.8 0.7 fusion.59
  4.4 2.3 %collective-permute-start.1 = (f32[9,1,16,128]{3,2,1,0:T(8,128)}, f32[9,1,16,128]{3,2,1,0:T(8,128)S(1)}, u32[]{:S(2)}, u32[]{:S(2)}) collective-permute-start(f32[9,1,16,128]{3,2,1,0:T(8,128)} %get-tuple-element.54), channel_id=1, source_target_pairs={{0,1},{2,3},{4,5},{6,7},{8,9},{10,11},{12,13},{14,15},{16,17},{18,... | collective-permute-start | bytes 221192 | tf_op jit(solution)/shard_map/ppermute | solution.py:15
  6.8 1.3 %collective-permute-start.2 = (f32[9,1,16,128]{3,2,1,0:T(8,128)}, f32[9,1,16,128]{3,2,1,0:T(8,128)S(1)}, u32[]{:S(2)}, u32[]{:S(2)}) collective-permute-start(f32[9,1,16,128]{3,2,1,0:T(8,128)} %get-tuple-element.55), channel_id=1, source_target_pairs={{1,0},{3,2},{5,4},{7,6},{9,8},{11,10},{13,12},{15,14},{17,16},{19,... | collective-permute-start | bytes 221192 | tf_op jit(solution)/shard_map/ppermute | solution.py:17
  8.2 3.0 %collective-permute-start = (f32[1,1,16,128]{3,2,1,0:T(8,128)S(1)}, f32[1,1,16,128]{3,2,1,0:T(8,128)S(1)}, u32[]{:S(2)}, u32[]{:S(2)}) collective-permute-start(f32[1,1,16,128]{3,2,1,0:T(8,128)S(1)} %slice.569), channel_id=1, source_target_pairs={{0,1},{2,3},{4,5},{6,7},{8,9},{10,11},{12,13},{14,15},{16,17},{18,... | collective-permute-start | bytes 24584 | tf_op jit(solution)/shard_map/ppermute | solution.py:15
  11.4 2.4 %collective-permute-start.3 = (f32[2,8,16,2]{3,2,1,0:T(8,128)S(1)}, f32[2,8,16,2]{3,2,1,0:T(8,128)S(1)}, u32[]{:S(2)}, u32[]{:S(2)}) collective-permute-start(f32[2,8,16,2]{3,2,1,0:T(8,128)S(1)} %get-tuple-element.60), channel_id=1, source_target_pairs={{0,4},{4,8},{8,12},{12,16},{16,20},{20,24},{24,28},{28,0},{1,5},{5... | collective-permute-start | bytes 6152 | tf_op jit(solution)/shard_map/ppermute | solution.py:15
  13.8 3.1 %collective-permute-start.4 = (f32[2,8,16,2]{3,2,1,0:T(8,128)S(1)}, f32[2,8,16,2]{3,2,1,0:T(8,128)S(1)}, u32[]{:S(2)}, u32[]{:S(2)}) collective-permute-start(f32[2,8,16,2]{3,2,1,0:T(8,128)S(1)} %get-tuple-element.61), channel_id=1, source_target_pairs={{4,0},{8,4},{12,8},{16,12},{20,16},{24,20},{28,24},{0,28},{5,1},{9... | collective-permute-start | bytes 6152 | tf_op jit(solution)/shard_map/ppermute | solution.py:17
  17.5 0.7 dynamic_slice.11
  18.1 1.9 %collective-permute-done.3 = f32[2,8,16,2]{3,2,1,0:T(8,128)S(1)} collective-permute-done((f32[2,8,16,2]{3,2,1,0:T(8,128)S(1)}, f32[2,8,16,2]{3,2,1,0:T(8,128)S(1)}, u32[]{:S(2)}, u32[]{:S(2)}) %collective-permute-start.3) | collective-permute-done | bytes 2080 | tf_op jit(solution)/shard_map/ppermute | solution.py:15
  20.0 3.4 %collective-permute-start.7 = (f32[2,8,2,128]{3,2,1,0:T(2,128)S(1)}, f32[2,8,2,128]{3,2,1,0:T(2,128)S(1)}, u32[]{:S(2)}, u32[]{:S(2)}) collective-permute-start(f32[2,8,2,128]{3,2,1,0:T(2,128)S(1)} %get-tuple-element.62), channel_id=1, source_target_pairs={{0,2},{1,3},{4,6},{5,7},{8,10},{9,11},{12,14},{13,15},{16,18},{17,... | collective-permute-start | bytes 49160 | tf_op jit(solution)/shard_map/ppermute | solution.py:15
  23.4 1.3 %collective-permute-start.8 = (f32[2,8,2,128]{3,2,1,0:T(2,128)S(1)}, f32[2,8,2,128]{3,2,1,0:T(2,128)S(1)}, u32[]{:S(2)}, u32[]{:S(2)}) collective-permute-start(f32[2,8,2,128]{3,2,1,0:T(2,128)S(1)} %get-tuple-element.63), channel_id=1, source_target_pairs={{2,0},{3,1},{6,4},{7,5},{10,8},{11,9},{14,12},{15,13},{18,16},{19,... | collective-permute-start | bytes 49160 | tf_op jit(solution)/shard_map/ppermute | solution.py:17
  24.9 0.7 fusion.35
  25.6 3.4 %collective-permute-done.8 = f32[2,8,2,128]{3,2,1,0:T(2,128)S(1)} collective-permute-done((f32[2,8,2,128]{3,2,1,0:T(2,128)S(1)}, f32[2,8,2,128]{3,2,1,0:T(2,128)S(1)}, u32[]{:S(2)}, u32[]{:S(2)}) %collective-permute-start.8) | collective-permute-done | bytes 16416 | tf_op jit(solution)/shard_map/ppermute | solution.py:17
  29.1 0.7 maximum_bitcast_fusion.1
  29.8 0.6 copy-done.16
  30.4 1.1 fusion.1
  31.6 1.2 fusion.57
  32.8 2.2 %copy.101 = f32[9,8,16,2]{2,1,3,0:T(8,128)} copy(f32[9,8,16,2]{3,2,1,0:T(8,128)} %get-tuple-element.50) | data formatting | bytes 18432 | tf_op jit(solution)/shard_map/slice | solution.py:12
  35.0 1.6 %collective-permute-start.5 = (f32[9,8,16,2]{2,1,3,0:T(8,128)}, f32[9,8,16,2]{2,1,3,0:T(8,128)}, u32[]{:S(2)}, u32[]{:S(2)}) collective-permute-start(f32[9,8,16,2]{2,1,3,0:T(8,128)} %copy.101), channel_id=1, source_target_pairs={{0,4},{4,8},{8,12},{12,16},{16,20},{20,24},{24,28},{28,0},{1,5},{5... | collective-permute-start | bytes 27656 | tf_op jit(solution)/shard_map/ppermute | solution.py:15
  36.5 2.2 %copy.102 = f32[9,8,16,2]{2,1,3,0:T(8,128)} copy(f32[9,8,16,2]{3,2,1,0:T(8,128)} %get-tuple-element.51) | data formatting | bytes 18432 | tf_op jit(solution)/shard_map/slice | solution.py:11
  38.7 3.1 %collective-permute-start.6 = (f32[9,8,16,2]{2,1,3,0:T(8,128)}, f32[9,8,16,2]{2,1,3,0:T(8,128)}, u32[]{:S(2)}, u32[]{:S(2)}) collective-permute-start(f32[9,8,16,2]{2,1,3,0:T(8,128)} %copy.102), channel_id=1, source_target_pairs={{4,0},{8,4},{12,8},{16,12},{20,16},{24,20},{28,24},{0,28},{5,1},{9... | collective-permute-start | bytes 27656 | tf_op jit(solution)/shard_map/ppermute | solution.py:17
  41.9 0.6 copy.105
  42.6 2.3 %collective-permute-start.9 = (f32[9,8,2,128]{3,1,2,0:T(8,128)}, f32[9,8,2,128]{3,1,2,0:T(8,128)}, u32[]{:S(2)}, u32[]{:S(2)}) collective-permute-start(f32[9,8,2,128]{3,1,2,0:T(8,128)} %copy.105), channel_id=1, source_target_pairs={{0,2},{1,3},{4,6},{5,7},{8,10},{9,11},{12,14},{13,15},{16,18},{17,... | collective-permute-start | bytes 221192 | tf_op jit(solution)/shard_map/ppermute | solution.py:15
  44.8 0.6 copy.106
  45.5 1.3 %collective-permute-start.10 = (f32[9,8,2,128]{3,1,2,0:T(8,128)}, f32[9,8,2,128]{3,1,2,0:T(8,128)}, u32[]{:S(2)}, u32[]{:S(2)}) collective-permute-start(f32[9,8,2,128]{3,1,2,0:T(8,128)} %copy.106), channel_id=1, source_target_pairs={{2,0},{3,1},{6,4},{7,5},{10,8},{11,9},{14,12},{15,13},{18,16},{19,... | collective-permute-start | bytes 221192 | tf_op jit(solution)/shard_map/ppermute | solution.py:17
  46.7 2.2 %copy.103 = f32[9,8,16,2]{3,2,1,0:T(8,128)} copy(f32[9,8,16,2]{2,1,3,0:T(8,128)} %collective-permute-done.5) | data formatting | bytes 18432 | tf_op jit(solution)/shard_map/ppermute | solution.py:15
  49.0 2.2 %copy.104 = f32[9,8,16,2]{3,2,1,0:T(8,128)} copy(f32[9,8,16,2]{2,1,3,0:T(8,128)} %collective-permute-done.6) | data formatting | bytes 18432 | tf_op jit(solution)/shard_map/ppermute | solution.py:17
  51.2 1.8 %pad_maximum_fusion = f32[9,8,16,132]{3,2,1,0:T(8,128)S(1)} fusion(f32[9,8,16,2]{3,2,1,0:T(8,128)} %copy.104, f32[9,8,16,128]{3,2,1,0:T(8,128)S(1)} %fusion.1, f32[9,8,16,2]{3,2,1,0:T(8,128)} %copy.103), kind=kLoop, calls=%fused_computation.3 | loop fusion | flops 304128 | bytes 1216512 | tf_op jit(solution)/shard_map/concatenate | solution.py:13
  53.4 1.0 copy.107
  54.4 0.9 copy.108
  55.7 0.7 copy-done.17
  56.4 0.7 fusion.25
  58.3 1.3 %collective-permute-start.11 = (f32[9,1,16,128]{3,2,1,0:T(8,128)S(1)}, f32[9,1,16,128]{3,2,1,0:T(8,128)S(1)}, u32[]{:S(2)}, u32[]{:S(2)}) collective-permute-start(f32[9,1,16,128]{3,2,1,0:T(8,128)S(1)} %get-tuple-element.48), channel_id=1, source_target_pairs={{0,1},{2,3},{4,5},{6,7},{8,9},{10,11},{12,13},{14,15},{16,17},{18,... | collective-permute-start | bytes 221192 | tf_op jit(solution)/shard_map/ppermute | solution.py:15
  59.6 1.3 %collective-permute-start.12 = (f32[9,1,16,128]{3,2,1,0:T(8,128)S(1)}, f32[9,1,16,128]{3,2,1,0:T(8,128)S(1)}, u32[]{:S(2)}, u32[]{:S(2)}) collective-permute-start(f32[9,1,16,128]{3,2,1,0:T(8,128)S(1)} %get-tuple-element.49), channel_id=1, source_target_pairs={{1,0},{3,2},{5,4},{7,6},{9,8},{11,10},{13,12},{15,14},{17,16},{19,... | collective-permute-start | bytes 221192 | tf_op jit(solution)/shard_map/ppermute | solution.py:17
  61.0 1.7 %collective-permute-done.12 = f32[9,1,16,128]{3,2,1,0:T(8,128)S(1)} collective-permute-done((f32[9,1,16,128]{3,2,1,0:T(8,128)S(1)}, f32[9,1,16,128]{3,2,1,0:T(8,128)S(1)}, u32[]{:S(2)}, u32[]{:S(2)}) %collective-permute-start.12) | collective-permute-done | bytes 73760 | tf_op jit(solution)/shard_map/ppermute | solution.py:17
  63.0 1.2 fusion.54
  64.2 2.2 %copy.109 = f32[9,8,16,2]{2,1,3,0:T(8,128)} copy(f32[9,8,16,2]{3,2,1,0:T(8,128)} %get-tuple-element.44) | data formatting | bytes 18432 | tf_op jit(solution)/shard_map/slice | solution.py:12
  66.4 2.2 %copy.110 = f32[9,8,16,2]{2,1,3,0:T(8,128)} copy(f32[9,8,16,2]{3,2,1,0:T(8,128)} %get-tuple-element.45) | data formatting | bytes 18432 | tf_op jit(solution)/shard_map/slice | solution.py:11
  68.6 4.7 %collective-permute-start.14 = (f32[9,8,16,2]{2,1,3,0:T(8,128)}, f32[9,8,16,2]{2,1,3,0:T(8,128)}, u32[]{:S(2)}, u32[]{:S(2)}) collective-permute-start(f32[9,8,16,2]{2,1,3,0:T(8,128)} %copy.110), channel_id=1, source_target_pairs={{4,0},{8,4},{12,8},{16,12},{20,16},{24,20},{28,24},{0,28},{5,1},{9... | collective-permute-start | bytes 27656 | tf_op jit(solution)/shard_map/ppermute | solution.py:17
  73.4 0.6 copy.113
  74.0 5.8 %collective-permute-start.15 = (f32[9,8,2,128]{3,1,2,0:T(8,128)}, f32[9,8,2,128]{3,1,2,0:T(8,128)}, u32[]{:S(2)}, u32[]{:S(2)}) collective-permute-start(f32[9,8,2,128]{3,1,2,0:T(8,128)} %copy.113), channel_id=1, source_target_pairs={{0,2},{1,3},{4,6},{5,7},{8,10},{9,11},{12,14},{13,15},{16,18},{17,... | collective-permute-start | bytes 221192 | tf_op jit(solution)/shard_map/ppermute | solution.py:15
  79.8 0.6 copy.114
  80.4 1.3 %collective-permute-start.16 = (f32[9,8,2,128]{3,1,2,0:T(8,128)}, f32[9,8,2,128]{3,1,2,0:T(8,128)}, u32[]{:S(2)}, u32[]{:S(2)}) collective-permute-start(f32[9,8,2,128]{3,1,2,0:T(8,128)} %copy.114), channel_id=1, source_target_pairs={{2,0},{3,1},{6,4},{7,5},{10,8},{11,9},{14,12},{15,13},{18,16},{19,... | collective-permute-start | bytes 221192 | tf_op jit(solution)/shard_map/ppermute | solution.py:17
  81.7 2.2 %copy.111 = f32[9,8,16,2]{3,2,1,0:T(8,128)} copy(f32[9,8,16,2]{2,1,3,0:T(8,128)} %collective-permute-done.13) | data formatting | bytes 18432 | tf_op jit(solution)/shard_map/ppermute | solution.py:15
  84.0 2.2 %copy.112 = f32[9,8,16,2]{3,2,1,0:T(8,128)} copy(f32[9,8,16,2]{2,1,3,0:T(8,128)} %collective-permute-done.14) | data formatting | bytes 18432 | tf_op jit(solution)/shard_map/ppermute | solution.py:17
  86.1 1.8 %pad_maximum_fusion.1 = f32[9,8,16,132]{3,2,1,0:T(8,128)S(1)} fusion(f32[9,8,16,2]{3,2,1,0:T(8,128)} %copy.112, f32[9,8,16,128]{3,2,1,0:T(8,128)S(1)} %fusion.3, f32[9,8,16,2]{3,2,1,0:T(8,128)} %copy.111), kind=kLoop, calls=%fused_computation.4 | loop fusion | flops 304128 | bytes 1216512 | tf_op jit(solution)/shard_map/concatenate | solution.py:13
  88.4 1.0 copy.115
  89.4 0.9 copy.116
  90.8 0.6 copy-done.10
  91.4 1.6 %multiply_reduce_fusion.1 = (f32[9,16,128]{2,1,0:T(8,128)}, f32[9,16,128]{2,1,0:T(8,128)}, f32[9,16,128]{2,1,0:T(8,128)}, f32[9,8,16,128]{3,2,1,0:T(8,128)S(1)}) fusion(f32[9,8,16,128]{3,2,1,0:T(8,128)S(1)} %fusion.25, f32[9,8]{1,0:T(8,128)S(1)} %broadcast_multiply_fusion.13, f32[9,8,16,128]{3,2,1,0:T(8,128)S(1)} %copy-done.1, ...), kind=kLoop, calls=%fused_computation.79 | loop fusion | flops 4663296 | bytes 7709248 | tf_op jit(solution)/shard_map/reduce_sum | solution.py:90
  94.5 1.3 %collective-permute-start.17 = (f32[9,1,16,128]{3,2,1,0:T(8,128)S(1)}, f32[9,1,16,128]{3,2,1,0:T(8,128)S(1)}, u32[]{:S(2)}, u32[]{:S(2)}) collective-permute-start(f32[9,1,16,128]{3,2,1,0:T(8,128)S(1)} %get-tuple-element.42), channel_id=1, source_target_pairs={{0,1},{2,3},{4,5},{6,7},{8,9},{10,11},{12,13},{14,15},{16,17},{18,... | collective-permute-start | bytes 221192 | tf_op jit(solution)/shard_map/ppermute | solution.py:15
  95.8 1.3 %collective-permute-start.18 = (f32[9,1,16,128]{3,2,1,0:T(8,128)S(1)}, f32[9,1,16,128]{3,2,1,0:T(8,128)S(1)}, u32[]{:S(2)}, u32[]{:S(2)}) collective-permute-start(f32[9,1,16,128]{3,2,1,0:T(8,128)S(1)} %get-tuple-element.43), channel_id=1, source_target_pairs={{1,0},{3,2},{5,4},{7,6},{9,8},{11,10},{13,12},{15,14},{17,16},{19,... | collective-permute-start | bytes 221192 | tf_op jit(solution)/shard_map/ppermute | solution.py:17
  97.1 5.0 %psum.7 = f32[3,16,128]{2,1,0:T(8,128)} all-reduce(f32[3,16,128]{2,1,0:T(8,128)S(1)} %add_multiply_fusion.3), channel_id=1, replica_groups=mesh['lon'=8,'lat'=2,'lev'=2] {'lev'}, use_global_device_ids=true, to_apply=%region_6.7 | all-reduce | flops 6144 | bytes 49152 | tf_op jit(solution)/shard_map/psum | solution.py:146
  102.5 0.5 copy.117
  103.2 0.5 copy.118
  103.7 4.7 %collective-permute-start.20 = (f32[9,8,16,2]{2,1,3,0:T(8,128)S(1)}, f32[9,8,16,2]{2,1,3,0:T(8,128)}, u32[]{:S(2)}, u32[]{:S(2)}) collective-permute-start(f32[9,8,16,2]{2,1,3,0:T(8,128)S(1)} %copy.118), channel_id=1, source_target_pairs={{4,0},{8,4},{12,8},{16,12},{20,16},{24,20},{28,24},{0,28},{5,1},{9... | collective-permute-start | bytes 27656 | tf_op jit(solution)/shard_map/ppermute | solution.py:17
  108.5 5.2 %collective-permute-start.21 = (f32[9,8,2,128]{3,1,2,0:T(8,128)S(1)}, f32[9,8,2,128]{3,1,2,0:T(8,128)S(1)}, u32[]{:S(2)}, u32[]{:S(2)}) collective-permute-start(f32[9,8,2,128]{3,1,2,0:T(8,128)S(1)} %copy.121), channel_id=1, source_target_pairs={{0,2},{1,3},{4,6},{5,7},{8,10},{9,11},{12,14},{13,15},{16,18},{17,... | collective-permute-start | bytes 221192 | tf_op jit(solution)/shard_map/ppermute | solution.py:15
  113.7 1.3 %collective-permute-start.22 = (f32[9,8,2,128]{3,1,2,0:T(8,128)S(1)}, f32[9,8,2,128]{3,1,2,0:T(8,128)S(1)}, u32[]{:S(2)}, u32[]{:S(2)}) collective-permute-start(f32[9,8,2,128]{3,1,2,0:T(8,128)S(1)} %copy.122), channel_id=1, source_target_pairs={{2,0},{3,1},{6,4},{7,5},{10,8},{11,9},{14,12},{15,13},{18,16},{19,... | collective-permute-start | bytes 221192 | tf_op jit(solution)/shard_map/ppermute | solution.py:17
  115.0 0.5 copy.119
  115.5 1.4 %copy.120 = f32[9,8,16,2]{3,2,1,0:T(8,128)S(1)} copy(f32[9,8,16,2]{2,1,3,0:T(8,128)} %collective-permute-done.20) | data formatting | bytes 18432 | tf_op jit(solution)/shard_map/ppermute | solution.py:17
  116.9 0.5 pad_maximum_fusion.2
  117.9 2.0 %collective-permute-done.22 = f32[9,8,2,128]{3,1,2,0:T(8,128)S(1)} collective-permute-done((f32[9,8,2,128]{3,1,2,0:T(8,128)S(1)}, f32[9,8,2,128]{3,1,2,0:T(8,128)S(1)}, u32[]{:S(2)}, u32[]{:S(2)}) %collective-permute-start.22) | collective-permute-done | bytes 73760 | tf_op jit(solution)/shard_map/ppermute | solution.py:17
  120.4 1.6 %fusion.7 = f32[9,8,16,128]{3,2,1,0:T(8,128)} fusion(f32[9,8,19,128]{3,2,1,0:T(8,128)S(1)} %get-tuple-element.30, f32[9,8,19,128]{3,2,1,0:T(8,128)S(1)} %get-tuple-element.29, f32[9,8,16,131]{3,2,1,0:T(8,128)S(1)} %get-tuple-element.24, f32[9,8,16,131]{3,2,1,0:T(8,128)S(1)} %get-tuple-element.23, f32[8,16,128]{2,1,0:T(8,128)S(1)} %broadcast_select_fusion, ...), kind=kLoop, calls=%fused_computation.23 | loop fusion | flops 3833856 | bytes 6308128 | tf_op jit(solution)/shard_map/add | solution.py:142
  (154 shorter events, 7.9 us)
Async XLA Ops:
  0.6 16.5 %copy-start = (f32[8,9]{1,0:T(8,128)S(1)}, f32[8,9]{1,0:T(8,128)}, u32[]{:S(2)}) copy-start(f32[8,9]{1,0:T(8,128)} %param.16) | copy-start | bytes 868
  1.4 1.5 %copy-start.29 = (f32[8]{0:T(128)}, f32[8]{0:T(128)S(1)}, u32[]{:S(2)}) copy-start(f32[8]{0:T(128)S(1)} %get-tuple-element.70) | copy-start | bytes 100
  1.4 1.7 %copy-start.27 = (f32[8]{0:T(128)}, f32[8]{0:T(128)S(1)}, u32[]{:S(2)}) copy-start(f32[8]{0:T(128)S(1)} %get-tuple-element.69) | copy-start | bytes 100
  1.4 1.6 %copy-start.25 = (f32[8]{0:T(128)}, f32[8]{0:T(128)S(1)}, u32[]{:S(2)}) copy-start(f32[8]{0:T(128)S(1)} %get-tuple-element.76) | copy-start | bytes 100
  1.4 2.0 %copy-start.23 = (f32[8]{0:T(128)}, f32[8]{0:T(128)S(1)}, u32[]{:S(2)}) copy-start(f32[8]{0:T(128)S(1)} %get-tuple-element.75) | copy-start | bytes 100
  1.5 1.4 %copy-start.1 = (f32[9,8,16,128]{3,2,1,0:T(8,128)S(1)}, f32[9,8,16,128]{3,2,1,0:T(8,128)}, u32[]{:S(2)}) copy-start(f32[9,8,16,128]{3,2,1,0:T(8,128)} %param.11) | copy-start | bytes 1769476
  3.6 4.5 %copy-start.8 = (f32[8,16,128]{2,1,0:T(8,128)S(1)}, f32[8,16,128]{2,1,0:T(8,128)}, u32[]{:S(2)}) copy-start(f32[8,16,128]{2,1,0:T(8,128)} %param.14) | copy-start | bytes 196612
  3.6 7.6 %copy-start.20 = (f32[2,8,16,128]{3,2,1,0:T(8,128)S(1)}, f32[2,8,16,128]{3,2,1,0:T(8,128)}, u32[]{:S(2)}) copy-start(f32[2,8,16,128]{3,2,1,0:T(8,128)} %param.13) | copy-start | bytes 393220
  3.6 13.4 %copy-start.21 = (s32[16,128]{1,0:T(8,128)S(1)}, s32[16,128]{1,0:T(8,128)}, u32[]{:S(2)}) copy-start(s32[16,128]{1,0:T(8,128)} %param.20) | copy-start | bytes 24580
  3.6 13.4 %copy-start.34 = (s32[16]{0:T(128)S(1)}, s32[16]{0:T(128)}, u32[]{:S(2)}) copy-start(s32[16]{0:T(128)} %param.17) | copy-start | bytes 196
  3.7 13.7 %copy-start.35 = (f32[16]{0:T(128)S(1)}, f32[16]{0:T(128)}, u32[]{:S(2)}) copy-start(f32[16]{0:T(128)} %param.18) | copy-start | bytes 196
  4.4 25.4 %collective-permute-start.1 = (f32[9,1,16,128]{3,2,1,0:T(8,128)}, f32[9,1,16,128]{3,2,1,0:T(8,128)S(1)}, u32[]{:S(2)}, u32[]{:S(2)}) collective-permute-start(f32[9,1,16,128]{3,2,1,0:T(8,128)} %get-tuple-element.54), channel_id=1, source_target_pairs={{0,1},{2,3},{4,5},{6,7},{8,9},{10,11},{12,13},{14,15},{16,17},{18,... | collective-permute-start | bytes 221192 | tf_op jit(solution)/shard_map/ppermute | solution.py:15
  6.8 23.0 %collective-permute-start.2 = (f32[9,1,16,128]{3,2,1,0:T(8,128)}, f32[9,1,16,128]{3,2,1,0:T(8,128)S(1)}, u32[]{:S(2)}, u32[]{:S(2)}) collective-permute-start(f32[9,1,16,128]{3,2,1,0:T(8,128)} %get-tuple-element.55), channel_id=1, source_target_pairs={{1,0},{3,2},{5,4},{7,6},{9,8},{11,10},{13,12},{15,14},{17,16},{19,... | collective-permute-start | bytes 221192 | tf_op jit(solution)/shard_map/ppermute | solution.py:17
  8.1 8.9 %copy-start.31 = (pred[8]{0:T(512)(128)(4,1)}, pred[8]{0:T(512)(128)(4,1)S(1)}, u32[]{:S(2)}) copy-start(pred[8]{0:T(512)(128)(4,1)S(1)} %fusion.46) | copy-start | bytes 28
  8.2 16.7 %collective-permute-start = (f32[1,1,16,128]{3,2,1,0:T(8,128)S(1)}, f32[1,1,16,128]{3,2,1,0:T(8,128)S(1)}, u32[]{:S(2)}, u32[]{:S(2)}) collective-permute-start(f32[1,1,16,128]{3,2,1,0:T(8,128)S(1)} %slice.569), channel_id=1, source_target_pairs={{0,1},{2,3},{4,5},{6,7},{8,9},{10,11},{12,13},{14,15},{16,17},{18,... | collective-permute-start | bytes 24584 | tf_op jit(solution)/shard_map/ppermute | solution.py:15
  11.4 8.6 %collective-permute-start.3 = (f32[2,8,16,2]{3,2,1,0:T(8,128)S(1)}, f32[2,8,16,2]{3,2,1,0:T(8,128)S(1)}, u32[]{:S(2)}, u32[]{:S(2)}) collective-permute-start(f32[2,8,16,2]{3,2,1,0:T(8,128)S(1)} %get-tuple-element.60), channel_id=1, source_target_pairs={{0,4},{4,8},{8,12},{12,16},{16,20},{20,24},{24,28},{28,0},{1,5},{5... | collective-permute-start | bytes 6152 | tf_op jit(solution)/shard_map/ppermute | solution.py:15
  13.8 9.6 %collective-permute-start.4 = (f32[2,8,16,2]{3,2,1,0:T(8,128)S(1)}, f32[2,8,16,2]{3,2,1,0:T(8,128)S(1)}, u32[]{:S(2)}, u32[]{:S(2)}) collective-permute-start(f32[2,8,16,2]{3,2,1,0:T(8,128)S(1)} %get-tuple-element.61), channel_id=1, source_target_pairs={{4,0},{8,4},{12,8},{16,12},{20,16},{24,20},{28,24},{0,28},{5,1},{9... | collective-permute-start | bytes 6152 | tf_op jit(solution)/shard_map/ppermute | solution.py:17
  20.0 5.6 %collective-permute-start.7 = (f32[2,8,2,128]{3,2,1,0:T(2,128)S(1)}, f32[2,8,2,128]{3,2,1,0:T(2,128)S(1)}, u32[]{:S(2)}, u32[]{:S(2)}) collective-permute-start(f32[2,8,2,128]{3,2,1,0:T(2,128)S(1)} %get-tuple-element.62), channel_id=1, source_target_pairs={{0,2},{1,3},{4,6},{5,7},{8,10},{9,11},{12,14},{13,15},{16,18},{17,... | collective-permute-start | bytes 49160 | tf_op jit(solution)/shard_map/ppermute | solution.py:15
  23.4 5.6 %collective-permute-start.8 = (f32[2,8,2,128]{3,2,1,0:T(2,128)S(1)}, f32[2,8,2,128]{3,2,1,0:T(2,128)S(1)}, u32[]{:S(2)}, u32[]{:S(2)}) collective-permute-start(f32[2,8,2,128]{3,2,1,0:T(2,128)S(1)} %get-tuple-element.63), channel_id=1, source_target_pairs={{2,0},{3,1},{6,4},{7,5},{10,8},{11,9},{14,12},{15,13},{18,16},{19,... | collective-permute-start | bytes 49160 | tf_op jit(solution)/shard_map/ppermute | solution.py:17
  29.8 0.6 copy-start.16
  29.8 0.7 copy-start.18
  35.0 11.8 %collective-permute-start.5 = (f32[9,8,16,2]{2,1,3,0:T(8,128)}, f32[9,8,16,2]{2,1,3,0:T(8,128)}, u32[]{:S(2)}, u32[]{:S(2)}) collective-permute-start(f32[9,8,16,2]{2,1,3,0:T(8,128)} %copy.101), channel_id=1, source_target_pairs={{0,4},{4,8},{8,12},{12,16},{16,20},{20,24},{24,28},{28,0},{1,5},{5... | collective-permute-start | bytes 27656 | tf_op jit(solution)/shard_map/ppermute | solution.py:15
  38.7 10.2 %collective-permute-start.6 = (f32[9,8,16,2]{2,1,3,0:T(8,128)}, f32[9,8,16,2]{2,1,3,0:T(8,128)}, u32[]{:S(2)}, u32[]{:S(2)}) collective-permute-start(f32[9,8,16,2]{2,1,3,0:T(8,128)} %copy.102), channel_id=1, source_target_pairs={{4,0},{8,4},{12,8},{16,12},{20,16},{24,20},{28,24},{0,28},{5,1},{9... | collective-permute-start | bytes 27656 | tf_op jit(solution)/shard_map/ppermute | solution.py:17
  42.6 10.8 %collective-permute-start.9 = (f32[9,8,2,128]{3,1,2,0:T(8,128)}, f32[9,8,2,128]{3,1,2,0:T(8,128)}, u32[]{:S(2)}, u32[]{:S(2)}) collective-permute-start(f32[9,8,2,128]{3,1,2,0:T(8,128)} %copy.105), channel_id=1, source_target_pairs={{0,2},{1,3},{4,6},{5,7},{8,10},{9,11},{12,14},{13,15},{16,18},{17,... | collective-permute-start | bytes 221192 | tf_op jit(solution)/shard_map/ppermute | solution.py:15
  45.5 8.9 %collective-permute-start.10 = (f32[9,8,2,128]{3,1,2,0:T(8,128)}, f32[9,8,2,128]{3,1,2,0:T(8,128)}, u32[]{:S(2)}, u32[]{:S(2)}) collective-permute-start(f32[9,8,2,128]{3,1,2,0:T(8,128)} %copy.106), channel_id=1, source_target_pairs={{2,0},{3,1},{6,4},{7,5},{10,8},{11,9},{14,12},{15,13},{18,16},{19,... | collective-permute-start | bytes 221192 | tf_op jit(solution)/shard_map/ppermute | solution.py:17
  53.4 2.1 %copy-start.2 = (f32[8,19,128]{2,1,0:T(8,128)S(1)}, f32[8,19,128]{2,1,0:T(8,128)}, u32[]{:S(2)}) copy-start(f32[8,19,128]{2,1,0:T(8,128)} %get-tuple-element.58) | copy-start | bytes 233476
  53.4 2.1 %copy-start.5 = (f32[8,19,128]{2,1,0:T(8,128)S(1)}, f32[8,19,128]{2,1,0:T(8,128)}, u32[]{:S(2)}) copy-start(f32[8,19,128]{2,1,0:T(8,128)} %get-tuple-element.59) | copy-start | bytes 233476
  55.5 0.9 copy-start.17
  55.5 0.9 copy-start.19
  56.4 0.8 copy-start.30
  56.4 1.0 copy-start.28
  57.3 0.7 copy-start.26
  57.4 0.7 copy-start.24
  58.1 2.9 %copy-start.32 = (f32[9]{0:T(128)S(1)}, f32[9]{0:T(128)}, u32[]{:S(2)}) copy-start(f32[9]{0:T(128)} %param.19) | copy-start | bytes 112
  58.1 2.9 %copy-start.33 = (f32[8]{0:T(128)S(1)}, f32[8]{0:T(128)}, u32[]{:S(2)}) copy-start(f32[8]{0:T(128)} %dynamic_slice.11) | copy-start | bytes 100
  58.1 2.9 %copy-start.22 = (s32[16,128]{1,0:T(8,128)S(1)}, s32[16,128]{1,0:T(8,128)}, u32[]{:S(2)}) copy-start(s32[16,128]{1,0:T(8,128)} %param.21) | copy-start | bytes 24580
  58.3 2.7 %collective-permute-start.11 = (f32[9,1,16,128]{3,2,1,0:T(8,128)S(1)}, f32[9,1,16,128]{3,2,1,0:T(8,128)S(1)}, u32[]{:S(2)}, u32[]{:S(2)}) collective-permute-start(f32[9,1,16,128]{3,2,1,0:T(8,128)S(1)} %get-tuple-element.48), channel_id=1, source_target_pairs={{0,1},{2,3},{4,5},{6,7},{8,9},{10,11},{12,13},{14,15},{16,17},{18,... | collective-permute-start | bytes 221192 | tf_op jit(solution)/shard_map/ppermute | solution.py:15
  59.6 3.2 %collective-permute-start.12 = (f32[9,1,16,128]{3,2,1,0:T(8,128)S(1)}, f32[9,1,16,128]{3,2,1,0:T(8,128)S(1)}, u32[]{:S(2)}, u32[]{:S(2)}) collective-permute-start(f32[9,1,16,128]{3,2,1,0:T(8,128)S(1)} %get-tuple-element.49), channel_id=1, source_target_pairs={{1,0},{3,2},{5,4},{7,6},{9,8},{11,10},{13,12},{15,14},{17,16},{19,... | collective-permute-start | bytes 221192 | tf_op jit(solution)/shard_map/ppermute | solution.py:17
  61.0 3.2 %copy-start.9 = (f32[9,1,16,128]{3,2,1,0:T(8,128)}, f32[9,1,16,128]{3,2,1,0:T(8,128)S(1)}, u32[]{:S(2)}) copy-start(f32[9,1,16,128]{3,2,1,0:T(8,128)S(1)} %collective-permute-done.11) | copy-start | bytes 221188
  62.8 1.5 %copy-start.11 = (f32[9,1,16,128]{3,2,1,0:T(8,128)}, f32[9,1,16,128]{3,2,1,0:T(8,128)S(1)}, u32[]{:S(2)}) copy-start(f32[9,1,16,128]{3,2,1,0:T(8,128)S(1)} %collective-permute-done.12) | copy-start | bytes 221188
  66.4 15.3 %collective-permute-start.13 = (f32[9,8,16,2]{2,1,3,0:T(8,128)}, f32[9,8,16,2]{2,1,3,0:T(8,128)}, u32[]{:S(2)}, u32[]{:S(2)}) collective-permute-start(f32[9,8,16,2]{2,1,3,0:T(8,128)} %copy.109), channel_id=1, source_target_pairs={{0,4},{4,8},{8,12},{12,16},{16,20},{20,24},{24,28},{28,0},{1,5},{5... | collective-permute-start | bytes 27656 | tf_op jit(solution)/shard_map/ppermute | solution.py:15
  68.6 15.3 %collective-permute-start.14 = (f32[9,8,16,2]{2,1,3,0:T(8,128)}, f32[9,8,16,2]{2,1,3,0:T(8,128)}, u32[]{:S(2)}, u32[]{:S(2)}) collective-permute-start(f32[9,8,16,2]{2,1,3,0:T(8,128)} %copy.110), channel_id=1, source_target_pairs={{4,0},{8,4},{12,8},{16,12},{20,16},{24,20},{28,24},{0,28},{5,1},{9... | collective-permute-start | bytes 27656 | tf_op jit(solution)/shard_map/ppermute | solution.py:17
  74.0 14.4 %collective-permute-start.15 = (f32[9,8,2,128]{3,1,2,0:T(8,128)}, f32[9,8,2,128]{3,1,2,0:T(8,128)}, u32[]{:S(2)}, u32[]{:S(2)}) collective-permute-start(f32[9,8,2,128]{3,1,2,0:T(8,128)} %copy.113), channel_id=1, source_target_pairs={{0,2},{1,3},{4,6},{5,7},{8,10},{9,11},{12,14},{13,15},{16,18},{17,... | collective-permute-start | bytes 221192 | tf_op jit(solution)/shard_map/ppermute | solution.py:15
  80.4 9.0 %collective-permute-start.16 = (f32[9,8,2,128]{3,1,2,0:T(8,128)}, f32[9,8,2,128]{3,1,2,0:T(8,128)}, u32[]{:S(2)}, u32[]{:S(2)}) collective-permute-start(f32[9,8,2,128]{3,1,2,0:T(8,128)} %copy.114), channel_id=1, source_target_pairs={{2,0},{3,1},{6,4},{7,5},{10,8},{11,9},{14,12},{15,13},{18,16},{19,... | collective-permute-start | bytes 221192 | tf_op jit(solution)/shard_map/ppermute | solution.py:17
  88.4 2.1 %copy-start.3 = (f32[8,19,128]{2,1,0:T(8,128)S(1)}, f32[8,19,128]{2,1,0:T(8,128)}, u32[]{:S(2)}) copy-start(f32[8,19,128]{2,1,0:T(8,128)} %get-tuple-element.58) | copy-start | bytes 233476
  88.4 2.1 %copy-start.6 = (f32[8,19,128]{2,1,0:T(8,128)S(1)}, f32[8,19,128]{2,1,0:T(8,128)}, u32[]{:S(2)}) copy-start(f32[8,19,128]{2,1,0:T(8,128)} %get-tuple-element.59) | copy-start | bytes 233476
  90.5 0.9 copy-start.10
  90.5 0.9 copy-start.12
  93.4 0.9 copy-start.15
  93.4 0.9 copy-start.14
  93.4 0.9 copy-start.13
  94.5 7.6 %collective-permute-start.17 = (f32[9,1,16,128]{3,2,1,0:T(8,128)S(1)}, f32[9,1,16,128]{3,2,1,0:T(8,128)S(1)}, u32[]{:S(2)}, u32[]{:S(2)}) collective-permute-start(f32[9,1,16,128]{3,2,1,0:T(8,128)S(1)} %get-tuple-element.42), channel_id=1, source_target_pairs={{0,1},{2,3},{4,5},{6,7},{8,9},{10,11},{12,13},{14,15},{16,17},{18,... | collective-permute-start | bytes 221192 | tf_op jit(solution)/shard_map/ppermute | solution.py:15
  95.8 6.3 %collective-permute-start.18 = (f32[9,1,16,128]{3,2,1,0:T(8,128)S(1)}, f32[9,1,16,128]{3,2,1,0:T(8,128)S(1)}, u32[]{:S(2)}, u32[]{:S(2)}) collective-permute-start(f32[9,1,16,128]{3,2,1,0:T(8,128)S(1)} %get-tuple-element.43), channel_id=1, source_target_pairs={{1,0},{3,2},{5,4},{7,6},{9,8},{11,10},{13,12},{15,14},{17,16},{19,... | collective-permute-start | bytes 221192 | tf_op jit(solution)/shard_map/ppermute | solution.py:17
  103.0 12.0 %collective-permute-start.19 = (f32[9,8,16,2]{2,1,3,0:T(8,128)S(1)}, f32[9,8,16,2]{2,1,3,0:T(8,128)S(1)}, u32[]{:S(2)}, u32[]{:S(2)}) collective-permute-start(f32[9,8,16,2]{2,1,3,0:T(8,128)S(1)} %copy.117), channel_id=1, source_target_pairs={{0,4},{4,8},{8,12},{12,16},{16,20},{20,24},{24,28},{28,0},{1,5},{5... | collective-permute-start | bytes 27656 | tf_op jit(solution)/shard_map/ppermute | solution.py:15
  103.7 11.8 %collective-permute-start.20 = (f32[9,8,16,2]{2,1,3,0:T(8,128)S(1)}, f32[9,8,16,2]{2,1,3,0:T(8,128)}, u32[]{:S(2)}, u32[]{:S(2)}) collective-permute-start(f32[9,8,16,2]{2,1,3,0:T(8,128)S(1)} %copy.118), channel_id=1, source_target_pairs={{4,0},{8,4},{12,8},{16,12},{20,16},{24,20},{28,24},{0,28},{5,1},{9... | collective-permute-start | bytes 27656 | tf_op jit(solution)/shard_map/ppermute | solution.py:17
  108.5 9.3 %collective-permute-start.21 = (f32[9,8,2,128]{3,1,2,0:T(8,128)S(1)}, f32[9,8,2,128]{3,1,2,0:T(8,128)S(1)}, u32[]{:S(2)}, u32[]{:S(2)}) collective-permute-start(f32[9,8,2,128]{3,1,2,0:T(8,128)S(1)} %copy.121), channel_id=1, source_target_pairs={{0,2},{1,3},{4,6},{5,7},{8,10},{9,11},{12,14},{13,15},{16,18},{17,... | collective-permute-start | bytes 221192 | tf_op jit(solution)/shard_map/ppermute | solution.py:15
  113.7 6.2 %collective-permute-start.22 = (f32[9,8,2,128]{3,1,2,0:T(8,128)S(1)}, f32[9,8,2,128]{3,1,2,0:T(8,128)S(1)}, u32[]{:S(2)}, u32[]{:S(2)}) collective-permute-start(f32[9,8,2,128]{3,1,2,0:T(8,128)S(1)} %copy.122), channel_id=1, source_target_pairs={{2,0},{3,1},{6,4},{7,5},{10,8},{11,9},{14,12},{15,13},{18,16},{19,... | collective-permute-start | bytes 221192 | tf_op jit(solution)/shard_map/ppermute | solution.py:17
  117.8 2.3 %copy-start.4 = (f32[8,19,128]{2,1,0:T(8,128)S(1)}, f32[8,19,128]{2,1,0:T(8,128)}, u32[]{:S(2)}) copy-start(f32[8,19,128]{2,1,0:T(8,128)} %get-tuple-element.58) | copy-start | bytes 233476
  117.9 2.3 %copy-start.7 = (f32[8,19,128]{2,1,0:T(8,128)S(1)}, f32[8,19,128]{2,1,0:T(8,128)}, u32[]{:S(2)}) copy-start(f32[8,19,128]{2,1,0:T(8,128)} %get-tuple-element.59) | copy-start | bytes 233476
where the time goes:
time: 123 us; the launch traced here: 122 us
  starting transfers between devices  53.5 us (43%)
  local copies, waits for them, and re-layouts  34.7 us (28%)
  other arithmetic  17.8 us (14%)
  waiting for transfers between devices  9.17 us (7%)
  blocking collectives  4.97 us (4%)
  between operations  1.62 us (1%)
    ppermute x12, starting transfers between devices, with_halo(): lax.ppermute(tail, axis, [(i, (i + 1) % count) for i in range(ends)])  28.8 us
    ppermute x11, starting transfers between devices, with_halo(): lax.ppermute(head, axis, [((i + 1) % count, i) for i in range(ends)])  24.7 us
    slice x16, local copies, waits for them, and re-layouts, with_halo(): lax.slice_in_dim(cells, cells.shape[dim] - width, cells.shape[dim], axis=...  9.57 us
    ppermute x6, local copies, waits for them, and re-layouts, with_halo(): lax.ppermute(head, axis, [((i + 1) % count, i) for i in range(ends)])  7.63 us
    ppermute x11, waiting for transfers between devices, with_halo(): lax.ppermute(head, axis, [((i + 1) % count, i) for i in range(ends)])  7.24 us
    ppermute x6, local copies, waits for them, and re-layouts, with_halo(): lax.ppermute(tail, axis, [(i, (i + 1) % count) for i in range(ends)])  6.89 us
    slice x6, local copies, waits for them, and re-layouts, with_halo(): head = lax.slice_in_dim(cells, 0, width, axis=dim)  6.14 us
    psum x1, blocking collectives, run_split(): emis_grad = lax.psum(emis_grad, 'lev')  4.97 us
  transfers between devices with their start and end apart: 23, of which 4 were waited for; matrix products, arithmetic and copies ran while one was open for 23% of the time, Pallas kernels for 0%

commit v1 on v0

v1 whole, which is shorter than its diff:
```python
import jax
import jax.numpy as jnp
from jax import lax
from jax.experimental import pallas as pl
from jax.experimental.pallas import tpu as pltpu
from jax.sharding import PartitionSpec as P

F32 = jnp.float32
BF16 = jnp.bfloat16
VMEM = pl.BlockSpec(memory_space=pltpu.VMEM)
SMEM = pl.BlockSpec(memory_space=pltpu.SMEM)
PAIRS = ((0, 1, 3), (0, 2, 4), (1, 2, 5))
LAT_TILES = 133
LON_TILES = 52
CORNER_TILES = 26


def iota(shape, axis):
    return lax.broadcasted_iota(jnp.int32, shape, axis)


def split(value):
    high = value.astype(BF16)
    low = (value - high.astype(F32)).astype(BF16)
    return high, low


def stack_rows(top, bottom):
    return jnp.concatenate([top, bottom], axis=0)


def halves(tile):
    wide = tile.astype(F32)
    return wide[:8], wide[8:]


def coag(adj, state, rate):
    out = list(adj)
    kn = {}
    for m, p, q in PAIRS:
        kn[m, p] = rate[q] * state[3 * p]
    for m in range(3):
        total = (2.0 * rate[m]) * state[3 * m]
        for p in range(m + 1, 3):
            total = total + kn[m, p]
        out[3 * m] = out[3 * m] - total * adj[3 * m]
        out[3 * m + 1] = out[3 * m + 1] + (2.0 * rate[m]) * (state[3 * m + 1] * adj[3 * m + 2])
    for m, p, q in PAIRS:
        d_vol = adj[3 * p + 1] - adj[3 * m + 1]
        d_six = adj[3 * p + 2] - adj[3 * m + 2]
        inner = d_vol * state[3 * m + 1] + d_six * state[3 * m + 2] - adj[3 * m] * state[3 * m]
        cross = (2.0 * rate[q]) * adj[3 * p + 2]
        out[3 * p] = out[3 * p] + rate[q] * inner
        out[3 * m + 1] = out[3 * m + 1] + (kn[m, p] * d_vol + cross * state[3 * p + 1])
        out[3 * p + 1] = out[3 * p + 1] + cross * state[3 * m + 1]
        out[3 * m + 2] = out[3 * m + 2] + kn[m, p] * d_six
    return out


def lane_roll(value, shift):
    return pltpu.roll(value, shift, 1)


def weights(east, north):
    pos = jnp.maximum(east, 0.0)
    neg = jnp.minimum(east, 0.0)
    pos_1 = lane_roll(pos, 127)
    neg_1 = lane_roll(neg, 1)
    neg_2 = lane_roll(neg, 2)
    n_pos = jnp.maximum(north[2], 0.0)
    n_pos_1 = jnp.maximum(north[3], 0.0)
    n_neg_1 = jnp.minimum(north[1], 0.0)
    n_neg_2 = jnp.minimum(north[0], 0.0)
    centre = 1.0 + 1.5 * ((neg_1 - pos) + (n_neg_1 - n_pos))
    return (
        centre,
        0.5 * neg_2,
        -1.5 * neg_1 - 0.5 * neg_2,
        1.5 * pos + 0.5 * pos_1,
        -0.5 * pos_1,
        0.5 * n_neg_2,
        -1.5 * n_neg_1 - 0.5 * n_neg_2,
        1.5 * n_pos + 0.5 * n_pos_1,
        -0.5 * n_pos_1,
    )


def transported(rows, w):
    mid = rows[2]
    lon = (w[1] * lane_roll(mid, 2) + w[2] * lane_roll(mid, 1)) + (
        w[3] * lane_roll(mid, 127) + w[4] * lane_roll(mid, 126)
    )
    lat = (w[5] * rows[0] + w[6] * rows[1]) + (w[7] * rows[3] + w[8] * rows[4])
    return w[0] * mid + (lon + lat)


def level_scalars(z, rate_ref, speed_ref, class_ref):
    rate = [rate_ref[q, z] for q in range(6)]
    kind = class_ref[z]
    speed = [speed_ref[kind, t] for t in range(9)]
    return rate, speed


def halo_lanes(core, rows):
    lane = iota((rows, 128), 1)
    return jnp.where(core == 0, (lane >= 120).astype(jnp.int32), (lane < 8).astype(jnp.int32)) > 0


def lat_pack_kernel(lat_count, adj_ref, traj_ref, wind_ref, mix_ref, land_ref, *outs):
    lat = lax.axis_index("lat")

    def fill(out_ref, high_rows):
        base = 8 if high_rows else 0
        sub = iota((8, 128), 0)
        keep = (sub >= 2) if high_rows else (sub < 6)

        def rolled(value, shift):
            return pltpu.roll(value, shift, 0)

        def tracer(t, _):
            v2s = []
            for l in range(8):
                adj = adj_ref[t, l, base : base + 8, :]
                high = adj.astype(BF16).astype(F32)
                low = adj - high
                tr = [traj_ref[k, t, l].astype(F32)[base : base + 8] for k in range(3)]
                if high_rows:
                    extra = (rolled(tr[0], 2), rolled(tr[1], 2), rolled(tr[1], 4))
                else:
                    extra = (rolled(tr[0], 6), rolled(tr[1], 6), rolled(tr[1], 4))
                v0 = jnp.where(keep, high, extra[0])
                v1 = jnp.where(keep, low, extra[1])
                v2s.append(jnp.where(keep, tr[2], extra[2]))
                out_ref[t * 8 + l] = stack_rows(v0, v1).astype(BF16)
            for j in range(4):
                out_ref[72 + t * 4 + j] = stack_rows(v2s[2 * j], v2s[2 * j + 1]).astype(BF16)
            return 0

        lax.fori_loop(0, 9, tracer, 0)

        def level(l, _):
            for q in range(3):
                value = (mix_ref[l] if q == 2 else wind_ref[1 - q, l])[base : base + 8]
                high = value.astype(BF16).astype(F32)
                out_ref[108 + q * 8 + l] = stack_rows(high, value - high).astype(BF16)
            return 0

        lax.fori_loop(0, 8, level, 0)
        land = land_ref[base : base + 8, :].astype(F32)
        out_ref[132] = stack_rows(land, jnp.zeros_like(land)).astype(BF16)

    if lat_count == 2:
        pl.when(lat == 0)(lambda: fill(outs[0], True))
        pl.when(lat == 1)(lambda: fill(outs[0], False))
    else:
        fill(outs[0], True)
        fill(outs[1], False)


def lon_pack_kernel(lat_count, *refs):
    own, other = refs[0:4], refs[4:8]
    land_ref = refs[8]
    out_ref = refs[9]
    corners = refs[10:-1]
    pk = refs[-1]
    core = lax.axis_index("lev")
    lat = lax.axis_index("lat")
    edge = jnp.where(core == 0, 0, 120)
    slot = iota((16, 128), 1) // 8

    def gather(read):
        acc = jnp.zeros((16, 128), F32)
        for s in range(2):
            for l in range(8):
                z = 8 * jnp.bitwise_xor(s, core) + l
                shift = lax.rem(8 * z - edge + 128, 128)
                acc = jnp.where(slot == z, lane_roll(read((own, other)[s], l), shift), acc)
        return acc

    def adj_kind(t, _):
        pk[t] = gather(lambda r, l: r[0][t, l])
        return 0

    lax.fori_loop(0, 9, adj_kind, 0)
    pk[9] = gather(lambda r, l: r[2][1, l])
    pk[10] = gather(lambda r, l: r[2][0, l])
    pk[11] = gather(lambda r, l: r[3][l])
    for k in range(3):

        def traj_kind(t, _):
            pk[12 + 9 * k + t] = gather(lambda r, l: r[1][k, t, l].astype(F32))
            return 0

        lax.fori_loop(0, 9, traj_kind, 0)
    land = land_ref[...].astype(F32)
    pk[39] = jnp.where(slot == 0, lane_roll(land, lax.rem(128 - edge, 128)), 0.0)

    def emit_pair(f, _):
        high, low = split(pk[f])
        out_ref[2 * f] = high
        out_ref[2 * f + 1] = low
        return 0

    lax.fori_loop(0, 12, emit_pair, 0)

    def emit_one(f, _):
        out_ref[24 + f] = pk[12 + f].astype(BF16)
        return 0

    lax.fori_loop(0, 28, emit_one, 0)

    def corner(ref, base):
        rows = pl.ds(base, 8)
        for f in range(12):
            value = pk[f, rows, :]
            high = value.astype(BF16).astype(F32)
            ref[f] = stack_rows(high, value - high).astype(BF16)
        for t in range(9):
            ref[12 + t] = stack_rows(pk[12 + 18 + t, rows, :], pk[12 + 9 + t, rows, :]).astype(BF16)
        for j in range(5):
            ref[21 + j] = stack_rows(
                pk[12 + 2 * j, rows, :], pk[39 if j == 4 else 13 + 2 * j, rows, :]
            ).astype(BF16)

    if lat_count == 2:
        corner(corners[0], pl.multiple_of(jnp.where(lat == 0, 8, 0), 8))
    else:
        corner(corners[0], 8)
        corner(corners[1], 0)


def interior_kernel(lat_count, *refs):
    own, other = refs[0:4], refs[4:8]
    land_ref, lon_ref = refs[8:10]
    rate_ref, speed_ref, class_ref, prof_ref, coef_ref = refs[10:15]
    ce_ref, te_ref, we_ref, le_ref, out_ref, em_ref = refs[15:21]
    a_s, b_s, c_s, w_s, n_s, e_s, d_s = refs[21:]
    core = lax.axis_index("lev")
    lat = lax.axis_index("lat")
    edge = jnp.where(core == 0, 120, 0)
    halo = halo_lanes(core, 16)
    row = iota((16, 128), 0)
    blocks = [pl.ds(pl.multiple_of(jnp.where(lat == 0, 8, 0), 8), 8)] if lat_count == 2 else [pl.ds(8, 8), pl.ds(0, 8)]
    zero = jnp.zeros((16, 128), F32)

    def unslot(value, z):
        return lane_roll(value, lax.rem(edge + 128 - 8 * z, 128))

    def paired(f):
        return lon_ref[2 * f].astype(F32) + lon_ref[2 * f + 1].astype(F32)

    land_halo = unslot(lon_ref[51].astype(F32), 0)
    deposit = 0.1 + 0.3 * jnp.where(halo, land_halo, land_ref[...].astype(F32))
    e_s[16] = deposit
    for e, block in enumerate(blocks):
        le_ref[e] = e_s[16, block, :]
    last_lat = lat == lat_count - 1

    def zero_pads(t, _):
        b_s[t, 0] = zero
        b_s[t, 17] = zero
        for z in range(16):
            c_s[t, z, 0:8, :] = zero[:8]
            c_s[t, z, 24:32, :] = zero[:8]
        return 0

    lax.fori_loop(0, 9, zero_pads, 0)
    d_s[0] = zero

    for s in range(2):
        r = (own, other)[s]

        def assemble(l, _):
            z = 8 * jnp.bitwise_xor(s, core) + l
            for t in range(9):
                a_s[t, z] = jnp.where(halo, unslot(paired(t), z), r[0][t, l])
            north = jnp.where(halo, unslot(paired(9), z), r[2][1, l])
            north = jnp.where((row == 15) & last_lat, 0.0, north)
            east = jnp.where(halo, unslot(paired(10), z), r[2][0, l])
            mix = jnp.where(halo, unslot(paired(11), z), r[3][l])
            n_s[z, 0:8, :] = zero[:8]
            n_s[z, 8:24, :] = north
            n_s[z, 24:32, :] = zero[:8]
            e_s[z] = east
            d_s[z + 1] = jnp.where(z == 15, 0.0, mix)
            for e, block in enumerate(blocks):
                we_ref[e, 0, z] = n_s[z, pl.ds(block.start + 8, 8), :]
                we_ref[e, 1, z] = e_s[z, block, :]
                we_ref[e, 2, z] = d_s[z + 1, block, :]
            shifted = [n_s[z, 6 + i : 22 + i, :] for i in range(4)]
            for i, value in enumerate(weights(east, shifted)):
                w_s[i, z] = value
            return 0

        lax.fori_loop(0, 8, assemble, 0)

    em = [zero, zero, zero]
    for step in range(3):
        k = 2 - step
        for s in range(2):
            r = (own, other)[s]

            def react(l, sums):
                z = 8 * jnp.bitwise_xor(s, core) + l
                rate = [rate_ref[q, z] for q in range(6)]
                share = prof_ref[z]
                adj = [a_s[t, z] for t in range(9)]
                sums = [
                    sums[m] + sum((share * coef_ref[3 * m + j]) * adj[3 * m + j] for j in range(3)) for m in range(3)
                ]
                state = []
                for t in range(9):
                    value = r[1][k, t, l].astype(F32)
                    state.append(jnp.where(halo, unslot(lon_ref[24 + 9 * k + t].astype(F32), z), value))
                done = coag(adj, state, rate)
                for t in range(9):
                    b_s[t, z + 1] = done[t]
                if k < 2:
                    for t in range(9):
                        if lat_count == 2:
                            te_ref[0, k, t, z] = jnp.where(lat == 0, state[t][8:], state[t][:8])
                        else:
                            te_ref[0, k, t, z] = state[t][8:]
                            te_ref[1, k, t, z] = state[t][:8]
                return sums

            if s == 0:
                sums = [zero, zero, zero]
            sums = lax.fori_loop(0, 8, react, sums)
        if step > 0:
            low, high = 2 * step, 15 - 2 * step
            if lat_count == 2:
                good = ((row <= high) | (lat != 0)) & ((row >= low) | (lat == 0))
            else:
                good = (row <= high) & (row >= low)
            sums = [jnp.where(good, v, 0.0) for v in sums]
        em = [em[m] + sums[m] for m in range(3)]

        def mixed(z, _):
            kind = class_ref[z]
            below, above = d_s[z], d_s[z + 1]
            base = 1.0 - above - below
            base = jnp.where(z == 0, base - deposit, base)
            for t in range(9):
                speed = speed_ref[kind, t]
                value = b_s[t, z + 1] * (base - speed) + b_s[t, z] * (below + speed) + b_s[t, z + 2] * above
                c_s[t, z, 8:24, :] = value
                for e, block in enumerate(blocks):
                    ce_ref[e, step, t, z] = c_s[t, z, pl.ds(block.start + 8, 8), :]
            return 0

        lax.fori_loop(0, 16, mixed, 0)

        def moved(z, _):
            for rb in range(2):
                w = [w_s[i, z, 8 * rb : 8 * rb + 8, :] for i in range(9)]
                for t in range(9):
                    rows = [c_s[t, z, 8 * rb + 6 + i : 8 * rb + 14 + i, :] for i in range(5)]
                    value = transported(rows, w)
                    if step < 2:
                        a_s[t, z, 8 * rb : 8 * rb + 8, :] = value
                    else:
                        out_ref[t, z, 8 * rb : 8 * rb + 8, :] = value
            return 0

        lax.fori_loop(0, 16, moved, 0)
    for m in range(3):
        em_ref[m] = em[m]


def edge_kernel(lat_count, *refs):
    edges = 1 if lat_count == 2 else 2
    ce_ref, te_ref, we_ref, le_ref, out_ref, em_ref = refs[0:6]
    lat_refs = refs[6 : 6 + 2 * edges]
    corner_refs = refs[6 + 2 * edges : 6 + 3 * edges]
    rate_ref, speed_ref, class_ref, prof_ref, coef_ref = refs[6 + 3 * edges : 11 + 3 * edges]
    keep_ref, send_ref = refs[11 + 3 * edges : 13 + 3 * edges]
    b_s, c_s, t_s, n_s, e_s, d_s, l_s, a_s, em_s, fin_s = refs[13 + 3 * edges :]
    core = lax.axis_index("lev")
    lat = lax.axis_index("lat")
    edge = jnp.where(core == 0, 120, 0)
    halo = halo_lanes(core, 8)
    sub = iota((8, 128), 0)
    zero = jnp.zeros((8, 128), F32)

    def unslot(value, z):
        return lane_roll(value, lax.rem(edge + 128 - 8 * z, 128))

    def rolled(value, shift):
        return pltpu.roll(value, shift, 0)

    def run(upper, e):
        own_at, halo_at = (0, 8) if upper else (8, 0)
        corner_ref = corner_refs[e]
        keep = (sub < 6) if upper else (sub >= 2)

        def corner_pair(tile, z):
            top, bottom = halves(corner_ref[tile])
            return unslot(top, z), unslot(bottom, z)

        _, land_c = corner_pair(25, 0)
        land_l, _ = halves(lat_refs[2 * e][132])
        l_s[pl.ds(halo_at, 8), :] = 0.1 + 0.3 * jnp.where(halo, land_c, land_l)
        l_s[pl.ds(own_at, 8), :] = le_ref[e]
        d_s[0] = jnp.zeros((16, 128), F32)

        def pads(t, _):
            b_s[t, 0] = zero
            b_s[t, 17] = zero
            for z in range(16):
                c_s[t, z, 0:8, :] = zero
                c_s[t, z, 24:32, :] = zero
            return 0

        lax.fori_loop(0, 9, pads, 0)

        for s in range(2):
            msg = lat_refs[2 * e + s]

            def receive(pair, _):
                for i in range(2):
                    l = 2 * pair + i
                    z = 8 * jnp.bitwise_xor(s, core) + l
                    rate = [rate_ref[q, z] for q in range(6)]
                    adj, state = [], []
                    for t in range(9):
                        v0, v1 = halves(msg[t * 8 + l])
                        v2 = halves(msg[72 + t * 4 + pair])[i]
                        high, low = corner_pair(t, z)
                        adj.append(jnp.where(halo, high + low, jnp.where(keep, v0 + v1, 0.0)))
                        tr2, tr1 = corner_pair(12 + t, z)
                        tile, part = divmod(t, 2)
                        tr0 = unslot(halves(corner_ref[21 + tile])[part], z)
                        state.append(jnp.where(halo, tr2, v2))
                        if upper:
                            own1 = jnp.where(sub < 2, rolled(v1, 2), rolled(v2, 4))
                            own0 = rolled(v0, 2)
                        else:
                            own1 = jnp.where(sub >= 6, rolled(v1, 6), rolled(v2, 4))
                            own0 = rolled(v0, 6)
                        t_s[1, t, z, pl.ds(halo_at, 8), :] = jnp.where(halo, tr1, own1)
                        t_s[0, t, z, pl.ds(halo_at, 8), :] = jnp.where(halo, tr0, own0)
                        t_s[1, t, z, pl.ds(own_at, 8), :] = te_ref[e, 1, t, z]
                        t_s[0, t, z, pl.ds(own_at, 8), :] = te_ref[e, 0, t, z]
                    done = coag(adj, state, rate)
                    for t in range(9):
                        b_s[t, z + 1] = done[t]
                    winds = []
                    for q in range(3):
                        high, low = halves(msg[108 + q * 8 + l])
                        c_high, c_low = corner_pair(9 + q, z)
                        winds.append(jnp.where(halo, c_high + c_low, high + low))
                    n_s[z, 0:8, :] = zero
                    n_s[z, 24:32, :] = zero
                    n_s[z, pl.ds(8 + halo_at, 8), :] = winds[0]
                    n_s[z, pl.ds(8 + own_at, 8), :] = we_ref[e, 0, z]
                    e_s[z, pl.ds(halo_at, 8), :] = winds[1]
                    e_s[z, pl.ds(own_at, 8), :] = we_ref[e, 1, z]
                    d_s[z + 1, pl.ds(halo_at, 8), :] = jnp.where(z == 15, 0.0, winds[2])
                    d_s[z + 1, pl.ds(own_at, 8), :] = we_ref[e, 2, z]
                return 0

            lax.fori_loop(0, 4, receive, 0)

        for m in range(3):
            for part in range(3):
                em_s[m, 8 * part : 8 * part + 8, :] = zero

        starts = (6, 4, 0) if upper else (2, 4, 8)
        at = halo_at
        for step in range(3):

            def mixed(z, _):
                kind = class_ref[z]
                below, above = d_s[z, at : at + 8, :], d_s[z + 1, at : at + 8, :]
                base = 1.0 - above - below
                base = jnp.where(z == 0, base - l_s[at : at + 8, :], base)
                for t in range(9):
                    speed = speed_ref[kind, t]
                    value = b_s[t, z + 1] * (base - speed) + b_s[t, z] * (below + speed) + b_s[t, z + 2] * above
                    c_s[t, z, 8 + own_at : 16 + own_at, :] = ce_ref[e, step, t, z]
                    c_s[t, z, 8 + at : 16 + at, :] = value
                return 0

            lax.fori_loop(0, 16, mixed, 0)
            at = starts[step]

            def moved(z, sums):
                shifted = [n_s[z, 6 + at + i : 14 + at + i, :] for i in range(4)]
                w = weights(e_s[z, at : at + 8, :], shifted)
                adj = []
                for t in range(9):
                    rows = [c_s[t, z, 6 + at + i : 14 + at + i, :] for i in range(5)]
                    adj.append(transported(rows, w))
                if step == 2:
                    for t in range(9):
                        fin_s[e, t, z] = adj[t]
                    return sums
                share = prof_ref[z]
                sums = [
                    sums[m] + sum((share * coef_ref[3 * m + j]) * adj[3 * m + j] for j in range(3)) for m in range(3)
                ]
                rate = [rate_ref[q, z] for q in range(6)]
                state = [t_s[1 - step, t, z, at : at + 8, :] for t in range(9)]
                done = coag(adj, state, rate)
                for t in range(9):
                    b_s[t, z + 1] = done[t]
                return sums

            sums = lax.fori_loop(0, 16, moved, [zero, zero, zero])
            if step < 2:
                buf_row = sub + at
                count = 2 + 2 * step
                if upper:
                    good = (buf_row >= 8 - count) & (buf_row < 8)
                else:
                    good = (buf_row >= 8) & (buf_row < 8 + count)
                for m in range(3):
                    em_s[m, at : at + 8, :] = em_s[m, at : at + 8, :] + jnp.where(good, sums[m], 0.0)
        for m in range(3):
            a_s[e, m] = em_s[m, own_at : own_at + 8, :]

    def finish(has_upper, has_lower, e_upper, e_lower):
        mine = (iota((16, 128), 1) < 64) == (core == 0)
        row8 = sub

        def rows_of(t, z):
            low = out_ref[t, z, 0:8, :]
            high = out_ref[t, z, 8:16, :]
            if has_upper:
                high = jnp.where(row8 >= 2, fin_s[e_upper, t, z], high)
            if has_lower:
                low = jnp.where(row8 < 6, fin_s[e_lower, t, z], low)
            return stack_rows(low, high)

        def tracer(t, _):
            for l in range(8):
                keep_ref[t, l] = rows_of(t, 8 * core + l)
            for l in range(4):
                z = 8 * (1 - core) + l
                send_ref[t * 4 + l] = jnp.where(mine, rows_of(t, z), lane_roll(rows_of(t, z + 4), 64))
            return 0

        lax.fori_loop(0, 9, tracer, 0)
        for m in range(3):
            low = em_ref[m, 0:8, :]
            high = em_ref[m, 8:16, :]
            if has_upper:
                high = high + a_s[e_upper, m]
            if has_lower:
                low = low + a_s[e_lower, m]
            send_ref[36 + m] = stack_rows(low, high)

    if lat_count == 2:

        def south():
            run(True, 0)
            finish(True, False, 0, 0)

        def north():
            run(False, 0)
            finish(False, True, 0, 0)

        pl.when(lat == 0)(south)
        pl.when(lat == 1)(north)
    else:
        run(True, 0)
        run(False, 1)
        finish(True, True, 0, 1)


def join_kernel(keep_ref, send_ref, recv_ref, source_ref, out_ref, em_ref):
    core = lax.axis_index("lev")
    mine = (iota((16, 128), 1) < 64) == (core == 0)

    def tracer(t, _):
        for l in range(4):
            got = recv_ref[t * 4 + l]
            out_ref[t, l] = jnp.where(mine, keep_ref[t, l], got)
            out_ref[t, l + 4] = jnp.where(mine, keep_ref[t, l + 4], lane_roll(got, 64))
        return 0

    lax.fori_loop(0, 9, tracer, 0)
    source = source_ref[...].astype(F32)
    for m in range(3):
        em_ref[m] = jnp.where(mine, send_ref[36 + m], recv_ref[36 + m]) * source


def shape(*dims, dtype=F32):
    return jax.ShapeDtypeStruct(dims, dtype)


def call(kernel, outs, scratch, *args, specs=None):
    return pl.pallas_call(
        kernel,
        out_shape=outs,
        in_specs=specs or [VMEM] * len(args),
        out_specs=[VMEM] * len(outs),
        scratch_shapes=scratch,
        compiler_params=pltpu.CompilerParams(vmem_limit_bytes=48 * 1024 * 1024),
    )(*args)


def shards(
    adjoint_in,
    trajectory,
    courant,
    mixing,
    coag_rates,
    settle_speed,
    settle_class,
    emis_profile,
    emis_coef,
    land_mask,
    source_mask,
):
    lat_count = lax.axis_size("lat")
    lon_count = lax.axis_size("lon")
    edges = 1 if lat_count == 2 else 2
    swap = [(0, 1), (1, 0)]

    def over_lev(value):
        return lax.ppermute(value, "lev", swap)

    def lat_moves(messages):
        if edges == 1:
            return [lax.ppermute(messages[0], "lat", swap)]
        up = [(j, j + 1) for j in range(lat_count - 1)]
        down = [(j + 1, j) for j in range(lat_count - 1)]
        return [lax.ppermute(messages[1], "lat", down), lax.ppermute(messages[0], "lat", up)]

    def corner_moves(messages):
        def pairs(shift):
            found = []
            for i in range(lon_count):
                for x in range(lat_count):
                    y = 1 - x if edges == 1 else x + shift
                    if 0 <= y < lat_count:
                        right, left = (i + 1) % lon_count, (i - 1) % lon_count
                        found.append(((i * lat_count + x) * 2 + 1, (right * lat_count + y) * 2))
                        found.append(((i * lat_count + x) * 2, (left * lat_count + y) * 2 + 1))
            return found

        axes = ("lon", "lat", "lev")
        if edges == 1:
            return [lax.ppermute(messages[0], axes, pairs(0))]
        return [lax.ppermute(messages[1], axes, pairs(-1)), lax.ppermute(messages[0], axes, pairs(1))]

    def bind(kernel):
        def run(*refs):
            return kernel(lat_count, *refs)

        return run

    own = (adjoint_in, trajectory, courant, mixing)
    other = tuple(over_lev(value) for value in own)
    lat_out = call(
        bind(lat_pack_kernel), [shape(LAT_TILES, 16, 128, dtype=BF16)] * edges, [], *own, land_mask
    )
    lat_in = lat_moves(lat_out)
    lon_out, *corner_out = call(
        bind(lon_pack_kernel),
        [shape(LON_TILES, 16, 128, dtype=BF16)] + [shape(CORNER_TILES, 16, 128, dtype=BF16)] * edges,
        [pltpu.VMEM((40, 16, 128), F32)],
        *own,
        *other,
        land_mask,
    )
    lon_pairs = []
    for i in range(lon_count):
        lon_pairs.append((2 * i + 1, 2 * ((i + 1) % lon_count)))
        lon_pairs.append((2 * i, 2 * ((i - 1) % lon_count) + 1))
    lon_in = lax.ppermute(lon_out, ("lon", "lev"), lon_pairs)
    corner_in = corner_moves(corner_out)
    scalars = (coag_rates, settle_speed, settle_class, emis_profile, emis_coef)
    inner = call(
        bind(interior_kernel),
        [
            shape(edges, 3, 9, 16, 8, 128),
            shape(edges, 2, 9, 16, 8, 128),
            shape(edges, 3, 16, 8, 128),
            shape(edges, 8, 128),
            shape(9, 16, 16, 128),
            shape(3, 16, 128),
        ],
        [
            pltpu.VMEM((9, 16, 16, 128), F32),
            pltpu.VMEM((9, 18, 16, 128), F32),
            pltpu.VMEM((9, 16, 32, 128), F32),
            pltpu.VMEM((9, 16, 16, 128), F32),
            pltpu.VMEM((16, 32, 128), F32),
            pltpu.VMEM((17, 16, 128), F32),
            pltpu.VMEM((17, 16, 128), F32),
        ],
        *own,
        *other,
        land_mask,
        lon_in,
        *scalars,
        specs=[VMEM] * 10 + [SMEM] * 5,
    )
    lat_all = []
    for value in lat_in:
        lat_all += [value, over_lev(value)]
    keep, send = call(
        bind(edge_kernel),
        [shape(9, 8, 16, 128), shape(39, 16, 128)],
        [
            pltpu.VMEM((9, 18, 8, 128), F32),
            pltpu.VMEM((9, 16, 32, 128), F32),
            pltpu.VMEM((2, 9, 16, 16, 128), F32),
            pltpu.VMEM((16, 32, 128), F32),
            pltpu.VMEM((16, 16, 128), F32),
            pltpu.VMEM((17, 16, 128), F32),
            pltpu.VMEM((16, 128), F32),
            pltpu.VMEM((edges, 3, 8, 128), F32),
            pltpu.VMEM((3, 24, 128), F32),
            pltpu.VMEM((edges, 9, 16, 8, 128), F32),
        ],
        *inner,
        *lat_all,
        *corner_in,
        *scalars,
        specs=[VMEM] * (6 + 3 * edges) + [SMEM] * 5,
    )
    recv = over_lev(send)
    out, emis = call(
        join_kernel, [shape(9, 8, 16, 128), shape(3, 16, 128)], [], keep, send, recv, source_mask
    )
    return (out, emis)


def solution(mesh):
    return jax.shard_map(
        shards,
        mesh=mesh,
        in_specs=(
            P(None, "lev", "lat", "lon"),
            P(None, None, "lev", "lat", "lon"),
            P(None, "lev", "lat", "lon"),
            P("lev", "lat", "lon"),
            P(),
            P(),
            P(),
            P(),
            P(),
            P("lat", "lon"),
            P("lat", "lon"),
        ),
        out_specs=(P(None, "lev", "lat", "lon"), P(None, "lat", "lon")),
        check_vma=False,
    )
```

time: 123 us -> 70.7 us (0.57)
  starting transfers between devices: 53.5 us -> 9.56 us
  Pallas kernels: 0 us -> 35.6 us
  local copies, waits for them, and re-layouts: 34.7 us -> 4.71 us
  other arithmetic: 17.8 us -> 0 us
  waiting for transfers between devices: 9.17 us -> 19.7 us
  blocking collectives: 4.97 us -> 0 us
    ppermute x23 -> x9, starting transfers between devices: 53.5 us -> 9.56 us  [the longest x1 4.62 us: shards(): lon_in = lax.ppermute(lon_out, ('lon', 'lev'), lon_pairs)]
    pallas_call x0 -> x5, Pallas kernels: none -> 35.6 us  [call(): pl.pallas_call(kernel, out_shape=outs, in_specs=specs or [VMEM] * len(arg...]
    slice x22 -> x0, local copies, waits for them, and re-layouts: 15.7 us -> none  [the longest x16 9.57 us: with_halo(): lax.slice_in_dim(cells, cells.shape[dim] - width, cells.shape[dim], axis=...]
    ppermute x12 -> x0, local copies, waits for them, and re-layouts: 14.5 us -> none  [the longest x6 7.63 us: with_halo(): lax.ppermute(head, axis, [((i + 1) % count, i) for i in range(ends)])]
    ppermute x23 -> x9, waiting for transfers between devices: 9.17 us -> 19.7 us  [the longest x1 12.8 us: lat_moves(): return [lax.ppermute(messages[0], 'lat', swap)]]
    psum x1 -> x0, blocking collectives: 4.97 us -> none  [run_split(): emis_grad = lax.psum(emis_grad, 'lev')]
    concatenate x6 -> x0, other arithmetic: 4.52 us -> none  [with_halo(): jnp.concatenate([lax.ppermute(tail, axis, [(i, (i + 1) % count) for i in...]
    add x10 -> x0, other arithmetic: 4.14 us -> none  [the longest x2 2.29 us: run_split(): adjoint + transport(lon_pad, east_pad, 3, col_count)]
  transfers between devices with their start and end apart: 23 -> 9, of which waited for: 4 -> 4; matrix products, arithmetic and copies ran while one was open for 23% -> 0% of each run, Pallas kernels for 0% -> 34%
where the time goes in v1:
time: 70.7 us; the launch traced here: 70.3 us
  Pallas kernels  35.6 us (50%)
  waiting for transfers between devices  19.7 us (28%)
  starting transfers between devices  9.56 us (14%)
  local copies, waits for them, and re-layouts  4.71 us (7%)
  between operations  0.75 us (1%)
    pallas_call x5, Pallas kernels, call(): pl.pallas_call(kernel, out_shape=outs, in_specs=specs or [VMEM] * len(arg...  35.6 us
    ppermute x1, waiting for transfers between devices, lat_moves(): return [lax.ppermute(messages[0], 'lat', swap)]  12.8 us
    unnamed x24, local copies, waits for them, and re-layouts  4.71 us
    ppermute x1, starting transfers between devices, shards(): lon_in = lax.ppermute(lon_out, ('lon', 'lev'), lon_pairs)  4.62 us
    ppermute x1, waiting for transfers between devices, shards(): lon_in = lax.ppermute(lon_out, ('lon', 'lev'), lon_pairs)  3.6 us
    ppermute x6, waiting for transfers between devices, over_lev(): return lax.ppermute(value, 'lev', swap)  3.32 us
    ppermute x1, starting transfers between devices, lat_moves(): return [lax.ppermute(messages[0], 'lat', swap)]  2.56 us
  transfers between devices with their start and end apart: 9, of which 4 were waited for; matrix products, arithmetic and copies ran while one was open for 0% of the time, Pallas kernels for 34%

profile of v1, /device:TPU:0, one launch (start us, length us, event | category | flops | bytes accessed | tf_op | source)
XLA Modules:
  0.0 70.3 jit_solution(12967428133496653364)
XLA Ops:
  0.6 0.5 collective-permute-start.1
  1.1 0.0 copy-start
  1.2 1.2 %copy-done = bf16[3,9,8,16,128]{4,3,2,1,0:T(8,128)(2,1)S(1)} copy-done((bf16[3,9,8,16,128]{4,3,2,1,0:T(8,128)(2,1)S(1)}, bf16[3,9,8,16,128]{4,3,2,1,0:T(8,128)(2,1)}, u32[]{:S(2)}) %copy-start) | copy-done | bytes 884760
  2.3 0.0 copy-start.1
  2.3 1.1 %copy-done.1 = f32[9,8,16,128]{3,2,1,0:T(8,128)S(1)} copy-done((f32[9,8,16,128]{3,2,1,0:T(8,128)S(1)}, f32[9,8,16,128]{3,2,1,0:T(8,128)}, u32[]{:S(2)}) %copy-start.1) | copy-done | bytes 589848
  3.4 0.0 copy-start.2
  3.4 0.9 %copy-done.2 = f32[2,8,16,128]{3,2,1,0:T(8,128)S(1)} copy-done((f32[2,8,16,128]{3,2,1,0:T(8,128)S(1)}, f32[2,8,16,128]{3,2,1,0:T(8,128)}, u32[]{:S(2)}) %copy-start.2) | copy-done | bytes 131096
  4.3 0.0 copy-start.3
  4.3 0.8 %copy-done.3 = f32[8,16,128]{2,1,0:T(8,128)S(1)} copy-done((f32[8,16,128]{2,1,0:T(8,128)S(1)}, f32[8,16,128]{2,1,0:T(8,128)}, u32[]{:S(2)}) %copy-start.3) | copy-done | bytes 65560
  5.1 0.0 copy-start.4
  5.1 0.7 copy-done.4
  5.8 0.0 copy-start.5
  5.8 0.2 shard_map.124
  6.1 0.0 copy-start.6
  6.1 0.0 copy-start.7
  6.1 0.0 copy-start.9
  6.1 0.0 copy-start.10
  6.1 0.0 copy-start.11
  6.1 2.6 %collective-permute-start.5 = (bf16[133,16,128]{2,1,0:T(8,128)(2,1)S(1)}, bf16[133,16,128]{2,1,0:T(8,128)(2,1)S(1)}, u32[]{:S(2)}, u32[]{:S(2)}) collective-permute-start(bf16[133,16,128]{2,1,0:T(8,128)(2,1)S(1)} %shard_map.124), channel_id=1, source_target_pairs={{0,2},{2,0},{1,3},{3,1},{4,6},{6,4},{5,7},{7,5},{8,10},{10,8},{9,1... | collective-permute-start | bytes 1634312 | tf_op jit(solution)/shard_map/ppermute | solution.py:627
  8.7 0.2 collective-permute-start
  8.9 12.8 %collective-permute-done.5.refs_6_ = bf16[133,16,128]{2,1,0:T(8,128)(2,1)S(1)} collective-permute-done((bf16[133,16,128]{2,1,0:T(8,128)(2,1)S(1)}, bf16[133,16,128]{2,1,0:T(8,128)(2,1)S(1)}, u32[]{:S(2)}, u32[]{:S(2)}) %collective-permute-start.5) | collective-permute-done | bytes 544800 | tf_op jit(solution)/shard_map/ppermute | solution.py:627
  21.7 0.0 collective-permute-start.6
  21.7 0.5 collective-permute-start.2
  22.2 0.0 collective-permute-start.3
  22.2 1.7 %collective-permute-done.3.refs_7_ = f32[8,16,128]{2,1,0:T(8,128)S(1)} collective-permute-done((f32[8,16,128]{2,1,0:T(8,128)S(1)}, f32[8,16,128]{2,1,0:T(8,128)S(1)}, u32[]{:S(2)}, u32[]{:S(2)}) %collective-permute-start.3) | collective-permute-done | bytes 65568 | tf_op jit(solution)/shard_map/ppermute | solution.py:623
  23.9 0.0 collective-permute-done.2.refs_6_
  23.9 0.0 collective-permute-done.refs_4_
  23.9 0.0 collective-permute-done.1.refs_5_
  23.9 0.0 copy-done.5
  24.0 3.8 %shard_map.122 = (bf16[52,16,128]{2,1,0:T(8,128)(2,1)S(1)}, bf16[26,16,128]{2,1,0:T(8,128)(2,1)S(1)}) custom-call(f32[9,8,16,128]{3,2,1,0:T(8,128)S(1)} %copy-done.1, bf16[3,9,8,16,128]{4,3,2,1,0:T(8,128)(2,1)S(1)} %copy-done, f32[2,8,16,128]{3,2,1,0:T(8,128)S(1)} %copy-done.2, f32[8,16,128]{2,1,0:T(8,128)S(1)} %copy-done.3, ...), custom_call_target="tpu_custom_call" | custom-call | tf_op jit(solution)/shard_map/pallas_call | solution.py:594
  27.8 4.6 %collective-permute-start.4 = (bf16[52,16,128]{2,1,0:T(8,128)(2,1)S(1)}, bf16[52,16,128]{2,1,0:T(8,128)(2,1)S(1)}, u32[]{:S(2)}, u32[]{:S(2)}) collective-permute-start(bf16[52,16,128]{2,1,0:T(8,128)(2,1)S(1)} %get-tuple-element.12), channel_id=1, source_target_pairs={{1,4},{0,29},{5,8},{4,1},{9,12},{8,5},{13,16},{12,9},{17,20},{16,1... | collective-permute-start | bytes 638984 | tf_op jit(solution)/shard_map/ppermute | solution.py:673
  32.4 1.1 %collective-permute-start.7 = (bf16[26,16,128]{2,1,0:T(8,128)(2,1)S(1)}, bf16[26,16,128]{2,1,0:T(8,128)(2,1)S(1)}, u32[]{:S(2)}, u32[]{:S(2)}) collective-permute-start(bf16[26,16,128]{2,1,0:T(8,128)(2,1)S(1)} %get-tuple-element.19), channel_id=1, source_target_pairs={{1,6},{0,31},{3,4},{2,29},{5,10},{4,3},{7,8},{6,1},{9,14},{8,7},{1... | collective-permute-start | bytes 319496 | tf_op jit(solution)/shard_map/ppermute | solution.py:646
  33.5 3.6 %collective-permute-done.4.refs_9_ = bf16[52,16,128]{2,1,0:T(8,128)(2,1)S(1)} collective-permute-done((bf16[52,16,128]{2,1,0:T(8,128)(2,1)S(1)}, bf16[52,16,128]{2,1,0:T(8,128)(2,1)S(1)}, u32[]{:S(2)}, u32[]{:S(2)}) %collective-permute-start.4) | collective-permute-done | bytes 213024 | tf_op jit(solution)/shard_map/ppermute | solution.py:673
  37.1 0.0 copy-done.6
  37.1 0.0 copy-done.7
  37.1 0.0 copy-done.9
  37.1 0.0 copy-done.10
  37.1 0.0 copy-done.11
  37.1 19.7 %shard_map.123 = (f32[1,3,9,16,8,128]{5,4,3,2,1,0:T(8,128)}, f32[1,2,9,16,8,128]{5,4,3,2,1,0:T(8,128)S(1)}, f32[1,3,16,8,128]{4,3,2,1,0:T(8,128)S(1)}, f32[1,8,1...) custom-call(f32[9,8,16,128]{3,2,1,0:T(8,128)S(1)} %copy-done.1, ...), custom_call_target="tpu_custom_call" | custom-call | tf_op jit(solution)/shard_map/pallas_call | solution.py:594
  56.8 0.0 collective-permute-done.7.refs_8_
  56.8 0.0 collective-permute-done.6.refs_7_
  56.8 0.0 copy-start.8
  56.8 10.3 %shard_map.125 = (f32[9,8,16,128]{3,2,1,0:T(8,128)S(1)}, f32[39,16,128]{2,1,0:T(8,128)S(1)}) custom-call(f32[1,3,9,16,8,128]{5,4,3,2,1,0:T(8,128)} %get-tuple-element.13.refs_0_, f32[1,2,9,16,8,128]{5,4,3,2,1,0:T(8,128)S(1)} %get-tuple-element.14.refs_1_, f32[1,3,16,8,128]{4,3,2,1,0:T(8,128)S(1)} %get-tuple-element.15.refs_2_, ...), custom_call_target="tpu_custom_call" | custom-call | tf_op jit(solution)/shard_map/pallas_call | solution.py:594
  67.1 0.1 collective-permute-start.8
  67.2 1.6 %collective-permute-done.8.recv_ref = f32[39,16,128]{2,1,0:T(8,128)S(1)} collective-permute-done((f32[39,16,128]{2,1,0:T(8,128)S(1)}, f32[39,16,128]{2,1,0:T(8,128)S(1)}, u32[]{:S(2)}, u32[]{:S(2)}) %collective-permute-start.8) | collective-permute-done | bytes 319520 | tf_op jit(solution)/shard_map/ppermute | solution.py:623
  68.8 0.0 copy-done.8
  68.8 1.5 %shard_map.126 = (f32[9,8,16,128]{3,2,1,0:T(8,128)}, f32[3,16,128]{2,1,0:T(8,128)}) custom-call(f32[9,8,16,128]{3,2,1,0:T(8,128)S(1)} %get-tuple-element.20.keep_ref, f32[39,16,128]{2,1,0:T(8,128)S(1)} %get-tuple-element.21.send_ref, f32[39,16,128]{2,1,0:T(8,128)S(1)} %collective-permute-done.8.recv_ref, s32[16,128]{1,0:T(8,128)S(1)} %copy-done.8), custom_call_target="tpu_custom_call" | custom-call | tf_op jit(solution)/shard_map/pallas_call | solution.py:594
Async XLA Ops:
  0.6 23.3 %collective-permute-start.1 = (bf16[3,9,8,16,128]{4,3,2,1,0:T(8,128)(2,1)}, bf16[3,9,8,16,128]{4,3,2,1,0:T(8,128)(2,1)S(1)}, u32[]{:S(2)}, u32[]{:S(2)}) collective-permute-start(bf16[3,9,8,16,128]{4,3,2,1,0:T(8,128)(2,1)} %refs_1_.5), channel_id=1, source_target_pairs={{0,1},{1,0},{2,3},{3,2},{4,5},{5,4},{6,7},{7,6},{8,9},{9,8},{10,11... | collective-permute-start | bytes 2654216 | tf_op jit(solution)/shard_map/ppermute | solution.py:623
  1.1 1.2 %copy-start = (bf16[3,9,8,16,128]{4,3,2,1,0:T(8,128)(2,1)S(1)}, bf16[3,9,8,16,128]{4,3,2,1,0:T(8,128)(2,1)}, u32[]{:S(2)}) copy-start(bf16[3,9,8,16,128]{4,3,2,1,0:T(8,128)(2,1)} %refs_1_.5) | copy-start | bytes 2654212
  2.3 1.1 %copy-start.1 = (f32[9,8,16,128]{3,2,1,0:T(8,128)S(1)}, f32[9,8,16,128]{3,2,1,0:T(8,128)}, u32[]{:S(2)}) copy-start(f32[9,8,16,128]{3,2,1,0:T(8,128)} %refs_0_.5) | copy-start | bytes 1769476
  3.4 0.9 %copy-start.2 = (f32[2,8,16,128]{3,2,1,0:T(8,128)S(1)}, f32[2,8,16,128]{3,2,1,0:T(8,128)}, u32[]{:S(2)}) copy-start(f32[2,8,16,128]{3,2,1,0:T(8,128)} %refs_2_.5) | copy-start | bytes 393220
  4.3 0.8 %copy-start.3 = (f32[8,16,128]{2,1,0:T(8,128)S(1)}, f32[8,16,128]{2,1,0:T(8,128)}, u32[]{:S(2)}) copy-start(f32[8,16,128]{2,1,0:T(8,128)} %refs_3_.5) | copy-start | bytes 196612
  5.1 0.7 copy-start.4
  5.8 18.1 %copy-start.5 = (s32[16,128]{1,0:T(8,128)S(1)}, s32[16,128]{1,0:T(8,128)}, u32[]{:S(2)}) copy-start(s32[16,128]{1,0:T(8,128)} %refs_4_.1) | copy-start | bytes 24580
  6.1 31.0 %copy-start.6 = (f32[6,16]{1,0:T(8,128)S(1)}, f32[6,16]{1,0:T(8,128)}, u32[]{:S(2)}) copy-start(f32[6,16]{1,0:T(8,128)} %refs_9_.1) | copy-start | bytes 1156
  6.1 31.0 %copy-start.7 = (f32[8,9]{1,0:T(8,128)S(1)}, f32[8,9]{1,0:T(8,128)}, u32[]{:S(2)}) copy-start(f32[8,9]{1,0:T(8,128)} %refs_10_.3) | copy-start | bytes 868
  6.1 31.0 %copy-start.9 = (s32[16]{0:T(128)S(1)}, s32[16]{0:T(128)}, u32[]{:S(2)}) copy-start(s32[16]{0:T(128)} %refs_11_.3) | copy-start | bytes 196
  6.1 31.0 %copy-start.10 = (f32[16]{0:T(128)S(1)}, f32[16]{0:T(128)}, u32[]{:S(2)}) copy-start(f32[16]{0:T(128)} %refs_12_.3) | copy-start | bytes 196
  6.1 31.0 %copy-start.11 = (f32[9]{0:T(128)S(1)}, f32[9]{0:T(128)}, u32[]{:S(2)}) copy-start(f32[9]{0:T(128)} %refs_13_.3) | copy-start | bytes 112
  6.1 15.6 %collective-permute-start.5 = (bf16[133,16,128]{2,1,0:T(8,128)(2,1)S(1)}, bf16[133,16,128]{2,1,0:T(8,128)(2,1)S(1)}, u32[]{:S(2)}, u32[]{:S(2)}) collective-permute-start(bf16[133,16,128]{2,1,0:T(8,128)(2,1)S(1)} %shard_map.124), channel_id=1, source_target_pairs={{0,2},{2,0},{1,3},{3,1},{4,6},{6,4},{5,7},{7,5},{8,10},{10,8},{9,1... | collective-permute-start | bytes 1634312 | tf_op jit(solution)/shard_map/ppermute | solution.py:627
  8.7 15.3 %collective-permute-start = (f32[9,8,16,128]{3,2,1,0:T(8,128)S(1)}, f32[9,8,16,128]{3,2,1,0:T(8,128)S(1)}, u32[]{:S(2)}, u32[]{:S(2)}) collective-permute-start(f32[9,8,16,128]{3,2,1,0:T(8,128)S(1)} %copy-done.1), channel_id=1, source_target_pairs={{0,1},{1,0},{2,3},{3,2},{4,5},{5,4},{6,7},{7,6},{8,9},{9,8},{10,11... | collective-permute-start | bytes 1769480 | tf_op jit(solution)/shard_map/ppermute | solution.py:623
  21.7 35.1 %collective-permute-start.6 = (bf16[133,16,128]{2,1,0:T(8,128)(2,1)S(1)}, bf16[133,16,128]{2,1,0:T(8,128)(2,1)S(1)}, u32[]{:S(2)}, u32[]{:S(2)}) collective-permute-start(bf16[133,16,128]{2,1,0:T(8,128)(2,1)S(1)} %collective-permute-done.5.refs_6_), channel_id=1, source_target_pairs={{0,1},{1,0},{2,3},{3,2},{4,5},{5,4},{6,7},{7,6},{8,9},{9,8},{10,11... | collective-permute-start | bytes 1634312 | tf_op jit(solution)/shard_map/ppermute | solution.py:623
  21.7 2.2 %collective-permute-start.2 = (f32[2,8,16,128]{3,2,1,0:T(8,128)S(1)}, f32[2,8,16,128]{3,2,1,0:T(8,128)S(1)}, u32[]{:S(2)}, u32[]{:S(2)}) collective-permute-start(f32[2,8,16,128]{3,2,1,0:T(8,128)S(1)} %copy-done.2), channel_id=1, source_target_pairs={{0,1},{1,0},{2,3},{3,2},{4,5},{5,4},{6,7},{7,6},{8,9},{9,8},{10,11... | collective-permute-start | bytes 393224 | tf_op jit(solution)/shard_map/ppermute | solution.py:623
  22.2 1.7 %collective-permute-start.3 = (f32[8,16,128]{2,1,0:T(8,128)S(1)}, f32[8,16,128]{2,1,0:T(8,128)S(1)}, u32[]{:S(2)}, u32[]{:S(2)}) collective-permute-start(f32[8,16,128]{2,1,0:T(8,128)S(1)} %copy-done.3), channel_id=1, source_target_pairs={{0,1},{1,0},{2,3},{3,2},{4,5},{5,4},{6,7},{7,6},{8,9},{9,8},{10,11... | collective-permute-start | bytes 196616 | tf_op jit(solution)/shard_map/ppermute | solution.py:623
  27.8 9.3 %collective-permute-start.4 = (bf16[52,16,128]{2,1,0:T(8,128)(2,1)S(1)}, bf16[52,16,128]{2,1,0:T(8,128)(2,1)S(1)}, u32[]{:S(2)}, u32[]{:S(2)}) collective-permute-start(bf16[52,16,128]{2,1,0:T(8,128)(2,1)S(1)} %get-tuple-element.12), channel_id=1, source_target_pairs={{1,4},{0,29},{5,8},{4,1},{9,12},{8,5},{13,16},{12,9},{17,20},{16,1... | collective-permute-start | bytes 638984 | tf_op jit(solution)/shard_map/ppermute | solution.py:673
  32.4 24.4 %collective-permute-start.7 = (bf16[26,16,128]{2,1,0:T(8,128)(2,1)S(1)}, bf16[26,16,128]{2,1,0:T(8,128)(2,1)S(1)}, u32[]{:S(2)}, u32[]{:S(2)}) collective-permute-start(bf16[26,16,128]{2,1,0:T(8,128)(2,1)S(1)} %get-tuple-element.19), channel_id=1, source_target_pairs={{1,6},{0,31},{3,4},{2,29},{5,10},{4,3},{7,8},{6,1},{9,14},{8,7},{1... | collective-permute-start | bytes 319496 | tf_op jit(solution)/shard_map/ppermute | solution.py:646
  56.8 12.0 %copy-start.8 = (s32[16,128]{1,0:T(8,128)S(1)}, s32[16,128]{1,0:T(8,128)}, u32[]{:S(2)}) copy-start(s32[16,128]{1,0:T(8,128)} %source_ref.1) | copy-start | bytes 24580
  67.1 1.7 %collective-permute-start.8 = (f32[39,16,128]{2,1,0:T(8,128)S(1)}, f32[39,16,128]{2,1,0:T(8,128)S(1)}, u32[]{:S(2)}, u32[]{:S(2)}) collective-permute-start(f32[39,16,128]{2,1,0:T(8,128)S(1)} %get-tuple-element.21.send_ref), channel_id=1, source_target_pairs={{0,1},{1,0},{2,3},{3,2},{4,5},{5,4},{6,7},{7,6},{8,9},{9,8},{10,11... | collective-permute-start | bytes 958472 | tf_op jit(solution)/shard_map/ppermute | solution.py:623

commit v2 on v1

v2 whole, which is shorter than its diff:
```python
import jax
import jax.numpy as jnp
from jax import lax
from jax.experimental import pallas as pl
from jax.experimental.pallas import tpu as pltpu
from jax.sharding import PartitionSpec as P

F32 = jnp.float32
BF16 = jnp.bfloat16
VMEM = pl.BlockSpec(memory_space=pltpu.VMEM)
SMEM = pl.BlockSpec(memory_space=pltpu.SMEM)
PAIRS = ((0, 1, 3), (0, 2, 4), (1, 2, 5))
LAT_TILES = 132
LON_TILES = 42
CORNER_TILES = 21


def iota(shape, axis):
    return lax.broadcasted_iota(jnp.int32, shape, axis)


def split(value):
    high = value.astype(BF16)
    low = (value - high.astype(F32)).astype(BF16)
    return high, low


def stack_rows(top, bottom):
    return jnp.concatenate([top, bottom], axis=0)


def halves(tile):
    wide = tile.astype(F32)
    return wide[:8], wide[8:]


def coag(adj, state, rate):
    out = list(adj)
    kn = {}
    for m, p, q in PAIRS:
        kn[m, p] = rate[q] * state[3 * p]
    for m in range(3):
        total = (2.0 * rate[m]) * state[3 * m]
        for p in range(m + 1, 3):
            total = total + kn[m, p]
        out[3 * m] = out[3 * m] - total * adj[3 * m]
        out[3 * m + 1] = out[3 * m + 1] + (2.0 * rate[m]) * (state[3 * m + 1] * adj[3 * m + 2])
    for m, p, q in PAIRS:
        d_vol = adj[3 * p + 1] - adj[3 * m + 1]
        d_six = adj[3 * p + 2] - adj[3 * m + 2]
        inner = d_vol * state[3 * m + 1] + d_six * state[3 * m + 2] - adj[3 * m] * state[3 * m]
        cross = (2.0 * rate[q]) * adj[3 * p + 2]
        out[3 * p] = out[3 * p] + rate[q] * inner
        out[3 * m + 1] = out[3 * m + 1] + (kn[m, p] * d_vol + cross * state[3 * p + 1])
        out[3 * p + 1] = out[3 * p + 1] + cross * state[3 * m + 1]
        out[3 * m + 2] = out[3 * m + 2] + kn[m, p] * d_six
    return out


def lane_roll(value, shift):
    return pltpu.roll(value, shift, 1)


def weights(east, north):
    pos = jnp.maximum(east, 0.0)
    neg = jnp.minimum(east, 0.0)
    pos_1 = lane_roll(pos, 127)
    neg_1 = lane_roll(neg, 1)
    neg_2 = lane_roll(neg, 2)
    n_pos = jnp.maximum(north[2], 0.0)
    n_pos_1 = jnp.maximum(north[3], 0.0)
    n_neg_1 = jnp.minimum(north[1], 0.0)
    n_neg_2 = jnp.minimum(north[0], 0.0)
    centre = 1.0 + 1.5 * ((neg_1 - pos) + (n_neg_1 - n_pos))
    return (
        centre,
        0.5 * neg_2,
        -1.5 * neg_1 - 0.5 * neg_2,
        1.5 * pos + 0.5 * pos_1,
        -0.5 * pos_1,
        0.5 * n_neg_2,
        -1.5 * n_neg_1 - 0.5 * n_neg_2,
        1.5 * n_pos + 0.5 * n_pos_1,
        -0.5 * n_pos_1,
    )


def transported(rows, w):
    mid = rows[2]
    lon = (w[1] * lane_roll(mid, 2) + w[2] * lane_roll(mid, 1)) + (
        w[3] * lane_roll(mid, 127) + w[4] * lane_roll(mid, 126)
    )
    lat = (w[5] * rows[0] + w[6] * rows[1]) + (w[7] * rows[3] + w[8] * rows[4])
    return w[0] * mid + (lon + lat)


def level_scalars(z, rate_ref, speed_ref, class_ref):
    rate = [rate_ref[q, z] for q in range(6)]
    kind = class_ref[z]
    speed = [speed_ref[kind, t] for t in range(9)]
    return rate, speed


def halo_lanes(core, rows):
    lane = iota((rows, 128), 1)
    return jnp.where(core == 0, (lane >= 120).astype(jnp.int32), (lane < 8).astype(jnp.int32)) > 0


def load_kernel(*refs):
    given, kept, sems = refs[0:5], refs[5:10], refs[10]
    copies = [pltpu.make_async_copy(given[i], kept[i], sems.at[i]) for i in range(5)]
    for copy in copies:
        copy.start()
    for copy in copies:
        copy.wait()


def marked(mix, land, z):
    return jnp.where((land * (z == 0).astype(jnp.int32)) > 0, -mix, mix)


def lat_pack_kernel(lat_count, adj_ref, traj_ref, wind_ref, mix_ref, land_ref, *outs):
    core = lax.axis_index("lev")
    lat = lax.axis_index("lat")

    def fill(out_ref, high_rows):
        base = 8 if high_rows else 0
        sub = iota((8, 128), 0)
        keep = (sub >= 2) if high_rows else (sub < 6)

        def rolled(value, shift):
            return pltpu.roll(value, shift, 0)

        def tracer(t, _):
            v2s = []
            for l in range(8):
                adj = adj_ref[t, l, base : base + 8, :]
                high = adj.astype(BF16).astype(F32)
                low = adj - high
                tr = [traj_ref[k, t, l].astype(F32)[base : base + 8] for k in range(3)]
                if high_rows:
                    extra = (rolled(tr[0], 2), rolled(tr[1], 2), rolled(tr[1], 4))
                else:
                    extra = (rolled(tr[0], 6), rolled(tr[1], 6), rolled(tr[1], 4))
                v0 = jnp.where(keep, high, extra[0])
                v1 = jnp.where(keep, low, extra[1])
                v2s.append(jnp.where(keep, tr[2], extra[2]))
                out_ref[t * 8 + l] = stack_rows(v0, v1).astype(BF16)
            for j in range(4):
                out_ref[72 + t * 4 + j] = stack_rows(v2s[2 * j], v2s[2 * j + 1]).astype(BF16)
            return 0

        lax.fori_loop(0, 9, tracer, 0)

        def level(l, _):
            for q in range(3):
                if q == 2:
                    value = marked(mix_ref[l, base : base + 8, :], land_ref[base : base + 8, :], l + 8 * core)
                else:
                    value = wind_ref[1 - q, l, base : base + 8, :]
                high = value.astype(BF16).astype(F32)
                out_ref[108 + q * 8 + l] = stack_rows(high, value - high).astype(BF16)
            return 0

        lax.fori_loop(0, 8, level, 0)

    if lat_count == 2:
        pl.when(lat == 0)(lambda: fill(outs[0], True))
        pl.when(lat == 1)(lambda: fill(outs[0], False))
    else:
        fill(outs[0], True)
        fill(outs[1], False)


def lon_pack_kernel(lat_count, *refs):
    own, other = refs[0:4], refs[4:8]
    land_ref = refs[8]
    out_ref = refs[9]
    corners = refs[10:]
    core = lax.axis_index("lev")
    lat = lax.axis_index("lat")
    edge = jnp.where(core == 0, 0, 120)
    lane = iota((16, 128), 1)
    slot = lane // 8
    slot_16 = slot.astype(BF16)
    far = (jnp.bitwise_xor((lane // 4) % 2, core)).astype(F32).astype(BF16)
    zero_32 = jnp.zeros((16, 128), F32)
    zero_16 = jnp.zeros((16, 128), BF16)
    lowers = [lat == 1] if lat_count == 2 else [False, True]

    def gather(read, zero, at):
        acc = zero
        for s in range(2):
            for l in range(8):
                g = 8 * s + l
                shift = lax.rem(8 * g - edge + 128, 128)
                acc = jnp.where(at == g, lane_roll(read((own, other)[s], l, jnp.bitwise_xor(s, core)), shift), acc)
        return acc

    def emit(f, value):
        high, low = split(value)
        out_ref[2 * f] = high
        out_ref[2 * f + 1] = low
        for ref, lower in zip(corners, lowers):
            ref[f] = stack_rows(half(high, lower), half(low, lower)).astype(BF16)

    def half(tile, lower):
        top, bottom = halves(tile)
        return jnp.where(lower, top, bottom)

    def tracer(t, _):
        emit(t, gather(lambda r, l, h: r[0][t, l], zero_32, slot))
        tr = [gather(lambda r, l, h: r[1][k, t, l], zero_16, slot_16) for k in range(3)]
        both = jnp.where(far > 0, lane_roll(tr[0], jnp.where(core == 0, 4, 124)), tr[1])
        out_ref[24 + t] = tr[2]
        out_ref[33 + t] = both
        for ref, lower in zip(corners, lowers):
            ref[12 + t] = stack_rows(half(tr[2], lower), half(both, lower)).astype(BF16)
        return 0

    lax.fori_loop(0, 9, tracer, 0)
    emit(9, gather(lambda r, l, h: r[2][1, l], zero_32, slot))
    emit(10, gather(lambda r, l, h: r[2][0, l], zero_32, slot))
    land = land_ref[...]
    emit(11, gather(lambda r, l, h: marked(r[3][l], land, l + 8 * h) if l == 0 else r[3][l], zero_32, slot))


def zero_rows(ref, depth):
    zero = jnp.zeros((8, 128), F32)

    def clear(t, _):
        for z in range(depth):
            ref[t, z, 0:8, :] = zero
            ref[t, z, 24:32, :] = zero
        return 0

    lax.fori_loop(0, 9, clear, 0)


def zero_ends(ref):
    for t in range(9):
        for z in (0, 17):
            ref[t, z] = jnp.zeros(ref.shape[2:], F32)


def react(scalars, traj, a_in, b_s, z, sums):
    rate_ref, speed_ref, class_ref, prof_ref, coef_ref = scalars
    rate = [rate_ref[q, z] for q in range(6)]
    share = [prof_ref[z] * coef_ref[t] for t in range(9)]
    tiles = [traj(t).astype(F32) for t in range(9)]
    parts = []
    for rb in range(2):
        rows = slice(8 * rb, 8 * rb + 8)
        adj = [a_in(t, rows) for t in range(9)]
        done = coag(adj, [tile[rows] for tile in tiles], rate)
        for t in range(9):
            b_s[t, z + 1, rows, :] = done[t]
        parts.append([sums[rb][m] + sum(share[3 * m + j] * adj[3 * m + j] for j in range(3)) for m in range(3)])
    return parts


def mixed(scalars, b_s, d, deposit, c_out, z):
    rate_ref, speed_ref, class_ref, prof_ref, coef_ref = scalars
    kind = class_ref[z]
    below, above = d(z - 1), d(z)
    base = 1.0 - above - below
    base = jnp.where(z == 0, base - deposit, base)
    for t in range(9):
        speed = speed_ref[kind, t]
        c_out[t, z, 8:24, :] = (
            b_s[t, z + 1] * (base - speed) + b_s[t, z] * (below + speed) + b_s[t, z + 2] * above
        )


def moved(c_in, w_ref, a_to, z):
    for rb in range(2):
        rows = slice(8 * rb, 8 * rb + 8)
        w = [w_ref[i, z, rows, :] for i in range(9)]
        for t in range(9):
            shifted = [c_in[t, z, 8 * rb + 6 + i : 8 * rb + 14 + i, :] for i in range(5)]
            a_to[t, z, rows, :] = transported(shifted, w)


def no_sums():
    return [[jnp.zeros((8, 128), F32)] * 3, [jnp.zeros((8, 128), F32)] * 3]


def total(lat_count, step, sums):
    lat = lax.axis_index("lat")
    row = iota((16, 128), 0)
    sums = [stack_rows(sums[0][m], sums[1][m]) for m in range(3)]
    if step == 0:
        return sums
    low, high = 2 * step, 15 - 2 * step
    if lat_count == 2:
        good = ((row <= high) | (lat != 0)) & ((row >= low) | (lat == 0))
    else:
        good = (row <= high) & (row >= low)
    return [jnp.where(good, v, 0.0) for v in sums]


def pipeline(scalars, c_in, w_ref, a_s, b_s, traj_ref, k, d, deposit, c_out):
    def do_react(z, sums):
        return react(scalars, lambda t: traj_ref[k, t, z], lambda t, rows: a_s[t, z, rows, :], b_s, z, sums)

    def do_mixed(z):
        mixed(scalars, b_s, d, deposit, c_out, z)

    moved(c_in, w_ref, a_s, 0)
    moved(c_in, w_ref, a_s, 1)
    sums = do_react(0, no_sums())
    moved(c_in, w_ref, a_s, 2)
    sums = do_react(1, sums)

    def body(z, sums):
        do_mixed(z - 3)
        sums = do_react(z - 1, sums)
        moved(c_in, w_ref, a_s, z)
        return sums

    sums = lax.fori_loop(3, 16, body, sums)
    do_mixed(13)
    sums = do_react(15, sums)
    do_mixed(14)
    do_mixed(15)
    return sums


def first_kernel(lat_count, *refs):
    own, other = refs[0:4], refs[4:8]
    land_ref = refs[8]
    scalars = refs[9:14]
    c_out, em_ref = refs[14:16]
    b_s = refs[16]
    core = lax.axis_index("lev")
    zero_rows(c_out, 16)
    zero_ends(b_s)
    deposit = 0.1 + 0.3 * land_ref[...].astype(F32)

    def run(low, high):
        def level(r, z, l, sums):
            return react(scalars, lambda t: r[1][2, t, l], lambda t, rows: r[0][t, l, rows, :], b_s, z, sums)

        def top(z):
            return jnp.where(z == 7, 0.0, high[3][z])

        def mix(d, z):
            mixed(scalars, b_s, d, deposit, c_out, z)

        below_0 = jnp.zeros((16, 128), F32)
        sums = level(low, 0, 0, no_sums())
        sums = level(low, 1, 1, sums)
        mix(lambda z: below_0 if z < 0 else low[3][z], 0)
        sums = level(low, 2, 2, sums)

        def lower(z, sums):
            mix(lambda i: low[3][i], z - 2)
            return level(low, z, z, sums)

        sums = lax.fori_loop(3, 8, lower, sums)
        mix(lambda i: low[3][i], 6)
        sums = level(high, 8, 0, sums)
        mix(lambda i: low[3][i], 7)
        sums = level(high, 9, 1, sums)
        mix(lambda i: high[3][0] if i == 8 else low[3][7], 8)
        sums = level(high, 10, 2, sums)

        def upper(z, sums):
            mix(lambda i: high[3][i - 8], z - 2)
            return level(high, z, z - 8, sums)

        sums = lax.fori_loop(11, 16, upper, sums)
        mix(lambda i: high[3][i - 8], 14)
        mix(lambda i: high[3][6] if i == 14 else below_0, 15)
        sums = total(lat_count, 0, sums)
        for m in range(3):
            em_ref[m] = sums[m]

    pl.when(core == 0)(lambda: run(own, other))
    pl.when(core == 1)(lambda: run(other, own))


def second_kernel(lat_count, *refs):
    own, other = refs[0:4], refs[4:8]
    land_ref, lon_ref, c_own, em_in = refs[8:12]
    scalars = refs[12:17]
    rate_ref, speed_ref, class_ref, prof_ref, coef_ref = scalars
    traj_out, c_first, c_next, n_out, e_out, d_out, land_out, w_s, em_ref = refs[17:26]
    a_s, b_s, p_s = refs[26:]
    core = lax.axis_index("lev")
    lat = lax.axis_index("lat")
    edge = jnp.where(core == 0, 120, 0)
    halo = halo_lanes(core, 16)
    edge_f = jnp.where(core == 0, 123.5, 3.5).astype(F32)
    halo_16 = jnp.abs(iota((16, 128), 1).astype(F32) - edge_f).astype(BF16) <= jnp.full((16, 128), 3.5, BF16)
    row = iota((16, 128), 0)
    zero = jnp.zeros((16, 128), F32)
    z_lane = jnp.bitwise_xor(iota((8, 128), 1) // 8, 8 * (1 - core))
    zero_rows(c_first, 16)
    zero_rows(c_next, 16)
    zero_ends(b_s)
    d_out[0] = zero

    def shift_of(z):
        return lax.rem(edge + 128 - 8 * jnp.bitwise_xor(z, 8 * (1 - core)), 128)

    def by_lane(read):
        acc = jnp.zeros((8, 128), F32)
        for z in range(16):
            acc = jnp.where(z_lane == z, read(z), acc)
        return acc

    for f in range(9, 12):
        p_s[f] = lon_ref[2 * f].astype(F32) + lon_ref[2 * f + 1].astype(F32)
    rate = [by_lane(lambda z: rate_ref[q, z]) for q in range(6)]
    speeds = [by_lane(lambda z: speed_ref[class_ref[z], t]) for t in range(9)]
    for rb in range(2):
        rows = slice(8 * rb, 8 * rb + 8)
        adj = [(lon_ref[2 * t].astype(F32) + lon_ref[2 * t + 1].astype(F32))[rows] for t in range(9)]
        done = coag(adj, [lon_ref[24 + t].astype(F32)[rows] for t in range(9)], rate)
        mark = p_s[11, rows, :]
        land = ((mark < 0) & (z_lane == 0)).astype(F32)
        size = jnp.abs(mark)
        above = jnp.where(z_lane == 15, 0.0, size)
        below = jnp.where(z_lane == 0, 0.0, lane_roll(size, 8))
        base = 1.0 - above - below - jnp.where(z_lane == 0, 0.1 + 0.3 * land, 0.0)
        for t in range(9):
            under = jnp.where(z_lane == 0, 0.0, lane_roll(done[t], 8))
            p_s[t, rows, :] = (
                done[t] * (base - speeds[t]) + under * (below + speeds[t]) + lane_roll(done[t], 120) * above
            )
    land_halo = (lane_roll(p_s[11], shift_of(0)) < 0).astype(F32)
    deposit = 0.1 + 0.3 * jnp.where(halo, land_halo, land_ref[...].astype(F32))
    land_out[...] = deposit
    last_lat = lat == lat_count - 1

    for s in range(2):
        r = (own, other)[s]

        def assemble(l, _):
            z = 8 * jnp.bitwise_xor(s, core) + l
            shift = shift_of(z)
            for t in range(9):
                c_first[t, z, 8:24, :] = jnp.where(halo, lane_roll(p_s[t], shift), c_own[t, z, 8:24, :])
                traj_out[1, t, z] = jnp.where(halo_16, lane_roll(lon_ref[33 + t], shift), r[1][1, t, l])
                shift_0 = lax.rem(shift + jnp.where(core == 0, 4, 124), 128)
                traj_out[0, t, z] = jnp.where(halo_16, lane_roll(lon_ref[33 + t], shift_0), r[1][0, t, l])
            north = jnp.where(halo, lane_roll(p_s[9], shift), r[2][1, l])
            north = jnp.where((row == 15) & last_lat, 0.0, north)
            east = jnp.where(halo, lane_roll(p_s[10], shift), r[2][0, l])
            mix = jnp.where(halo, jnp.abs(lane_roll(p_s[11], shift)), r[3][l])
            n_out[z, 0:8, :] = zero[:8]
            n_out[z, 8:24, :] = north
            n_out[z, 24:32, :] = zero[:8]
            e_out[z] = east
            d_out[z + 1] = jnp.where(z == 15, 0.0, mix)
            return 0

        lax.fori_loop(0, 8, assemble, 0)

    def weigh(pair, _):
        for i in range(2):
            z = 2 * pair + i
            shifted = [n_out[z, 6 + j : 22 + j, :] for j in range(4)]
            for j, value in enumerate(weights(e_out[z], shifted)):
                w_s[j, z] = value
        return 0

    lax.fori_loop(0, 8, weigh, 0)
    sums = pipeline(
        scalars, c_first, w_s, a_s, b_s, traj_out, 1, lambda z: d_out[z + 1], land_out[...], c_next
    )
    sums = total(lat_count, 1, sums)
    for m in range(3):
        em_ref[m] = em_in[m] + sums[m]


def third_kernel(lat_count, *refs):
    traj_ref, d_ref, land_ref, w_ref, c_in, em_in = refs[0:6]
    scalars = refs[6:11]
    c_next, out_ref, em_ref = refs[11:14]
    a_s, b_s = refs[14:]
    zero_rows(c_next, 16)
    zero_ends(b_s)
    sums = pipeline(scalars, c_in, w_ref, a_s, b_s, traj_ref, 0, lambda z: d_ref[z + 1], land_ref[...], c_next)

    def last(pair, _):
        moved(c_next, w_ref, out_ref, 2 * pair)
        moved(c_next, w_ref, out_ref, 2 * pair + 1)
        return 0

    lax.fori_loop(0, 8, last, 0)
    sums = total(lat_count, 2, sums)
    for m in range(3):
        em_ref[m] = em_in[m] + sums[m]


def edge_kernel(lat_count, *refs):
    edges = 1 if lat_count == 2 else 2
    traj_ref, c_first, c_next, n_ref, e_ref, d_ref, land_ref, c_last, out_ref, em_ref = refs[0:10]
    lat_refs = refs[10 : 10 + 2 * edges]
    corner_refs = refs[10 + 2 * edges : 10 + 3 * edges]
    rate_ref, speed_ref, class_ref, prof_ref, coef_ref = refs[10 + 3 * edges : 15 + 3 * edges]
    keep_ref, send_ref = refs[15 + 3 * edges : 17 + 3 * edges]
    b_0, b_1, c_0, c_1, c_2, t_s, n_s, e_s, d_s, l_s, a_s, em_s, fin_s = refs[17 + 3 * edges :]
    core = lax.axis_index("lev")
    lat = lax.axis_index("lat")
    edge = jnp.where(core == 0, 120, 0)
    flip = 1 - core
    halo = halo_lanes(core, 8)
    sub = iota((8, 128), 0)
    zero = jnp.zeros((8, 128), F32)

    def rolled(value, shift):
        return pltpu.roll(value, shift, 0)

    def run(upper, e):
        own_at, halo_at = (0, 8) if upper else (8, 0)
        own_row = 8 if upper else 0
        corner_ref = corner_refs[e]
        keep = (sub < 6) if upper else (sub >= 2)
        starts = (6, 4, 0) if upper else (2, 4, 8)
        b_bufs, c_bufs = (b_0, b_1, b_0), (c_0, c_1, c_2)

        def shift_of(z):
            return lax.rem(edge + 128 - 8 * jnp.bitwise_xor(z, 8 * flip), 128)

        def corner_pair(tile, z):
            return halves(lane_roll(corner_ref[tile], shift_of(z)))

        land_c = sum(corner_pair(11, 0))
        land_l = jnp.where(core == 0, sum(halves(lat_refs[2 * e][124])), sum(halves(lat_refs[2 * e + 1][124])))
        l_s[pl.ds(halo_at, 8), :] = 0.1 + 0.3 * (jnp.where(halo, land_c, land_l) < 0).astype(F32)
        l_s[pl.ds(own_at, 8), :] = land_ref[pl.ds(own_row, 8), :]
        d_s[0] = jnp.zeros((16, 128), F32)

        def pads(t, _):
            for b in (b_0, b_1):
                b[t, 0] = zero
                b[t, 17] = zero
            for c in c_bufs:
                for z in range(16):
                    c[t, z, 0:8, :] = zero
                    c[t, z, 24:32, :] = zero
            return 0

        lax.fori_loop(0, 9, pads, 0)

        for s in range(2):
            msg = lat_refs[2 * e + s]

            def receive(pair, _):
                for i in range(2):
                    l = 2 * pair + i
                    z = 8 * jnp.bitwise_xor(s, core) + l
                    rate = [rate_ref[q, z] for q in range(6)]
                    adj, state = [], []
                    for t in range(9):
                        v0, v1 = halves(msg[t * 8 + l])
                        v2 = halves(msg[72 + t * 4 + pair])[i]
                        high, low = corner_pair(t, z)
                        adj.append(jnp.where(halo, high + low, jnp.where(keep, v0 + v1, 0.0)))
                        tr2, tr1 = corner_pair(12 + t, z)
                        tr0 = lane_roll(tr1, jnp.where(core == 0, 4, 124))
                        state.append(jnp.where(halo, tr2, v2))
                        if upper:
                            own1 = jnp.where(sub < 2, rolled(v1, 2), rolled(v2, 4))
                            own0 = rolled(v0, 2)
                        else:
                            own1 = jnp.where(sub >= 6, rolled(v1, 6), rolled(v2, 4))
                            own0 = rolled(v0, 6)
                        t_s[1, t, z, pl.ds(halo_at, 8), :] = jnp.where(halo, tr1, own1)
                        t_s[0, t, z, pl.ds(halo_at, 8), :] = jnp.where(halo, tr0, own0)
                        near = 1 if upper else 0
                        t_s[1, t, z, pl.ds(own_at, 8), :] = halves(traj_ref[1, t, z])[near]
                        t_s[0, t, z, pl.ds(own_at, 8), :] = halves(traj_ref[0, t, z])[near]
                    done = coag(adj, state, rate)
                    for t in range(9):
                        b_0[t, z + 1] = done[t]
                    winds = []
                    for q in range(3):
                        high, low = halves(msg[108 + q * 8 + l])
                        c_high, c_low = corner_pair(9 + q, z)
                        winds.append(jnp.where(halo, c_high + c_low, high + low))
                    n_s[z, 0:8, :] = zero
                    n_s[z, 24:32, :] = zero
                    n_s[z, pl.ds(8 + halo_at, 8), :] = winds[0]
                    n_s[z, pl.ds(8 + own_at, 8), :] = n_ref[z, pl.ds(8 + own_row, 8), :]
                    e_s[z, pl.ds(halo_at, 8), :] = winds[1]
                    e_s[z, pl.ds(own_at, 8), :] = e_ref[z, pl.ds(own_row, 8), :]
                    d_s[z + 1, pl.ds(halo_at, 8), :] = jnp.where(z == 15, 0.0, jnp.abs(winds[2]))
                    d_s[z + 1, pl.ds(own_at, 8), :] = d_ref[z + 1, pl.ds(own_row, 8), :]
                return 0

            lax.fori_loop(0, 4, receive, 0)

        for m in range(3):
            for part in range(3):
                em_s[m, 8 * part : 8 * part + 8, :] = zero

        def mix(step, z):
            at = halo_at if step == 0 else starts[step - 1]
            b, c = b_bufs[step], c_bufs[step]
            c_ref = (c_first, c_next, c_last)[step]
            kind = class_ref[z]
            below, above = d_s[z, at : at + 8, :], d_s[z + 1, at : at + 8, :]
            base = 1.0 - above - below
            base = jnp.where(z == 0, base - l_s[at : at + 8, :], base)
            for t in range(9):
                speed = speed_ref[kind, t]
                value = b[t, z + 1] * (base - speed) + b[t, z] * (below + speed) + b[t, z + 2] * above
                c[t, z, 8 + own_at : 16 + own_at, :] = c_ref[t, z, 8 + own_row : 16 + own_row, :]
                c[t, z, 8 + at : 16 + at, :] = value

        def move(step, z, sums):
            at = starts[step]
            c = c_bufs[step]
            shifted = [n_s[z, 6 + at + i : 14 + at + i, :] for i in range(4)]
            w = weights(e_s[z, at : at + 8, :], shifted)
            adj = []
            for t in range(9):
                rows = [c[t, z, 6 + at + i : 14 + at + i, :] for i in range(5)]
                adj.append(transported(rows, w))
            if step == 2:
                for t in range(9):
                    fin_s[e, t, z] = adj[t]
                return sums
            share = [prof_ref[z] * coef_ref[t] for t in range(9)]
            sums = [sums[m] + sum(share[3 * m + j] * adj[3 * m + j] for j in range(3)) for m in range(3)]
            rate = [rate_ref[q, z] for q in range(6)]
            state = [t_s[1 - step, t, z, at : at + 8, :] for t in range(9)]
            done = coag(adj, state, rate)
            for t in range(9):
                b_bufs[step + 1][t, z + 1] = done[t]
            return sums

        def count(step, sums):
            at = starts[step]
            buf_row = sub + at
            rows = 2 + 2 * step
            if upper:
                good = (buf_row >= 8 - rows) & (buf_row < 8)
            else:
                good = (buf_row >= 8) & (buf_row < 8 + rows)
            for m in range(3):
                em_s[m, at : at + 8, :] = em_s[m, at : at + 8, :] + jnp.where(good, sums[m], 0.0)

        none = [zero, zero, zero]
        mix(0, 0)
        mix(0, 1)
        sums = move(0, 0, none)
        mix(0, 2)
        sums = move(0, 1, sums)

        def first(z, sums):
            mix(0, z + 1)
            sums = move(0, z, sums)
            mix(1, z - 2)
            return sums

        sums = lax.fori_loop(2, 15, first, sums)
        sums = move(0, 15, sums)
        mix(1, 13)
        mix(1, 14)
        mix(1, 15)
        count(0, sums)
        sums = move(1, 0, none)
        sums = move(1, 1, sums)

        def second(z, sums):
            sums = move(1, z, sums)
            mix(2, z - 2)
            return sums

        sums = lax.fori_loop(2, 16, second, sums)
        mix(2, 14)
        mix(2, 15)
        count(1, sums)

        def third(pair, _):
            move(2, 2 * pair, none)
            move(2, 2 * pair + 1, none)
            return 0

        lax.fori_loop(0, 8, third, 0)
        for m in range(3):
            a_s[e, m] = em_s[m, own_at : own_at + 8, :]

    def finish(has_upper, has_lower, e_upper, e_lower):
        mine = (iota((16, 128), 1) < 64) == (core == 0)
        row8 = sub

        def rows_of(t, z):
            low = out_ref[t, z, 0:8, :]
            high = out_ref[t, z, 8:16, :]
            if has_upper:
                high = jnp.where(row8 >= 2, fin_s[e_upper, t, z], high)
            if has_lower:
                low = jnp.where(row8 < 6, fin_s[e_lower, t, z], low)
            return stack_rows(low, high)

        def tracer(t, _):
            for l in range(8):
                keep_ref[t, l] = rows_of(t, 8 * core + l)
            for l in range(4):
                z = 8 * (1 - core) + l
                send_ref[t * 4 + l] = jnp.where(mine, rows_of(t, z), lane_roll(rows_of(t, z + 4), 64))
            return 0

        lax.fori_loop(0, 9, tracer, 0)
        for m in range(3):
            low = em_ref[m, 0:8, :]
            high = em_ref[m, 8:16, :]
            if has_upper:
                high = high + a_s[e_upper, m]
            if has_lower:
                low = low + a_s[e_lower, m]
            send_ref[36 + m] = stack_rows(low, high)

    if lat_count == 2:

        def south():
            run(True, 0)
            finish(True, False, 0, 0)

        def north():
            run(False, 0)
            finish(False, True, 0, 0)

        pl.when(lat == 0)(south)
        pl.when(lat == 1)(north)
    else:
        run(True, 0)
        run(False, 1)
        finish(True, True, 0, 1)


def join_kernel(keep_ref, send_ref, recv_ref, source_ref, out_ref, em_ref):
    core = lax.axis_index("lev")
    mine = (iota((16, 128), 1) < 64) == (core == 0)

    def tracer(t, _):
        for l in range(4):
            got = recv_ref[t * 4 + l]
            out_ref[t, l] = jnp.where(mine, keep_ref[t, l], got)
            out_ref[t, l + 4] = jnp.where(mine, keep_ref[t, l + 4], lane_roll(got, 64))
        return 0

    lax.fori_loop(0, 9, tracer, 0)
    source = source_ref[...].astype(F32)
    for m in range(3):
        em_ref[m] = jnp.where(mine, send_ref[36 + m], recv_ref[36 + m]) * source


def shape(*dims, dtype=F32):
    return jax.ShapeDtypeStruct(dims, dtype)


def call(kernel, outs, scratch, *args, specs=None, mib=32):
    return pl.pallas_call(
        kernel,
        out_shape=outs,
        in_specs=specs or [VMEM] * len(args),
        out_specs=[VMEM] * len(outs),
        scratch_shapes=scratch,
        compiler_params=pltpu.CompilerParams(vmem_limit_bytes=mib * 1024 * 1024),
    )(*args)


def shards(
    adjoint_in,
    trajectory,
    courant,
    mixing,
    coag_rates,
    settle_speed,
    settle_class,
    emis_profile,
    emis_coef,
    land_mask,
    source_mask,
):
    lat_count = lax.axis_size("lat")
    lon_count = lax.axis_size("lon")
    edges = 1 if lat_count == 2 else 2
    swap = [(0, 1), (1, 0)]

    def over_lev(value):
        return lax.ppermute(value, "lev", swap)

    def lat_moves(messages):
        if edges == 1:
            return [lax.ppermute(messages[0], "lat", swap)]
        up = [(j, j + 1) for j in range(lat_count - 1)]
        down = [(j + 1, j) for j in range(lat_count - 1)]
        return [lax.ppermute(messages[1], "lat", down), lax.ppermute(messages[0], "lat", up)]

    def corner_moves(messages):
        def pairs(shift):
            found = []
            for i in range(lon_count):
                for x in range(lat_count):
                    y = 1 - x if edges == 1 else x + shift
                    if 0 <= y < lat_count:
                        right, left = (i + 1) % lon_count, (i - 1) % lon_count
                        found.append(((i * lat_count + x) * 2 + 1, (right * lat_count + y) * 2))
                        found.append(((i * lat_count + x) * 2, (left * lat_count + y) * 2 + 1))
            return found

        axes = ("lon", "lat", "lev")
        if edges == 1:
            return [lax.ppermute(messages[0], axes, pairs(0))]
        return [lax.ppermute(messages[1], axes, pairs(-1)), lax.ppermute(messages[0], axes, pairs(1))]

    def bind(kernel):
        def run(*refs):
            return kernel(lat_count, *refs)

        return run

    given = (adjoint_in, trajectory, courant, mixing)
    other = tuple(over_lev(value) for value in given)
    *own, land = call(
        load_kernel,
        [jax.ShapeDtypeStruct(v.shape, v.dtype) for v in given + (land_mask,)],
        [pltpu.SemaphoreType.DMA((5,))],
        *[pltpu.with_memory_space_constraint(v, pltpu.HBM) for v in given + (land_mask,)],
        specs=[pl.BlockSpec(memory_space=pltpu.HBM)] * 5,
        mib=16,
    )
    lon_out, *corner_out = call(
        bind(lon_pack_kernel),
        [shape(LON_TILES, 16, 128, dtype=BF16)] + [shape(CORNER_TILES, 16, 128, dtype=BF16)] * edges,
        [],
        *own,
        *other,
        land,
        mib=16,
    )
    lat_out = call(
        bind(lat_pack_kernel), [shape(LAT_TILES, 16, 128, dtype=BF16)] * edges, [], *own, land, mib=16
    )
    lat_in = lat_moves(lat_out)
    lon_pairs = []
    for i in range(lon_count):
        lon_pairs.append((2 * i + 1, 2 * ((i + 1) % lon_count)))
        lon_pairs.append((2 * i, 2 * ((i - 1) % lon_count) + 1))
    lon_in = lax.ppermute(lon_out, ("lon", "lev"), lon_pairs)
    corner_in = corner_moves(corner_out)
    scalars = (coag_rates, settle_speed, settle_class, emis_profile, emis_coef)
    state = pltpu.VMEM((9, 16, 16, 128), F32)
    between = pltpu.VMEM((9, 18, 16, 128), F32)
    padded = shape(9, 16, 32, 128)
    c_own, emis = call(
        bind(first_kernel),
        [padded, shape(3, 16, 128)],
        [between],
        *own,
        *other,
        land,
        *scalars,
        specs=[VMEM] * 9 + [SMEM] * 5,
    )
    lon_in, c_own = lax.optimization_barrier((lon_in, c_own))
    traj_all, c_first, c_next, north, east, mix, land_all, weight, emis = call(
        bind(second_kernel),
        [
            shape(2, 9, 16, 16, 128, dtype=BF16),
            padded,
            padded,
            shape(16, 32, 128),
            shape(16, 16, 128),
            shape(17, 16, 128),
            shape(16, 128),
            shape(9, 16, 16, 128),
            shape(3, 16, 128),
        ],
        [state, between, pltpu.VMEM((12, 16, 128), F32)],
        *own,
        *other,
        land,
        lon_in,
        c_own,
        emis,
        *scalars,
        specs=[VMEM] * 12 + [SMEM] * 5,
    )
    c_next, *lat_in = lax.optimization_barrier((c_next, *lat_in))
    c_last, final, emis = call(
        bind(third_kernel),
        [padded, shape(9, 16, 16, 128), shape(3, 16, 128)],
        [state, between],
        traj_all,
        mix,
        land_all,
        weight,
        c_next,
        emis,
        *scalars,
        specs=[VMEM] * 6 + [SMEM] * 5,
    )
    inner = (traj_all, c_first, c_next, north, east, mix, land_all, c_last, final, emis)
    lat_all = []
    for value in lat_in:
        lat_all += [value, over_lev(value)]
    keep, send = call(
        bind(edge_kernel),
        [shape(9, 8, 16, 128), shape(39, 16, 128)],
        [
            pltpu.VMEM((9, 18, 8, 128), F32),
            pltpu.VMEM((9, 18, 8, 128), F32),
            pltpu.VMEM((9, 16, 32, 128), F32),
            pltpu.VMEM((9, 16, 32, 128), F32),
            pltpu.VMEM((9, 16, 32, 128), F32),
            pltpu.VMEM((2, 9, 16, 16, 128), F32),
            pltpu.VMEM((16, 32, 128), F32),
            pltpu.VMEM((16, 16, 128), F32),
            pltpu.VMEM((17, 16, 128), F32),
            pltpu.VMEM((16, 128), F32),
            pltpu.VMEM((edges, 3, 8, 128), F32),
            pltpu.VMEM((3, 24, 128), F32),
            pltpu.VMEM((edges, 9, 16, 8, 128), F32),
        ],
        *inner,
        *lat_all,
        *corner_in,
        *scalars,
        specs=[VMEM] * (10 + 3 * edges) + [SMEM] * 5,
        mib=40,
    )
    recv = over_lev(send)
    out, emis = call(
        join_kernel, [shape(9, 8, 16, 128), shape(3, 16, 128)], [], keep, send, recv, source_mask
    )
    return (out, emis)


def solution(mesh):
    return jax.shard_map(
        shards,
        mesh=mesh,
        in_specs=(
            P(None, "lev", "lat", "lon"),
            P(None, None, "lev", "lat", "lon"),
            P(None, "lev", "lat", "lon"),
            P("lev", "lat", "lon"),
            P(),
            P(),
            P(),
            P(),
            P(),
            P("lat", "lon"),
            P("lat", "lon"),
        ),
        out_specs=(P(None, "lev", "lat", "lon"), P(None, "lat", "lon")),
        check_vma=False,
    )
```

time: 70.7 us -> 44.2 us (0.63)
  waiting for transfers between devices: 19.7 us -> 3.86 us
  Pallas kernels: 35.6 us -> 26.1 us
  local copies, waits for them, and re-layouts: 4.71 us -> 0.05 us
  starting transfers between devices: 9.56 us -> 13.3 us
    ppermute x1, waiting for transfers between devices: 12.8 us -> 0.01 us  [lat_moves(): return [lax.ppermute(messages[0], 'lat', swap)]]
    pallas_call x5 -> x8, Pallas kernels: 35.6 us -> 26.1 us  [call(): pl.pallas_call(kernel, out_shape=outs, in_specs=specs or [VMEM] * len(arg...]
    unnamed x24 -> x16, local copies, waits for them, and re-layouts: 4.71 us -> 0.05 us
    ppermute x1, starting transfers between devices: 1.07 us -> 4.47 us  [corner_moves(): return [lax.ppermute(messages[0], axes, pairs(0))]]
    ppermute x1, waiting for transfers between devices: 3.6 us -> 1.31 us  [shards(): lon_in = lax.ppermute(lon_out, ('lon', 'lev'), lon_pairs)]
    ppermute x6, waiting for transfers between devices: 3.32 us -> 2.54 us  [over_lev(): return lax.ppermute(value, 'lev', swap)]
  transfers between devices with their start and end apart: 9 -> 9, of which waited for: 4 -> 3; matrix products, arithmetic and copies ran while one was open for 0% -> 0% of each run, Pallas kernels for 34% -> 37%
where the time goes in v2:
time: 44.2 us; the launch traced here: 44.1 us
  Pallas kernels  26.1 us (59%)
  starting transfers between devices  13.3 us (30%)
  waiting for transfers between devices  3.86 us (9%)
  between operations  0.82 us (2%)
    pallas_call x8, Pallas kernels, call(): pl.pallas_call(kernel, out_shape=outs, in_specs=specs or [VMEM] * len(arg...  26.1 us
    ppermute x1, starting transfers between devices, shards(): lon_in = lax.ppermute(lon_out, ('lon', 'lev'), lon_pairs)  4.55 us
    ppermute x1, starting transfers between devices, corner_moves(): return [lax.ppermute(messages[0], axes, pairs(0))]  4.47 us
    ppermute x1, starting transfers between devices, lat_moves(): return [lax.ppermute(messages[0], 'lat', swap)]  2.98 us
    ppermute x6, waiting for transfers between devices, over_lev(): return lax.ppermute(value, 'lev', swap)  2.54 us
    ppermute x1, waiting for transfers between devices, shards(): lon_in = lax.ppermute(lon_out, ('lon', 'lev'), lon_pairs)  1.31 us
    ppermute x6, starting transfers between devices, over_lev(): return lax.ppermute(value, 'lev', swap)  1.25 us
  transfers between devices with their start and end apart: 9, of which 3 were waited for; matrix products, arithmetic and copies ran while one was open for 0% of the time, Pallas kernels for 37%

profile of v2, /device:TPU:0, one launch (start us, length us, event | category | flops | bytes accessed | tf_op | source)
XLA Modules:
  0.0 44.1 jit_solution(6474853179145684378)
XLA Ops:
  0.6 0.0 copy-start.6
  0.6 0.0 copy-start.7
  0.7 0.5 %collective-permute-start.1 = (bf16[3,9,8,16,128]{4,3,2,1,0:T(8,128)(2,1)}, bf16[3,9,8,16,128]{4,3,2,1,0:T(8,128)(2,1)S(1)}, u32[]{:S(2)}, u32[]{:S(2)}) collective-permute-start(bf16[3,9,8,16,128]{4,3,2,1,0:T(8,128)(2,1)} %refs_1_.1), channel_id=1, source_target_pairs={{0,1},{1,0},{2,3},{3,2},{4,5},{5,4},{6,7},{7,6},{8,9},{9,8},{10,11... | collective-permute-start | bytes 2654216 | tf_op jit(solution)/shard_map/ppermute | solution.py:789
  1.2 0.1 collective-permute-start
  1.2 1.4 %shard_map.122 = (f32[9,8,16,128]{3,2,1,0:T(8,128)S(1)}, bf16[3,9,8,16,128]{4,3,2,1,0:T(8,128)(2,1)S(1)}, f32[2,8,16,128]{3,2,1,0:T(8,128)S(1)}, f32[8,16,128]{2,1,0:T(8,128)S(1)}, s32[16,128]{1,0:T(8,128)S(1)}) custom-call(f32[9,8,16,128]{3,2,1,0:T(8,128)} %refs_0_.1, bf16[3,9,8,16,128]{4,3,2,1,0:T(8,128)(2,1)} %refs_1_.1, f32[2,8,16,128]{3,2,1,0:T(8,128)} %refs_2_.1, ...), custom_call_target="tpu_custom_call" | custom-call | tf_op jit(solution)/shard_map/pallas_call | solution.py:760
  2.7 0.0 copy-start
  2.7 0.0 copy-start.1
  2.7 0.0 copy-start.3
  2.7 0.0 copy-start.4
  2.7 0.0 copy-start.5
  2.7 0.3 shard_map.126
  3.0 3.0 %collective-permute-start.5 = (bf16[132,16,128]{2,1,0:T(8,128)(2,1)S(1)}, bf16[132,16,128]{2,1,0:T(8,128)(2,1)S(1)}, u32[]{:S(2)}, u32[]{:S(2)}) collective-permute-start(bf16[132,16,128]{2,1,0:T(8,128)(2,1)S(1)} %shard_map.126), channel_id=1, source_target_pairs={{0,2},{2,0},{1,3},{3,1},{4,6},{6,4},{5,7},{7,5},{8,10},{10,8},{9,1... | collective-permute-start | bytes 1622024 | tf_op jit(solution)/shard_map/ppermute | solution.py:793
  6.0 0.0 copy-done.6
  6.0 0.0 collective-permute-start.2
  6.0 0.0 copy-done.7
  6.0 0.5 %collective-permute-start.3 = (f32[8,16,128]{2,1,0:T(8,128)S(1)}, f32[8,16,128]{2,1,0:T(8,128)S(1)}, u32[]{:S(2)}, u32[]{:S(2)}) collective-permute-start(f32[8,16,128]{2,1,0:T(8,128)S(1)} %copy-done.7), channel_id=1, source_target_pairs={{0,1},{1,0},{2,3},{3,2},{4,5},{5,4},{6,7},{7,6},{8,9},{9,8},{10,11... | collective-permute-start | bytes 196616 | tf_op jit(solution)/shard_map/ppermute | solution.py:789
  6.5 0.9 %collective-permute-done.3.refs_7_ = f32[8,16,128]{2,1,0:T(8,128)S(1)} collective-permute-done((f32[8,16,128]{2,1,0:T(8,128)S(1)}, f32[8,16,128]{2,1,0:T(8,128)S(1)}, u32[]{:S(2)}, u32[]{:S(2)}) %collective-permute-start.3) | collective-permute-done | bytes 65568 | tf_op jit(solution)/shard_map/ppermute | solution.py:789
  7.4 0.0 collective-permute-done.2.refs_6_
  7.4 0.0 collective-permute-done.refs_4_
  7.4 0.0 collective-permute-done.1.refs_5_
  7.4 1.7 %shard_map.123 = (bf16[42,16,128]{2,1,0:T(8,128)(2,1)S(1)}, bf16[21,16,128]{2,1,0:T(8,128)(2,1)S(1)}) custom-call(f32[9,8,16,128]{3,2,1,0:T(8,128)S(1)} %get-tuple-element.29.refs_0_, bf16[3,9,8,16,128]{4,3,2,1,0:T(8,128)(2,1)S(1)} %get-tuple-element.30.refs_1_, f32[2,8,16,128]{3,2,1,0:T(8,128)S(1)} %get-tuple-element.31.refs_2_, ...), custom_call_target="tpu_custom_call" | custom-call | tf_op jit(solution)/shard_map/pallas_call | solution.py:760
  9.1 4.6 %collective-permute-start.4 = (bf16[42,16,128]{2,1,0:T(8,128)(2,1)S(1)}, bf16[42,16,128]{2,1,0:T(8,128)(2,1)S(1)}, u32[]{:S(2)}, u32[]{:S(2)}) collective-permute-start(bf16[42,16,128]{2,1,0:T(8,128)(2,1)S(1)} %get-tuple-element.34), channel_id=1, source_target_pairs={{1,4},{0,29},{5,8},{4,1},{9,12},{8,5},{13,16},{12,9},{17,20},{16,1... | collective-permute-start | bytes 516104 | tf_op jit(solution)/shard_map/ppermute | solution.py:848
  13.7 0.0 copy-done
  13.7 0.0 copy-done.1
  13.7 0.0 copy-done.3
  13.7 0.0 copy-done.4
  13.7 0.0 copy-done.5
  13.7 1.7 %shard_map.124 = (f32[9,16,32,128]{3,2,1,0:T(8,128)S(1)}, f32[3,16,128]{2,1,0:T(8,128)S(1)}) custom-call(f32[9,8,16,128]{3,2,1,0:T(8,128)S(1)} %get-tuple-element.29.refs_0_, bf16[3,9,8,16,128]{4,3,2,1,0:T(8,128)(2,1)S(1)} %get-tuple-element.30.refs_1_, f32[2,8,16,128]{3,2,1,0:T(8,128)S(1)} %get-tuple-element.31.refs_2_, ...), custom_call_target="tpu_custom_call" | custom-call | tf_op jit(solution)/shard_map/pallas_call | solution.py:760
  15.4 1.3 %collective-permute-done.4.refs_9_ = bf16[42,16,128]{2,1,0:T(8,128)(2,1)S(1)} collective-permute-done((bf16[42,16,128]{2,1,0:T(8,128)(2,1)S(1)}, bf16[42,16,128]{2,1,0:T(8,128)(2,1)S(1)}, u32[]{:S(2)}, u32[]{:S(2)}) %collective-permute-start.4) | collective-permute-done | bytes 172064 | tf_op jit(solution)/shard_map/ppermute | solution.py:848
  16.7 6.1 %shard_map.125 = (bf16[2,9,16,16,128]{4,3,2,1,0:T(8,128)(2,1)S(1)}, f32[9,16,32,128]{3,2,1,0:T(8,128)S(1)}, f32[9,16,32,128]{3,2,1,0:T(8,128)S(1)}, f32[16,32,12...) custom-call(f32[9,8,16,128]{3,2,1,0:T(8,128)S(1)} %get-tuple-element, ...), custom_call_target="tpu_custom_call" | custom-call | tf_op jit(solution)/shard_map/pallas_call | solution.py:760
  22.8 0.0 collective-permute-done.5.refs_10_
  22.8 0.1 collective-permute-start.6
  22.9 4.5 %collective-permute-start.7 = (bf16[21,16,128]{2,1,0:T(8,128)(2,1)S(1)}, bf16[21,16,128]{2,1,0:T(8,128)(2,1)S(1)}, u32[]{:S(2)}, u32[]{:S(2)}) collective-permute-start(bf16[21,16,128]{2,1,0:T(8,128)(2,1)S(1)} %get-tuple-element.53), channel_id=1, source_target_pairs={{1,6},{0,31},{3,4},{2,29},{5,10},{4,3},{7,8},{6,1},{9,14},{8,7},{1... | collective-permute-start | bytes 258056 | tf_op jit(solution)/shard_map/ppermute | solution.py:812
  27.4 5.1 %shard_map.127 = (f32[9,16,32,128]{3,2,1,0:T(8,128)S(1)}, f32[9,16,16,128]{3,2,1,0:T(8,128)S(1)}, f32[3,16,128]{2,1,0:T(8,128)S(1)}) custom-call(bf16[2,9,16,16,128]{4,3,2,1,0:T(8,128)(2,1)S(1)} %get-tuple-element.39.refs_0_, f32[17,16,128]{2,1,0:T(8,128)S(1)} %get-tuple-element.45.refs_1_.refs_5_, f32[16,128]{1,0:T(8,128)S(1)} %get-tuple-element.46.refs_2_.refs_6_, ...), custom_call_target="tpu_custom_call" | custom-call | tf_op jit(solution)/shard_map/pallas_call | solution.py:760
  32.5 0.0 collective-permute-done.7.refs_12_
  32.5 0.0 collective-permute-done.6.refs_11_
  32.5 0.0 copy-start.2
  32.5 8.4 %shard_map.128 = (f32[9,8,16,128]{3,2,1,0:T(8,128)S(1)}, f32[39,16,128]{2,1,0:T(8,128)S(1)}) custom-call(bf16[2,9,16,16,128]{4,3,2,1,0:T(8,128)(2,1)S(1)} %get-tuple-element.39.refs_0_, f32[9,16,32,128]{3,2,1,0:T(8,128)S(1)} %get-tuple-element.40.refs_1_, f32[9,16,32,128]{3,2,1,0:T(8,128)S(1)} %get-tuple-element.42.refs_4_.refs_2_, ...), custom_call_target="tpu_custom_call" | custom-call | tf_op jit(solution)/shard_map/pallas_call | solution.py:760
  40.9 0.1 collective-permute-start.8
  41.0 1.6 %collective-permute-done.8.recv_ref = f32[39,16,128]{2,1,0:T(8,128)S(1)} collective-permute-done((f32[39,16,128]{2,1,0:T(8,128)S(1)}, f32[39,16,128]{2,1,0:T(8,128)S(1)}, u32[]{:S(2)}, u32[]{:S(2)}) %collective-permute-start.8) | collective-permute-done | bytes 319520 | tf_op jit(solution)/shard_map/ppermute | solution.py:789
  42.6 0.0 copy-done.2
  42.6 1.5 %shard_map.129 = (f32[9,8,16,128]{3,2,1,0:T(8,128)}, f32[3,16,128]{2,1,0:T(8,128)}) custom-call(f32[9,8,16,128]{3,2,1,0:T(8,128)S(1)} %get-tuple-element.54.keep_ref, f32[39,16,128]{2,1,0:T(8,128)S(1)} %get-tuple-element.55.send_ref, f32[39,16,128]{2,1,0:T(8,128)S(1)} %collective-permute-done.8.recv_ref, s32[16,128]{1,0:T(8,128)S(1)} %copy-done.2), custom_call_target="tpu_custom_call" | custom-call | tf_op jit(solution)/shard_map/pallas_call | solution.py:760
Async XLA Ops:
  0.6 5.4 %copy-start.6 = (f32[2,8,16,128]{3,2,1,0:T(8,128)S(1)}, f32[2,8,16,128]{3,2,1,0:T(8,128)}, u32[]{:S(2)}) copy-start(f32[2,8,16,128]{3,2,1,0:T(8,128)} %refs_2_.1) | copy-start | bytes 393220
  0.6 5.3 %copy-start.7 = (f32[8,16,128]{2,1,0:T(8,128)S(1)}, f32[8,16,128]{2,1,0:T(8,128)}, u32[]{:S(2)}) copy-start(f32[8,16,128]{2,1,0:T(8,128)} %refs_3_.1) | copy-start | bytes 196612
  0.7 6.8 %collective-permute-start.1 = (bf16[3,9,8,16,128]{4,3,2,1,0:T(8,128)(2,1)}, bf16[3,9,8,16,128]{4,3,2,1,0:T(8,128)(2,1)S(1)}, u32[]{:S(2)}, u32[]{:S(2)}) collective-permute-start(bf16[3,9,8,16,128]{4,3,2,1,0:T(8,128)(2,1)} %refs_1_.1), channel_id=1, source_target_pairs={{0,1},{1,0},{2,3},{3,2},{4,5},{5,4},{6,7},{7,6},{8,9},{9,8},{10,11... | collective-permute-start | bytes 2654216 | tf_op jit(solution)/shard_map/ppermute | solution.py:789
  1.2 6.3 %collective-permute-start = (f32[9,8,16,128]{3,2,1,0:T(8,128)}, f32[9,8,16,128]{3,2,1,0:T(8,128)S(1)}, u32[]{:S(2)}, u32[]{:S(2)}) collective-permute-start(f32[9,8,16,128]{3,2,1,0:T(8,128)} %refs_0_.1), channel_id=1, source_target_pairs={{0,1},{1,0},{2,3},{3,2},{4,5},{5,4},{6,7},{7,6},{8,9},{9,8},{10,11... | collective-permute-start | bytes 1769480 | tf_op jit(solution)/shard_map/ppermute | solution.py:789
  2.7 11.0 %copy-start = (f32[6,16]{1,0:T(8,128)S(1)}, f32[6,16]{1,0:T(8,128)}, u32[]{:S(2)}) copy-start(f32[6,16]{1,0:T(8,128)} %refs_13_.5) | copy-start | bytes 1156
  2.7 11.0 %copy-start.1 = (f32[8,9]{1,0:T(8,128)S(1)}, f32[8,9]{1,0:T(8,128)}, u32[]{:S(2)}) copy-start(f32[8,9]{1,0:T(8,128)} %refs_14_.3) | copy-start | bytes 868
  2.7 11.0 %copy-start.3 = (s32[16]{0:T(128)S(1)}, s32[16]{0:T(128)}, u32[]{:S(2)}) copy-start(s32[16]{0:T(128)} %refs_15_.3) | copy-start | bytes 196
  2.7 11.0 %copy-start.4 = (f32[16]{0:T(128)S(1)}, f32[16]{0:T(128)}, u32[]{:S(2)}) copy-start(f32[16]{0:T(128)} %refs_16_.3) | copy-start | bytes 196
  2.7 11.0 %copy-start.5 = (f32[9]{0:T(128)S(1)}, f32[9]{0:T(128)}, u32[]{:S(2)}) copy-start(f32[9]{0:T(128)} %refs_17_.1) | copy-start | bytes 112
  3.0 19.8 %collective-permute-start.5 = (bf16[132,16,128]{2,1,0:T(8,128)(2,1)S(1)}, bf16[132,16,128]{2,1,0:T(8,128)(2,1)S(1)}, u32[]{:S(2)}, u32[]{:S(2)}) collective-permute-start(bf16[132,16,128]{2,1,0:T(8,128)(2,1)S(1)} %shard_map.126), channel_id=1, source_target_pairs={{0,2},{2,0},{1,3},{3,1},{4,6},{6,4},{5,7},{7,5},{8,10},{10,8},{9,1... | collective-permute-start | bytes 1622024 | tf_op jit(solution)/shard_map/ppermute | solution.py:793
  6.0 1.4 %collective-permute-start.2 = (f32[2,8,16,128]{3,2,1,0:T(8,128)S(1)}, f32[2,8,16,128]{3,2,1,0:T(8,128)S(1)}, u32[]{:S(2)}, u32[]{:S(2)}) collective-permute-start(f32[2,8,16,128]{3,2,1,0:T(8,128)S(1)} %copy-done.6), channel_id=1, source_target_pairs={{0,1},{1,0},{2,3},{3,2},{4,5},{5,4},{6,7},{7,6},{8,9},{9,8},{10,11... | collective-permute-start | bytes 393224 | tf_op jit(solution)/shard_map/ppermute | solution.py:789
  6.0 1.4 %collective-permute-start.3 = (f32[8,16,128]{2,1,0:T(8,128)S(1)}, f32[8,16,128]{2,1,0:T(8,128)S(1)}, u32[]{:S(2)}, u32[]{:S(2)}) collective-permute-start(f32[8,16,128]{2,1,0:T(8,128)S(1)} %copy-done.7), channel_id=1, source_target_pairs={{0,1},{1,0},{2,3},{3,2},{4,5},{5,4},{6,7},{7,6},{8,9},{9,8},{10,11... | collective-permute-start | bytes 196616 | tf_op jit(solution)/shard_map/ppermute | solution.py:789
  9.1 7.6 %collective-permute-start.4 = (bf16[42,16,128]{2,1,0:T(8,128)(2,1)S(1)}, bf16[42,16,128]{2,1,0:T(8,128)(2,1)S(1)}, u32[]{:S(2)}, u32[]{:S(2)}) collective-permute-start(bf16[42,16,128]{2,1,0:T(8,128)(2,1)S(1)} %get-tuple-element.34), channel_id=1, source_target_pairs={{1,4},{0,29},{5,8},{4,1},{9,12},{8,5},{13,16},{12,9},{17,20},{16,1... | collective-permute-start | bytes 516104 | tf_op jit(solution)/shard_map/ppermute | solution.py:848
  22.8 9.7 %collective-permute-start.6 = (bf16[132,16,128]{2,1,0:T(8,128)(2,1)S(1)}, bf16[132,16,128]{2,1,0:T(8,128)(2,1)S(1)}, u32[]{:S(2)}, u32[]{:S(2)}) collective-permute-start(bf16[132,16,128]{2,1,0:T(8,128)(2,1)S(1)} %collective-permute-done.5.refs_10_), channel_id=1, source_target_pairs={{0,1},{1,0},{2,3},{3,2},{4,5},{5,4},{6,7},{7,6},{8,9},{9,8},{10,11... | collective-permute-start | bytes 1622024 | tf_op jit(solution)/shard_map/ppermute | solution.py:789
  22.9 9.6 %collective-permute-start.7 = (bf16[21,16,128]{2,1,0:T(8,128)(2,1)S(1)}, bf16[21,16,128]{2,1,0:T(8,128)(2,1)S(1)}, u32[]{:S(2)}, u32[]{:S(2)}) collective-permute-start(bf16[21,16,128]{2,1,0:T(8,128)(2,1)S(1)} %get-tuple-element.53), channel_id=1, source_target_pairs={{1,6},{0,31},{3,4},{2,29},{5,10},{4,3},{7,8},{6,1},{9,14},{8,7},{1... | collective-permute-start | bytes 258056 | tf_op jit(solution)/shard_map/ppermute | solution.py:812
  32.5 10.1 %copy-start.2 = (s32[16,128]{1,0:T(8,128)S(1)}, s32[16,128]{1,0:T(8,128)}, u32[]{:S(2)}) copy-start(s32[16,128]{1,0:T(8,128)} %source_ref.1) | copy-start | bytes 24580
  40.9 1.7 %collective-permute-start.8 = (f32[39,16,128]{2,1,0:T(8,128)S(1)}, f32[39,16,128]{2,1,0:T(8,128)S(1)}, u32[]{:S(2)}, u32[]{:S(2)}) collective-permute-start(f32[39,16,128]{2,1,0:T(8,128)S(1)} %get-tuple-element.55.send_ref), channel_id=1, source_target_pairs={{0,1},{1,0},{2,3},{3,2},{4,5},{5,4},{6,7},{7,6},{8,9},{9,8},{10,11... | collective-permute-start | bytes 958472 | tf_op jit(solution)/shard_map/ppermute | solution.py:789

commit v3 on v2

--- a/solution.py
+++ b/solution.py
@@ -12,7 +12,6 @@
 PAIRS = ((0, 1, 3), (0, 2, 4), (1, 2, 5))
 LAT_TILES = 132
 LON_TILES = 42
-CORNER_TILES = 21
 
 
 def iota(shape, axis):
@@ -176,9 +175,7 @@
     own, other = refs[0:4], refs[4:8]
     land_ref = refs[8]
     out_ref = refs[9]
-    corners = refs[10:]
     core = lax.axis_index("lev")
-    lat = lax.axis_index("lat")
     edge = jnp.where(core == 0, 0, 120)
     lane = iota((16, 128), 1)
     slot = lane // 8
@@ -186,7 +183,6 @@
     far = (jnp.bitwise_xor((lane // 4) % 2, core)).astype(F32).astype(BF16)
     zero_32 = jnp.zeros((16, 128), F32)
     zero_16 = jnp.zeros((16, 128), BF16)
-    lowers = [lat == 1] if lat_count == 2 else [False, True]
 
     def gather(read, zero, at):
         acc = zero
@@ -201,12 +197,6 @@
         high, low = split(value)
         out_ref[2 * f] = high
         out_ref[2 * f + 1] = low
-        for ref, lower in zip(corners, lowers):
-            ref[f] = stack_rows(half(high, lower), half(low, lower)).astype(BF16)
-
-    def half(tile, lower):
-        top, bottom = halves(tile)
-        return jnp.where(lower, top, bottom)
 
     def tracer(t, _):
         emit(t, gather(lambda r, l, h: r[0][t, l], zero_32, slot))
@@ -214,8 +204,6 @@
         both = jnp.where(far > 0, lane_roll(tr[0], jnp.where(core == 0, 4, 124)), tr[1])
         out_ref[24 + t] = tr[2]
         out_ref[33 + t] = both
-        for ref, lower in zip(corners, lowers):
-            ref[12 + t] = stack_rows(half(tr[2], lower), half(both, lower)).astype(BF16)
         return 0
 
     lax.fori_loop(0, 9, tracer, 0)
@@ -299,79 +287,72 @@
     return [jnp.where(good, v, 0.0) for v in sums]
 
 
-def pipeline(scalars, c_in, w_ref, a_s, b_s, traj_ref, k, d, deposit, c_out):
-    def do_react(z, sums):
-        return react(scalars, lambda t: traj_ref[k, t, z], lambda t, rows: a_s[t, z, rows, :], b_s, z, sums)
-
-    def do_mixed(z):
-        mixed(scalars, b_s, d, deposit, c_out, z)
-
-    moved(c_in, w_ref, a_s, 0)
-    moved(c_in, w_ref, a_s, 1)
-    sums = do_react(0, no_sums())
-    moved(c_in, w_ref, a_s, 2)
-    sums = do_react(1, sums)
-
-    def body(z, sums):
-        do_mixed(z - 3)
-        sums = do_react(z - 1, sums)
-        moved(c_in, w_ref, a_s, z)
-        return sums
-
-    sums = lax.fori_loop(3, 16, body, sums)
-    do_mixed(13)
-    sums = do_react(15, sums)
-    do_mixed(14)
-    do_mixed(15)
-    return sums
+def pipeline(stages, carry=None):
+    stages = sorted(stages, key=lambda stage: -stage[0])
+    depth = stages[0][0]
+
+    def at(z, carry):
+        for lag, stage in stages:
+            if not isinstance(z, int) or 0 <= z - lag < 16:
+                carry = stage(z - lag, carry)
+        return carry
+
+    for z in range(depth):
+        carry = at(z, carry)
+    carry = lax.fori_loop(depth, 16, at, carry)
+    for z in range(16, 16 + depth):
+        carry = at(z, carry)
+    return carry
 
 
 def first_kernel(lat_count, *refs):
     own, other = refs[0:4], refs[4:8]
     land_ref = refs[8]
     scalars = refs[9:14]
-    c_out, em_ref = refs[14:16]
-    b_s = refs[16]
+    c_out, em_ref, traj_out, wind_out, mix_out = refs[14:19]
+    b_s = refs[19]
     core = lax.axis_index("lev")
     zero_rows(c_out, 16)
     zero_ends(b_s)
     deposit = 0.1 + 0.3 * land_ref[...].astype(F32)
+    nothing = jnp.zeros((16, 128), F32)
 
     def run(low, high):
         def level(r, z, l, sums):
+            for k in range(2):
+                for t in range(9):
+                    traj_out[k, t, z] = r[1][k, t, l]
+            for i in range(2):
+                wind_out[i, z] = r[2][i, l]
+            mix_out[z] = r[3][l]
             return react(scalars, lambda t: r[1][2, t, l], lambda t, rows: r[0][t, l, rows, :], b_s, z, sums)
 
-        def top(z):
-            return jnp.where(z == 7, 0.0, high[3][z])
-
-        def mix(d, z):
+        def mix(z):
+            def d(i):
+                if isinstance(i, int) and i in (-1, 15):
+                    return nothing
+                return mix_out[i]
+
             mixed(scalars, b_s, d, deposit, c_out, z)
 
-        below_0 = jnp.zeros((16, 128), F32)
-        sums = level(low, 0, 0, no_sums())
-        sums = level(low, 1, 1, sums)
-        mix(lambda z: below_0 if z < 0 else low[3][z], 0)
-        sums = level(low, 2, 2, sums)
+        sums = no_sums()
+        for z in range(3):
+            sums = level(low, z, z, sums)
+        mix(0)
 
         def lower(z, sums):
-            mix(lambda i: low[3][i], z - 2)
+            mix(z - 2)
             return level(low, z, z, sums)
 
         sums = lax.fori_loop(3, 8, lower, sums)
-        mix(lambda i: low[3][i], 6)
-        sums = level(high, 8, 0, sums)
-        mix(lambda i: low[3][i], 7)
-        sums = level(high, 9, 1, sums)
-        mix(lambda i: high[3][0] if i == 8 else low[3][7], 8)
-        sums = level(high, 10, 2, sums)
 
         def upper(z, sums):
-            mix(lambda i: high[3][i - 8], z - 2)
+            mix(z - 2)
             return level(high, z, z - 8, sums)
 
-        sums = lax.fori_loop(11, 16, upper, sums)
-        mix(lambda i: high[3][i - 8], 14)
-        mix(lambda i: high[3][6] if i == 14 else below_0, 15)
+        sums = lax.fori_loop(8, 16, upper, sums)
+        mix(14)
+        mix(15)
         sums = total(lat_count, 0, sums)
         for m in range(3):
             em_ref[m] = sums[m]
@@ -381,12 +362,11 @@
 
 
 def second_kernel(lat_count, *refs):
-    own, other = refs[0:4], refs[4:8]
-    land_ref, lon_ref, c_own, em_in = refs[8:12]
-    scalars = refs[12:17]
+    land_ref, lon_ref, c_own, em_in, traj_own, wind_own, mix_own = refs[0:7]
+    scalars = refs[7:12]
     rate_ref, speed_ref, class_ref, prof_ref, coef_ref = scalars
-    traj_out, c_first, c_next, n_out, e_out, d_out, land_out, w_s, em_ref = refs[17:26]
-    a_s, b_s, p_s = refs[26:]
+    traj_out, c_first, c_next, n_out, e_out, d_out, land_out, w_s, em_ref = refs[12:21]
+    a_s, b_s, p_s = refs[21:]
     core = lax.axis_index("lev")
     lat = lax.axis_index("lat")
     edge = jnp.where(core == 0, 120, 0)
@@ -434,45 +414,50 @@
     land_out[...] = deposit
     last_lat = lat == lat_count - 1
 
-    for s in range(2):
-        r = (own, other)[s]
-
-        def assemble(l, _):
-            z = 8 * jnp.bitwise_xor(s, core) + l
-            shift = shift_of(z)
-            for t in range(9):
-                c_first[t, z, 8:24, :] = jnp.where(halo, lane_roll(p_s[t], shift), c_own[t, z, 8:24, :])
-                traj_out[1, t, z] = jnp.where(halo_16, lane_roll(lon_ref[33 + t], shift), r[1][1, t, l])
-                shift_0 = lax.rem(shift + jnp.where(core == 0, 4, 124), 128)
-                traj_out[0, t, z] = jnp.where(halo_16, lane_roll(lon_ref[33 + t], shift_0), r[1][0, t, l])
-            north = jnp.where(halo, lane_roll(p_s[9], shift), r[2][1, l])
-            north = jnp.where((row == 15) & last_lat, 0.0, north)
-            east = jnp.where(halo, lane_roll(p_s[10], shift), r[2][0, l])
-            mix = jnp.where(halo, jnp.abs(lane_roll(p_s[11], shift)), r[3][l])
-            n_out[z, 0:8, :] = zero[:8]
-            n_out[z, 8:24, :] = north
-            n_out[z, 24:32, :] = zero[:8]
-            e_out[z] = east
-            d_out[z + 1] = jnp.where(z == 15, 0.0, mix)
-            return 0
-
-        lax.fori_loop(0, 8, assemble, 0)
-
-    def weigh(pair, _):
-        for i in range(2):
-            z = 2 * pair + i
-            shifted = [n_out[z, 6 + j : 22 + j, :] for j in range(4)]
-            for j, value in enumerate(weights(e_out[z], shifted)):
-                w_s[j, z] = value
-        return 0
-
-    lax.fori_loop(0, 8, weigh, 0)
-    sums = pipeline(
-        scalars, c_first, w_s, a_s, b_s, traj_out, 1, lambda z: d_out[z + 1], land_out[...], c_next
-    )
+    def assemble(z, sums):
+        shift = shift_of(z)
+        shift_0 = lax.rem(shift + jnp.where(core == 0, 4, 124), 128)
+        for t in range(9):
+            c_first[t, z, 8:24, :] = jnp.where(halo, lane_roll(p_s[t], shift), c_own[t, z, 8:24, :])
+            traj_out[1, t, z] = jnp.where(halo_16, lane_roll(lon_ref[33 + t], shift), traj_own[1, t, z])
+            traj_out[0, t, z] = jnp.where(halo_16, lane_roll(lon_ref[33 + t], shift_0), traj_own[0, t, z])
+        north = jnp.where(halo, lane_roll(p_s[9], shift), wind_own[1, z])
+        north = jnp.where((row == 15) & last_lat, 0.0, north)
+        east = jnp.where(halo, lane_roll(p_s[10], shift), wind_own[0, z])
+        mix = jnp.where(halo, jnp.abs(lane_roll(p_s[11], shift)), mix_own[z])
+        n_out[z, 0:8, :] = zero[:8]
+        n_out[z, 8:24, :] = north
+        n_out[z, 24:32, :] = zero[:8]
+        e_out[z] = east
+        d_out[z + 1] = jnp.where(z == 15, 0.0, mix)
+        return sums
+
+    def weigh(z, sums):
+        shifted = [n_out[z, 6 + j : 22 + j, :] for j in range(4)]
+        for j, value in enumerate(weights(e_out[z], shifted)):
+            w_s[j, z] = value
+        return sums
+
+    steps = stages(scalars, c_first, w_s, a_s, b_s, traj_out, 1, lambda z: d_out[z + 1], land_out[...], c_next, 2)
+    sums = pipeline([(0, assemble), (1, weigh)] + steps, no_sums())
     sums = total(lat_count, 1, sums)
     for m in range(3):
         em_ref[m] = em_in[m] + sums[m]
+
+
+def stages(scalars, c_in, w_ref, a_s, b_s, traj_ref, k, d, deposit, c_out, lag):
+    def move(z, sums):
+        moved(c_in, w_ref, a_s, z)
+        return sums
+
+    def do_react(z, sums):
+        return react(scalars, lambda t: traj_ref[k, t, z], lambda t, rows: a_s[t, z, rows, :], b_s, z, sums)
+
+    def mix(z, sums):
+        mixed(scalars, b_s, d, deposit, c_out, z)
+        return sums
+
+    return [(lag, move), (lag + 1, do_react), (lag + 3, mix)]
 
 
 def third_kernel(lat_count, *refs):
@@ -482,14 +467,13 @@
     a_s, b_s = refs[14:]
     zero_rows(c_next, 16)
     zero_ends(b_s)
-    sums = pipeline(scalars, c_in, w_ref, a_s, b_s, traj_ref, 0, lambda z: d_ref[z + 1], land_ref[...], c_next)
-
-    def last(pair, _):
-        moved(c_next, w_ref, out_ref, 2 * pair)
-        moved(c_next, w_ref, out_ref, 2 * pair + 1)
-        return 0
-
-    lax.fori_loop(0, 8, last, 0)
+    steps = stages(scalars, c_in, w_ref, a_s, b_s, traj_ref, 0, lambda z: d_ref[z + 1], land_ref[...], c_next, 0)
+
+    def last(z, sums):
+        moved(c_next, w_ref, out_ref, z)
+        return sums
+
+    sums = pipeline(steps + [(4, last)], no_sums())
     sums = total(lat_count, 2, sums)
     for m in range(3):
         em_ref[m] = em_in[m] + sums[m]
@@ -525,10 +509,15 @@
         def shift_of(z):
             return lax.rem(edge + 128 - 8 * jnp.bitwise_xor(z, 8 * flip), 128)
 
-        def corner_pair(tile, z):
-            return halves(lane_roll(corner_ref[tile], shift_of(z)))
-
-        land_c = sum(corner_pair(11, 0))
+        def corner(tile, z):
+            return lane_roll(halves(corner_ref[tile])[0 if upper else 1], shift_of(z))
+
+        def corner_sum(f, z):
+            high = halves(corner_ref[2 * f])[0 if upper else 1]
+            low = halves(corner_ref[2 * f + 1])[0 if upper else 1]
+            return lane_roll(high + low, shift_of(z))
+
+        land_c = corner_sum(11, 0)
         land_l = jnp.where(core == 0, sum(halves(lat_refs[2 * e][124])), sum(halves(lat_refs[2 * e + 1][124])))
         l_s[pl.ds(halo_at, 8), :] = 0.1 + 0.3 * (jnp.where(halo, land_c, land_l) < 0).astype(F32)
         l_s[pl.ds(own_at, 8), :] = land_ref[pl.ds(own_row, 8), :]
@@ -558,9 +547,8 @@
                     for t in range(9):
                         v0, v1 = halves(msg[t * 8 + l])
                         v2 = halves(msg[72 + t * 4 + pair])[i]
-                        high, low = corner_pair(t, z)
-                        adj.append(jnp.where(halo, high + low, jnp.where(keep, v0 + v1, 0.0)))
-                        tr2, tr1 = corner_pair(12 + t, z)
+                        adj.append(jnp.where(halo, corner_sum(t, z), jnp.where(keep, v0 + v1, 0.0)))
+                        tr2, tr1 = corner(24 + t, z), corner(33 + t, z)
                         tr0 = lane_roll(tr1, jnp.where(core == 0, 4, 124))
                         state.append(jnp.where(halo, tr2, v2))
                         if upper:
@@ -580,8 +568,7 @@
                     winds = []
                     for q in range(3):
                         high, low = halves(msg[108 + q * 8 + l])
-                        c_high, c_low = corner_pair(9 + q, z)
-                        winds.append(jnp.where(halo, c_high + c_low, high + low))
+                        winds.append(jnp.where(halo, corner_sum(9 + q, z), high + low))
                     n_s[z, 0:8, :] = zero
                     n_s[z, 24:32, :] = zero
                     n_s[z, pl.ds(8 + halo_at, 8), :] = winds[0]
@@ -646,43 +633,19 @@
                 em_s[m, at : at + 8, :] = em_s[m, at : at + 8, :] + jnp.where(good, sums[m], 0.0)
 
         none = [zero, zero, zero]
-        mix(0, 0)
-        mix(0, 1)
-        sums = move(0, 0, none)
-        mix(0, 2)
-        sums = move(0, 1, sums)
-
-        def first(z, sums):
-            mix(0, z + 1)
-            sums = move(0, z, sums)
-            mix(1, z - 2)
-            return sums
-
-        sums = lax.fori_loop(2, 15, first, sums)
-        sums = move(0, 15, sums)
-        mix(1, 13)
-        mix(1, 14)
-        mix(1, 15)
-        count(0, sums)
-        sums = move(1, 0, none)
-        sums = move(1, 1, sums)
-
-        def second(z, sums):
-            sums = move(1, z, sums)
-            mix(2, z - 2)
-            return sums
-
-        sums = lax.fori_loop(2, 16, second, sums)
-        mix(2, 14)
-        mix(2, 15)
-        count(1, sums)
-
-        def third(pair, _):
-            move(2, 2 * pair, none)
-            move(2, 2 * pair + 1, none)
-            return 0
-
-        lax.fori_loop(0, 8, third, 0)
+
+        def mixing(step):
+            def stage(z, sums):
+                mix(step, z)
+                return sums
+
+            return stage
+
+        def moving(step):
+            return lambda z, sums: move(step, z, sums)
+
+        count(0, pipeline([(0, mixing(0)), (1, moving(0)), (3, mixing(1))], none))
+        count(1, pipeline([(0, moving(1)), (2, mixing(2)), (3, moving(2))], none))
         for m in range(3):
             a_s[e, m] = em_s[m, own_at : own_at + 8, :]
 
@@ -793,24 +756,7 @@
             return [lax.ppermute(messages[0], "lat", swap)]
         up = [(j, j + 1) for j in range(lat_count - 1)]
         down = [(j + 1, j) for j in range(lat_count - 1)]
-        return [lax.ppermute(messages[1], "lat", down), lax.ppermute(messages[0], "lat", up)]
-
-    def corner_moves(messages):
-        def pairs(shift):
-            found = []
-            for i in range(lon_count):
-                for x in range(lat_count):
-                    y = 1 - x if edges == 1 else x + shift
-                    if 0 <= y < lat_count:
-                        right, left = (i + 1) % lon_count, (i - 1) % lon_count
-                        found.append(((i * lat_count + x) * 2 + 1, (right * lat_count + y) * 2))
-                        found.append(((i * lat_count + x) * 2, (left * lat_count + y) * 2 + 1))
-            return found
-
-        axes = ("lon", "lat", "lev")
-        if edges == 1:
-            return [lax.ppermute(messages[0], axes, pairs(0))]
-        return [lax.ppermute(messages[1], axes, pairs(-1)), lax.ppermute(messages[0], axes, pairs(1))]
+        return [lax.ppermute(messages[-1], "lat", down), lax.ppermute(messages[0], "lat", up)]
 
     def bind(kernel):
         def run(*refs):
@@ -828,15 +774,10 @@
         specs=[pl.BlockSpec(memory_space=pltpu.HBM)] * 5,
         mib=16,
     )
-    lon_out, *corner_out = call(
-        bind(lon_pack_kernel),
-        [shape(LON_TILES, 16, 128, dtype=BF16)] + [shape(CORNER_TILES, 16, 128, dtype=BF16)] * edges,
-        [],
-        *own,
-        *other,
-        land,
-        mib=16,
-    )
+    (lon_out,) = call(
+        bind(lon_pack_kernel), [shape(LON_TILES, 16, 128, dtype=BF16)], [], *own, *other, land, mib=16
+    )
+    *own, lon_out = lax.optimization_barrier((*own, lon_out))
     lat_out = call(
         bind(lat_pack_kernel), [shape(LAT_TILES, 16, 128, dtype=BF16)] * edges, [], *own, land, mib=16
     )
@@ -846,14 +787,19 @@
         lon_pairs.append((2 * i + 1, 2 * ((i + 1) % lon_count)))
         lon_pairs.append((2 * i, 2 * ((i - 1) % lon_count) + 1))
     lon_in = lax.ppermute(lon_out, ("lon", "lev"), lon_pairs)
-    corner_in = corner_moves(corner_out)
     scalars = (coag_rates, settle_speed, settle_class, emis_profile, emis_coef)
     state = pltpu.VMEM((9, 16, 16, 128), F32)
     between = pltpu.VMEM((9, 18, 16, 128), F32)
     padded = shape(9, 16, 32, 128)
-    c_own, emis = call(
+    c_own, emis, traj_own, wind_own, mix_own = call(
         bind(first_kernel),
-        [padded, shape(3, 16, 128)],
+        [
+            padded,
+            shape(3, 16, 128),
+            shape(2, 9, 16, 16, 128, dtype=BF16),
+            shape(2, 16, 16, 128),
+            shape(16, 16, 128),
+        ],
         [between],
         *own,
         *other,
@@ -862,6 +808,7 @@
         specs=[VMEM] * 9 + [SMEM] * 5,
     )
     lon_in, c_own = lax.optimization_barrier((lon_in, c_own))
+    corner_in = lat_moves([lon_in])
     traj_all, c_first, c_next, north, east, mix, land_all, weight, emis = call(
         bind(second_kernel),
         [
@@ -876,14 +823,15 @@
             shape(3, 16, 128),
         ],
         [state, between, pltpu.VMEM((12, 16, 128), F32)],
-        *own,
-        *other,
         land,
         lon_in,
         c_own,
         emis,
+        traj_own,
+        wind_own,
+        mix_own,
         *scalars,
-        specs=[VMEM] * 12 + [SMEM] * 5,
+        specs=[VMEM] * 7 + [SMEM] * 5,
     )
     c_next, *lat_in = lax.optimization_barrier((c_next, *lat_in))
     c_last, final, emis = call(

time: 44.2 us -> 39.8 us (0.900)
  starting transfers between devices: 13.3 us -> 9.86 us
  Pallas kernels: 26.1 us -> 23.2 us
  waiting for transfers between devices: 3.86 us -> 5.73 us
    ppermute x1 -> x0, starting transfers between devices: 4.47 us -> none  [corner_moves(): return [lax.ppermute(messages[0], axes, pairs(0))]]
    pallas_call x8, Pallas kernels: 26.1 us -> 23.2 us  [call(): pl.pallas_call(kernel, out_shape=outs, in_specs=specs or [VMEM] * len(arg...]
    ppermute x1 -> x2, starting transfers between devices: 2.98 us -> 4.67 us  [lat_moves(): return [lax.ppermute(messages[0], 'lat', swap)]]
    ppermute x1 -> x2, waiting for transfers between devices: 0.01 us -> 1.14 us  [lat_moves(): return [lax.ppermute(messages[0], 'lat', swap)]]
    ppermute x1, starting transfers between devices: 4.55 us -> 4.02 us  [shards(): lon_in = lax.ppermute(lon_out, ('lon', 'lev'), lon_pairs)]
    ppermute x6, waiting for transfers between devices: 2.54 us -> 3.01 us  [over_lev(): return lax.ppermute(value, 'lev', swap)]
  transfers between devices with their start and end apart: 9 -> 9, of which waited for: 3 -> 5; matrix products, arithmetic and copies ran while one was open for 0% -> 0% of each run, Pallas kernels for 37% -> 31%
where the time goes in v3:
time: 39.8 us; the launch traced here: 39.6 us
  Pallas kernels  23.2 us (58%)
  starting transfers between devices  9.86 us (25%)
  waiting for transfers between devices  5.73 us (14%)
  between operations  0.75 us (2%)
    pallas_call x8, Pallas kernels, call(): pl.pallas_call(kernel, out_shape=outs, in_specs=specs or [VMEM] * len(arg...  23.2 us
    ppermute x2, starting transfers between devices, lat_moves(): return [lax.ppermute(messages[0], 'lat', swap)]  4.67 us
    ppermute x1, starting transfers between devices, shards(): lon_in = lax.ppermute(lon_out, ('lon', 'lev'), lon_pairs)  4.02 us
    ppermute x6, waiting for transfers between devices, over_lev(): return lax.ppermute(value, 'lev', swap)  3.01 us
    ppermute x1, waiting for transfers between devices, shards(): lon_in = lax.ppermute(lon_out, ('lon', 'lev'), lon_pairs)  1.57 us
    ppermute x6, starting transfers between devices, over_lev(): return lax.ppermute(value, 'lev', swap)  1.18 us
    ppermute x2, waiting for transfers between devices, lat_moves(): return [lax.ppermute(messages[0], 'lat', swap)]  1.14 us
  transfers between devices with their start and end apart: 9, of which 5 were waited for; matrix products, arithmetic and copies ran while one was open for 0% of the time, Pallas kernels for 31%

profile of v3, /device:TPU:0, one launch (start us, length us, event | category | flops | bytes accessed | tf_op | source)
XLA Modules:
  0.0 39.6 jit_solution(2491056778693520622)
XLA Ops:
  0.6 0.5 %collective-permute-start.1 = (bf16[3,9,8,16,128]{4,3,2,1,0:T(8,128)(2,1)}, bf16[3,9,8,16,128]{4,3,2,1,0:T(8,128)(2,1)S(1)}, u32[]{:S(2)}, u32[]{:S(2)}) collective-permute-start(bf16[3,9,8,16,128]{4,3,2,1,0:T(8,128)(2,1)} %refs_1_.1), channel_id=1, source_target_pairs={{0,1},{1,0},{2,3},{3,2},{4,5},{5,4},{6,7},{7,6},{8,9},{9,8},{10,11... | collective-permute-start | bytes 2654216 | tf_op jit(solution)/shard_map/ppermute | solution.py:752
  1.1 0.1 collective-permute-start
  1.2 0.4 %collective-permute-start.2 = (f32[2,8,16,128]{3,2,1,0:T(8,128)}, f32[2,8,16,128]{3,2,1,0:T(8,128)S(1)}, u32[]{:S(2)}, u32[]{:S(2)}) collective-permute-start(f32[2,8,16,128]{3,2,1,0:T(8,128)} %refs_2_.1), channel_id=1, source_target_pairs={{0,1},{1,0},{2,3},{3,2},{4,5},{5,4},{6,7},{7,6},{8,9},{9,8},{10,11... | collective-permute-start | bytes 393224 | tf_op jit(solution)/shard_map/ppermute | solution.py:752
  1.7 0.1 collective-permute-start.3
  1.7 1.4 %shard_map.122 = (f32[9,8,16,128]{3,2,1,0:T(8,128)S(1)}, bf16[3,9,8,16,128]{4,3,2,1,0:T(8,128)(2,1)S(1)}, f32[2,8,16,128]{3,2,1,0:T(8,128)S(1)}, f32[8,16,128]{2,1,0:T(8,128)S(1)}, s32[16,128]{1,0:T(8,128)S(1)}) custom-call(f32[9,8,16,128]{3,2,1,0:T(8,128)} %refs_0_.1, bf16[3,9,8,16,128]{4,3,2,1,0:T(8,128)(2,1)} %refs_1_.1, f32[2,8,16,128]{3,2,1,0:T(8,128)} %refs_2_.1, ...), custom_call_target="tpu_custom_call" | custom-call | tf_op jit(solution)/shard_map/pallas_call | solution.py:723
  3.1 1.4 %collective-permute-done.3.refs_7_ = f32[8,16,128]{2,1,0:T(8,128)S(1)} collective-permute-done((f32[8,16,128]{2,1,0:T(8,128)}, f32[8,16,128]{2,1,0:T(8,128)S(1)}, u32[]{:S(2)}, u32[]{:S(2)}) %collective-permute-start.3) | collective-permute-done | bytes 65568 | tf_op jit(solution)/shard_map/ppermute | solution.py:752
  4.5 0.0 collective-permute-done.2.refs_6_
  4.5 0.0 collective-permute-done.refs_4_
  4.5 0.0 collective-permute-done.1.refs_5_
  4.5 0.0 copy-start
  4.6 0.0 copy-start.1
  4.6 0.0 copy-start.3
  4.6 0.0 copy-start.4
  4.6 0.0 copy-start.5
  4.6 1.6 %shard_map.123 = bf16[42,16,128]{2,1,0:T(8,128)(2,1)S(1)} custom-call(f32[9,8,16,128]{3,2,1,0:T(8,128)S(1)} %get-tuple-element.41.refs_0_, bf16[3,9,8,16,128]{4,3,2,1,0:T(8,128)(2,1)S(1)} %get-tuple-element.42.refs_1_, f32[2,8,16,128]{3,2,1,0:T(8,128)S(1)} %get-tuple-element.43.refs_2_, f32[8,16,128]{2,1,0:T(8,128)S(1)} %get-tuple-element.44.refs_3_, ...), custom_call_target="tpu_custom_call" | custom-call | tf_op jit(solution)/shard_map/pallas_call | solution.py:723
  6.3 0.3 shard_map.126
  6.5 2.9 %collective-permute-start.5 = (bf16[132,16,128]{2,1,0:T(8,128)(2,1)S(1)}, bf16[132,16,128]{2,1,0:T(8,128)(2,1)S(1)}, u32[]{:S(2)}, u32[]{:S(2)}) collective-permute-start(bf16[132,16,128]{2,1,0:T(8,128)(2,1)S(1)} %shard_map.126), channel_id=1, source_target_pairs={{0,2},{2,0},{1,3},{3,1},{4,6},{6,4},{5,7},{7,5},{8,10},{10,8},{9,1... | collective-permute-start | bytes 1622024 | tf_op jit(solution)/shard_map/ppermute | solution.py:756
  9.5 4.0 %collective-permute-start.4 = (bf16[42,16,128]{2,1,0:T(8,128)(2,1)S(1)}, bf16[42,16,128]{2,1,0:T(8,128)(2,1)S(1)}, u32[]{:S(2)}, u32[]{:S(2)}) collective-permute-start(bf16[42,16,128]{2,1,0:T(8,128)(2,1)S(1)} %shard_map.123), channel_id=1, source_target_pairs={{1,4},{0,29},{5,8},{4,1},{9,12},{8,5},{13,16},{12,9},{17,20},{16,1... | collective-permute-start | bytes 516104 | tf_op jit(solution)/shard_map/ppermute | solution.py:789
  13.5 0.0 copy-done
  13.5 0.0 copy-done.1
  13.5 0.0 copy-done.3
  13.5 0.0 copy-done.4
  13.5 0.0 copy-done.5
  13.5 1.9 %shard_map.124 = (f32[9,16,32,128]{3,2,1,0:T(8,128)S(1)}, f32[3,16,128]{2,1,0:T(8,128)S(1)}, bf16[2,9,16,16,128]{4,3,2,1,0:T(8,128)(2,1)S(1)}, f32[2,16,16,128]{3,2,1,0:T(8,128)S(1)}, f32[16,16,128]{2,1,0:T(8,128)S(1)}) custom-call(f32[9,8,16,128]{3,2,1,0:T(8,128)S(1)} %get-tuple-element.41.refs_0_, ...), custom_call_target="tpu_custom_call" | custom-call | tf_op jit(solution)/shard_map/pallas_call | solution.py:723
  15.4 1.6 %collective-permute-done.4.refs_1_ = bf16[42,16,128]{2,1,0:T(8,128)(2,1)S(1)} collective-permute-done((bf16[42,16,128]{2,1,0:T(8,128)(2,1)S(1)}, bf16[42,16,128]{2,1,0:T(8,128)(2,1)S(1)}, u32[]{:S(2)}, u32[]{:S(2)}) %collective-permute-start.4) | collective-permute-done | bytes 172064 | tf_op jit(solution)/shard_map/ppermute | solution.py:789
  17.0 4.4 %shard_map.125 = (bf16[2,9,16,16,128]{4,3,2,1,0:T(8,128)(2,1)S(1)}, f32[9,16,32,128]{3,2,1,0:T(8,128)S(1)}, f32[9,16,32,128]{3,2,1,0:T(8,128)S(1)}, f32[16,32,12...) custom-call(s32[16,128]{1,0:T(8,128)S(1)} %get-tuple-element.35.refs, ...), custom_call_target="tpu_custom_call" | custom-call | tf_op jit(solution)/shard_map/pallas_call | solution.py:723
  21.4 0.7 %collective-permute-done.5.refs_10_ = bf16[132,16,128]{2,1,0:T(8,128)(2,1)S(1)} collective-permute-done((bf16[132,16,128]{2,1,0:T(8,128)(2,1)S(1)}, bf16[132,16,128]{2,1,0:T(8,128)(2,1)S(1)}, u32[]{:S(2)}, u32[]{:S(2)}) %collective-permute-start.5) | collective-permute-done | bytes 540704 | tf_op jit(solution)/shard_map/ppermute | solution.py:756
  22.0 0.0 collective-permute-start.6
  22.1 1.7 %collective-permute-start.7 = (bf16[42,16,128]{2,1,0:T(8,128)(2,1)S(1)}, bf16[42,16,128]{2,1,0:T(8,128)(2,1)S(1)}, u32[]{:S(2)}, u32[]{:S(2)}) collective-permute-start(bf16[42,16,128]{2,1,0:T(8,128)(2,1)S(1)} %collective-permute-done.4.refs_1_), channel_id=1, source_target_pairs={{0,2},{2,0},{1,3},{3,1},{4,6},{6,4},{5,7},{7,5},{8,10},{10,8},{9,1... | collective-permute-start | bytes 516104 | tf_op jit(solution)/shard_map/ppermute | solution.py:756
  23.8 4.6 %shard_map.127 = (f32[9,16,32,128]{3,2,1,0:T(8,128)S(1)}, f32[9,16,16,128]{3,2,1,0:T(8,128)S(1)}, f32[3,16,128]{2,1,0:T(8,128)S(1)}) custom-call(bf16[2,9,16,16,128]{4,3,2,1,0:T(8,128)(2,1)S(1)} %get-tuple-element.52.refs_0_, f32[17,16,128]{2,1,0:T(8,128)S(1)} %get-tuple-element.58.refs_1_.refs_5_, f32[16,128]{1,0:T(8,128)S(1)} %get-tuple-element.59.refs_2_.refs_6_, ...), custom_call_target="tpu_custom_call" | custom-call | tf_op jit(solution)/shard_map/pallas_call | solution.py:723
  28.4 0.5 %collective-permute-done.7.refs_12_ = bf16[42,16,128]{2,1,0:T(8,128)(2,1)S(1)} collective-permute-done((bf16[42,16,128]{2,1,0:T(8,128)(2,1)S(1)}, bf16[42,16,128]{2,1,0:T(8,128)(2,1)S(1)}, u32[]{:S(2)}, u32[]{:S(2)}) %collective-permute-start.7) | collective-permute-done | bytes 172064 | tf_op jit(solution)/shard_map/ppermute | solution.py:756
  28.8 0.0 collective-permute-done.6.refs_11_
  28.8 0.0 copy-start.2
  28.8 7.6 %shard_map.128 = (f32[9,8,16,128]{3,2,1,0:T(8,128)S(1)}, f32[39,16,128]{2,1,0:T(8,128)S(1)}) custom-call(bf16[2,9,16,16,128]{4,3,2,1,0:T(8,128)(2,1)S(1)} %get-tuple-element.52.refs_0_, f32[9,16,32,128]{3,2,1,0:T(8,128)S(1)} %get-tuple-element.53.refs_1_, f32[9,16,32,128]{3,2,1,0:T(8,128)S(1)} %get-tuple-element.55.refs_4_.refs_2_, ...), custom_call_target="tpu_custom_call" | custom-call | tf_op jit(solution)/shard_map/pallas_call | solution.py:723
  36.4 0.1 collective-permute-start.8
  36.5 1.6 %collective-permute-done.8.recv_ref = f32[39,16,128]{2,1,0:T(8,128)S(1)} collective-permute-done((f32[39,16,128]{2,1,0:T(8,128)S(1)}, f32[39,16,128]{2,1,0:T(8,128)S(1)}, u32[]{:S(2)}, u32[]{:S(2)}) %collective-permute-start.8) | collective-permute-done | bytes 319520 | tf_op jit(solution)/shard_map/ppermute | solution.py:752
  38.1 0.0 copy-done.2
  38.1 1.5 %shard_map.129 = (f32[9,8,16,128]{3,2,1,0:T(8,128)}, f32[3,16,128]{2,1,0:T(8,128)}) custom-call(f32[9,8,16,128]{3,2,1,0:T(8,128)S(1)} %get-tuple-element.66.keep_ref, f32[39,16,128]{2,1,0:T(8,128)S(1)} %get-tuple-element.67.send_ref, f32[39,16,128]{2,1,0:T(8,128)S(1)} %collective-permute-done.8.recv_ref, s32[16,128]{1,0:T(8,128)S(1)} %copy-done.2), custom_call_target="tpu_custom_call" | custom-call | tf_op jit(solution)/shard_map/pallas_call | solution.py:723
Async XLA Ops:
  0.6 3.9 %collective-permute-start.1 = (bf16[3,9,8,16,128]{4,3,2,1,0:T(8,128)(2,1)}, bf16[3,9,8,16,128]{4,3,2,1,0:T(8,128)(2,1)S(1)}, u32[]{:S(2)}, u32[]{:S(2)}) collective-permute-start(bf16[3,9,8,16,128]{4,3,2,1,0:T(8,128)(2,1)} %refs_1_.1), channel_id=1, source_target_pairs={{0,1},{1,0},{2,3},{3,2},{4,5},{5,4},{6,7},{7,6},{8,9},{9,8},{10,11... | collective-permute-start | bytes 2654216 | tf_op jit(solution)/shard_map/ppermute | solution.py:752
  1.1 3.4 %collective-permute-start = (f32[9,8,16,128]{3,2,1,0:T(8,128)}, f32[9,8,16,128]{3,2,1,0:T(8,128)S(1)}, u32[]{:S(2)}, u32[]{:S(2)}) collective-permute-start(f32[9,8,16,128]{3,2,1,0:T(8,128)} %refs_0_.1), channel_id=1, source_target_pairs={{0,1},{1,0},{2,3},{3,2},{4,5},{5,4},{6,7},{7,6},{8,9},{9,8},{10,11... | collective-permute-start | bytes 1769480 | tf_op jit(solution)/shard_map/ppermute | solution.py:752
  1.2 3.3 %collective-permute-start.2 = (f32[2,8,16,128]{3,2,1,0:T(8,128)}, f32[2,8,16,128]{3,2,1,0:T(8,128)S(1)}, u32[]{:S(2)}, u32[]{:S(2)}) collective-permute-start(f32[2,8,16,128]{3,2,1,0:T(8,128)} %refs_2_.1), channel_id=1, source_target_pairs={{0,1},{1,0},{2,3},{3,2},{4,5},{5,4},{6,7},{7,6},{8,9},{9,8},{10,11... | collective-permute-start | bytes 393224 | tf_op jit(solution)/shard_map/ppermute | solution.py:752
  1.7 2.9 %collective-permute-start.3 = (f32[8,16,128]{2,1,0:T(8,128)}, f32[8,16,128]{2,1,0:T(8,128)S(1)}, u32[]{:S(2)}, u32[]{:S(2)}) collective-permute-start(f32[8,16,128]{2,1,0:T(8,128)} %refs_3_.1), channel_id=1, source_target_pairs={{0,1},{1,0},{2,3},{3,2},{4,5},{5,4},{6,7},{7,6},{8,9},{9,8},{10,11... | collective-permute-start | bytes 196616 | tf_op jit(solution)/shard_map/ppermute | solution.py:752
  4.5 8.9 %copy-start = (f32[6,16]{1,0:T(8,128)S(1)}, f32[6,16]{1,0:T(8,128)}, u32[]{:S(2)}) copy-start(f32[6,16]{1,0:T(8,128)} %refs_13_.3) | copy-start | bytes 1156
  4.6 8.9 %copy-start.1 = (f32[8,9]{1,0:T(8,128)S(1)}, f32[8,9]{1,0:T(8,128)}, u32[]{:S(2)}) copy-start(f32[8,9]{1,0:T(8,128)} %refs_14_.1) | copy-start | bytes 868
  4.6 8.9 %copy-start.3 = (s32[16]{0:T(128)S(1)}, s32[16]{0:T(128)}, u32[]{:S(2)}) copy-start(s32[16]{0:T(128)} %refs_15_.1) | copy-start | bytes 196
  4.6 8.9 %copy-start.4 = (f32[16]{0:T(128)S(1)}, f32[16]{0:T(128)}, u32[]{:S(2)}) copy-start(f32[16]{0:T(128)} %refs_16_.1) | copy-start | bytes 196
  4.6 8.9 %copy-start.5 = (f32[9]{0:T(128)S(1)}, f32[9]{0:T(128)}, u32[]{:S(2)}) copy-start(f32[9]{0:T(128)} %refs_17_.1) | copy-start | bytes 112
  6.5 15.5 %collective-permute-start.5 = (bf16[132,16,128]{2,1,0:T(8,128)(2,1)S(1)}, bf16[132,16,128]{2,1,0:T(8,128)(2,1)S(1)}, u32[]{:S(2)}, u32[]{:S(2)}) collective-permute-start(bf16[132,16,128]{2,1,0:T(8,128)(2,1)S(1)} %shard_map.126), channel_id=1, source_target_pairs={{0,2},{2,0},{1,3},{3,1},{4,6},{6,4},{5,7},{7,5},{8,10},{10,8},{9,1... | collective-permute-start | bytes 1622024 | tf_op jit(solution)/shard_map/ppermute | solution.py:756
  9.5 7.5 %collective-permute-start.4 = (bf16[42,16,128]{2,1,0:T(8,128)(2,1)S(1)}, bf16[42,16,128]{2,1,0:T(8,128)(2,1)S(1)}, u32[]{:S(2)}, u32[]{:S(2)}) collective-permute-start(bf16[42,16,128]{2,1,0:T(8,128)(2,1)S(1)} %shard_map.123), channel_id=1, source_target_pairs={{1,4},{0,29},{5,8},{4,1},{9,12},{8,5},{13,16},{12,9},{17,20},{16,1... | collective-permute-start | bytes 516104 | tf_op jit(solution)/shard_map/ppermute | solution.py:789
  22.0 6.8 %collective-permute-start.6 = (bf16[132,16,128]{2,1,0:T(8,128)(2,1)S(1)}, bf16[132,16,128]{2,1,0:T(8,128)(2,1)S(1)}, u32[]{:S(2)}, u32[]{:S(2)}) collective-permute-start(bf16[132,16,128]{2,1,0:T(8,128)(2,1)S(1)} %collective-permute-done.5.refs_10_), channel_id=1, source_target_pairs={{0,1},{1,0},{2,3},{3,2},{4,5},{5,4},{6,7},{7,6},{8,9},{9,8},{10,11... | collective-permute-start | bytes 1622024 | tf_op jit(solution)/shard_map/ppermute | solution.py:752
  22.1 6.8 %collective-permute-start.7 = (bf16[42,16,128]{2,1,0:T(8,128)(2,1)S(1)}, bf16[42,16,128]{2,1,0:T(8,128)(2,1)S(1)}, u32[]{:S(2)}, u32[]{:S(2)}) collective-permute-start(bf16[42,16,128]{2,1,0:T(8,128)(2,1)S(1)} %collective-permute-done.4.refs_1_), channel_id=1, source_target_pairs={{0,2},{2,0},{1,3},{3,1},{4,6},{6,4},{5,7},{7,5},{8,10},{10,8},{9,1... | collective-permute-start | bytes 516104 | tf_op jit(solution)/shard_map/ppermute | solution.py:756
  28.8 9.3 %copy-start.2 = (s32[16,128]{1,0:T(8,128)S(1)}, s32[16,128]{1,0:T(8,128)}, u32[]{:S(2)}) copy-start(s32[16,128]{1,0:T(8,128)} %source_ref.1) | copy-start | bytes 24580
  36.4 1.7 %collective-permute-start.8 = (f32[39,16,128]{2,1,0:T(8,128)S(1)}, f32[39,16,128]{2,1,0:T(8,128)S(1)}, u32[]{:S(2)}, u32[]{:S(2)}) collective-permute-start(f32[39,16,128]{2,1,0:T(8,128)S(1)} %get-tuple-element.67.send_ref), channel_id=1, source_target_pairs={{0,1},{1,0},{2,3},{3,2},{4,5},{5,4},{6,7},{7,6},{8,9},{9,8},{10,11... | collective-permute-start | bytes 958472 | tf_op jit(solution)/shard_map/ppermute | solution.py:752

commit v4 on v3

--- a/solution.py
+++ b/solution.py
@@ -11,7 +11,7 @@
 SMEM = pl.BlockSpec(memory_space=pltpu.SMEM)
 PAIRS = ((0, 1, 3), (0, 2, 4), (1, 2, 5))
 LAT_TILES = 132
-LON_TILES = 42
+LON_TILES = 21
 
 
 def iota(shape, axis):
@@ -195,34 +195,33 @@
 
     def emit(f, value):
         high, low = split(value)
-        out_ref[2 * f] = high
-        out_ref[2 * f + 1] = low
+        pair(f, high, low)
+
+    def pair(f, first, second):
+        tops, bottoms = halves(first), halves(second)
+        for h in range(2):
+            out_ref[h, f] = stack_rows(tops[h], bottoms[h]).astype(BF16)
 
     def tracer(t, _):
         emit(t, gather(lambda r, l, h: r[0][t, l], zero_32, slot))
         tr = [gather(lambda r, l, h: r[1][k, t, l], zero_16, slot_16) for k in range(3)]
         both = jnp.where(far > 0, lane_roll(tr[0], jnp.where(core == 0, 4, 124)), tr[1])
-        out_ref[24 + t] = tr[2]
-        out_ref[33 + t] = both
+        pair(12 + t, tr[2], both)
         return 0
 
-    lax.fori_loop(0, 9, tracer, 0)
+    for t in range(9):
+        tracer(t, 0)
     emit(9, gather(lambda r, l, h: r[2][1, l], zero_32, slot))
     emit(10, gather(lambda r, l, h: r[2][0, l], zero_32, slot))
     land = land_ref[...]
     emit(11, gather(lambda r, l, h: marked(r[3][l], land, l + 8 * h) if l == 0 else r[3][l], zero_32, slot))
 
 
-def zero_rows(ref, depth):
+def put_rows(ref, t, z, value):
     zero = jnp.zeros((8, 128), F32)
-
-    def clear(t, _):
-        for z in range(depth):
-            ref[t, z, 0:8, :] = zero
-            ref[t, z, 24:32, :] = zero
-        return 0
-
-    lax.fori_loop(0, 9, clear, 0)
+    ref[t, z, 0:8, :] = zero
+    ref[t, z, 8:24, :] = value
+    ref[t, z, 24:32, :] = zero
 
 
 def zero_ends(ref):
@@ -247,7 +246,7 @@
     return parts
 
 
-def mixed(scalars, b_s, d, deposit, c_out, z):
+def mixed(scalars, b_s, d, deposit, put, z):
     rate_ref, speed_ref, class_ref, prof_ref, coef_ref = scalars
     kind = class_ref[z]
     below, above = d(z - 1), d(z)
@@ -255,9 +254,7 @@
     base = jnp.where(z == 0, base - deposit, base)
     for t in range(9):
         speed = speed_ref[kind, t]
-        c_out[t, z, 8:24, :] = (
-            b_s[t, z + 1] * (base - speed) + b_s[t, z] * (below + speed) + b_s[t, z + 2] * above
-        )
+        put(t, z, b_s[t, z + 1] * (base - speed) + b_s[t, z] * (below + speed) + b_s[t, z + 2] * above)
 
 
 def moved(c_in, w_ref, a_to, z):
@@ -293,14 +290,13 @@
 
     def at(z, carry):
         for lag, stage in stages:
-            if not isinstance(z, int) or 0 <= z - lag < 16:
+            if 0 <= z - lag < 16:
                 carry = stage(z - lag, carry)
         return carry
 
     for z in range(depth):
         carry = at(z, carry)
-    carry = lax.fori_loop(depth, 16, at, carry)
-    for z in range(16, 16 + depth):
+    for z in range(depth, 16 + depth):
         carry = at(z, carry)
     return carry
 
@@ -312,10 +308,12 @@
     c_out, em_ref, traj_out, wind_out, mix_out = refs[14:19]
     b_s = refs[19]
     core = lax.axis_index("lev")
-    zero_rows(c_out, 16)
     zero_ends(b_s)
     deposit = 0.1 + 0.3 * land_ref[...].astype(F32)
     nothing = jnp.zeros((16, 128), F32)
+
+    def put(t, z, value):
+        c_out[t, z] = value
 
     def run(low, high):
         def level(r, z, l, sums):
@@ -333,7 +331,7 @@
                     return nothing
                 return mix_out[i]
 
-            mixed(scalars, b_s, d, deposit, c_out, z)
+            mixed(scalars, b_s, d, deposit, put, z)
 
         sums = no_sums()
         for z in range(3):
@@ -366,7 +364,7 @@
     scalars = refs[7:12]
     rate_ref, speed_ref, class_ref, prof_ref, coef_ref = scalars
     traj_out, c_first, c_next, n_out, e_out, d_out, land_out, w_s, em_ref = refs[12:21]
-    a_s, b_s, p_s = refs[21:]
+    a_s, b_s, p_s, q_s = refs[21:]
     core = lax.axis_index("lev")
     lat = lax.axis_index("lat")
     edge = jnp.where(core == 0, 120, 0)
@@ -376,8 +374,6 @@
     row = iota((16, 128), 0)
     zero = jnp.zeros((16, 128), F32)
     z_lane = jnp.bitwise_xor(iota((8, 128), 1) // 8, 8 * (1 - core))
-    zero_rows(c_first, 16)
-    zero_rows(c_next, 16)
     zero_ends(b_s)
     d_out[0] = zero
 
@@ -391,13 +387,16 @@
         return acc
 
     for f in range(9, 12):
-        p_s[f] = lon_ref[2 * f].astype(F32) + lon_ref[2 * f + 1].astype(F32)
+        for h in range(2):
+            p_s[f, 8 * h : 8 * h + 8, :] = sum(halves(lon_ref[h, f]))
+    for t in range(9):
+        q_s[t] = stack_rows(halves(lon_ref[0, 12 + t])[1], halves(lon_ref[1, 12 + t])[1]).astype(BF16)
     rate = [by_lane(lambda z: rate_ref[q, z]) for q in range(6)]
     speeds = [by_lane(lambda z: speed_ref[class_ref[z], t]) for t in range(9)]
     for rb in range(2):
         rows = slice(8 * rb, 8 * rb + 8)
-        adj = [(lon_ref[2 * t].astype(F32) + lon_ref[2 * t + 1].astype(F32))[rows] for t in range(9)]
-        done = coag(adj, [lon_ref[24 + t].astype(F32)[rows] for t in range(9)], rate)
+        adj = [sum(halves(lon_ref[rb, t])) for t in range(9)]
+        done = coag(adj, [halves(lon_ref[rb, 12 + t])[0] for t in range(9)], rate)
         mark = p_s[11, rows, :]
         land = ((mark < 0) & (z_lane == 0)).astype(F32)
         size = jnp.abs(mark)
@@ -418,9 +417,9 @@
         shift = shift_of(z)
         shift_0 = lax.rem(shift + jnp.where(core == 0, 4, 124), 128)
         for t in range(9):
-            c_first[t, z, 8:24, :] = jnp.where(halo, lane_roll(p_s[t], shift), c_own[t, z, 8:24, :])
-            traj_out[1, t, z] = jnp.where(halo_16, lane_roll(lon_ref[33 + t], shift), traj_own[1, t, z])
-            traj_out[0, t, z] = jnp.where(halo_16, lane_roll(lon_ref[33 + t], shift_0), traj_own[0, t, z])
+            put_rows(c_first, t, z, jnp.where(halo, lane_roll(p_s[t], shift), c_own[t, z]))
+            traj_out[1, t, z] = jnp.where(halo_16, lane_roll(q_s[t], shift), traj_own[1, t, z])
+            traj_out[0, t, z] = jnp.where(halo_16, lane_roll(q_s[t], shift_0), traj_own[0, t, z])
         north = jnp.where(halo, lane_roll(p_s[9], shift), wind_own[1, z])
         north = jnp.where((row == 15) & last_lat, 0.0, north)
         east = jnp.where(halo, lane_roll(p_s[10], shift), wind_own[0, z])
@@ -454,7 +453,7 @@
         return react(scalars, lambda t: traj_ref[k, t, z], lambda t, rows: a_s[t, z, rows, :], b_s, z, sums)
 
     def mix(z, sums):
-        mixed(scalars, b_s, d, deposit, c_out, z)
+        mixed(scalars, b_s, d, deposit, lambda t, i, value: put_rows(c_out, t, i, value), z)
         return sums
 
     return [(lag, move), (lag + 1, do_react), (lag + 3, mix)]
@@ -463,30 +462,24 @@
 def third_kernel(lat_count, *refs):
     traj_ref, d_ref, land_ref, w_ref, c_in, em_in = refs[0:6]
     scalars = refs[6:11]
-    c_next, out_ref, em_ref = refs[11:14]
-    a_s, b_s = refs[14:]
-    zero_rows(c_next, 16)
+    c_next, em_ref = refs[11:13]
+    a_s, b_s = refs[13:]
     zero_ends(b_s)
     steps = stages(scalars, c_in, w_ref, a_s, b_s, traj_ref, 0, lambda z: d_ref[z + 1], land_ref[...], c_next, 0)
-
-    def last(z, sums):
-        moved(c_next, w_ref, out_ref, z)
-        return sums
-
-    sums = pipeline(steps + [(4, last)], no_sums())
-    sums = total(lat_count, 2, sums)
+    sums = total(lat_count, 2, pipeline(steps, no_sums()))
     for m in range(3):
         em_ref[m] = em_in[m] + sums[m]
 
 
 def edge_kernel(lat_count, *refs):
     edges = 1 if lat_count == 2 else 2
-    traj_ref, c_first, c_next, n_ref, e_ref, d_ref, land_ref, c_last, out_ref, em_ref = refs[0:10]
+    traj_ref, c_first, c_next, n_ref, e_ref, d_ref, land_ref, c_last, w_ref, em_ref = refs[0:10]
     lat_refs = refs[10 : 10 + 2 * edges]
     corner_refs = refs[10 + 2 * edges : 10 + 3 * edges]
     rate_ref, speed_ref, class_ref, prof_ref, coef_ref = refs[10 + 3 * edges : 15 + 3 * edges]
     keep_ref, send_ref = refs[15 + 3 * edges : 17 + 3 * edges]
     b_0, b_1, c_0, c_1, c_2, t_s, n_s, e_s, d_s, l_s, a_s, em_s, fin_s = refs[17 + 3 * edges :]
+    far = 2 - edges
     core = lax.axis_index("lev")
     lat = lax.axis_index("lat")
     edge = jnp.where(core == 0, 120, 0)
@@ -510,12 +503,10 @@
             return lax.rem(edge + 128 - 8 * jnp.bitwise_xor(z, 8 * flip), 128)
 
         def corner(tile, z):
-            return lane_roll(halves(corner_ref[tile])[0 if upper else 1], shift_of(z))
+            return halves(lane_roll(corner_ref[tile], shift_of(z)))
 
         def corner_sum(f, z):
-            high = halves(corner_ref[2 * f])[0 if upper else 1]
-            low = halves(corner_ref[2 * f + 1])[0 if upper else 1]
-            return lane_roll(high + low, shift_of(z))
+            return sum(corner(f, z))
 
         land_c = corner_sum(11, 0)
         land_l = jnp.where(core == 0, sum(halves(lat_refs[2 * e][124])), sum(halves(lat_refs[2 * e + 1][124])))
@@ -523,17 +514,8 @@
         l_s[pl.ds(own_at, 8), :] = land_ref[pl.ds(own_row, 8), :]
         d_s[0] = jnp.zeros((16, 128), F32)
 
-        def pads(t, _):
-            for b in (b_0, b_1):
-                b[t, 0] = zero
-                b[t, 17] = zero
-            for c in c_bufs:
-                for z in range(16):
-                    c[t, z, 0:8, :] = zero
-                    c[t, z, 24:32, :] = zero
-            return 0
-
-        lax.fori_loop(0, 9, pads, 0)
+        zero_ends(b_0)
+        zero_ends(b_1)
 
         for s in range(2):
             msg = lat_refs[2 * e + s]
@@ -548,7 +530,7 @@
                         v0, v1 = halves(msg[t * 8 + l])
                         v2 = halves(msg[72 + t * 4 + pair])[i]
                         adj.append(jnp.where(halo, corner_sum(t, z), jnp.where(keep, v0 + v1, 0.0)))
-                        tr2, tr1 = corner(24 + t, z), corner(33 + t, z)
+                        tr2, tr1 = corner(12 + t, z)
                         tr0 = lane_roll(tr1, jnp.where(core == 0, 4, 124))
                         state.append(jnp.where(halo, tr2, v2))
                         if upper:
@@ -569,8 +551,10 @@
                     for q in range(3):
                         high, low = halves(msg[108 + q * 8 + l])
                         winds.append(jnp.where(halo, corner_sum(9 + q, z), high + low))
-                    n_s[z, 0:8, :] = zero
-                    n_s[z, 24:32, :] = zero
+                    if upper:
+                        n_s[z, 0:8, :] = n_ref[z, 8:16, :]
+                    else:
+                        n_s[z, 24:32, :] = n_ref[z, 16:24, :]
                     n_s[z, pl.ds(8 + halo_at, 8), :] = winds[0]
                     n_s[z, pl.ds(8 + own_at, 8), :] = n_ref[z, pl.ds(8 + own_row, 8), :]
                     e_s[z, pl.ds(halo_at, 8), :] = winds[1]
@@ -596,7 +580,12 @@
             for t in range(9):
                 speed = speed_ref[kind, t]
                 value = b[t, z + 1] * (base - speed) + b[t, z] * (below + speed) + b[t, z + 2] * above
-                c[t, z, 8 + own_at : 16 + own_at, :] = c_ref[t, z, 8 + own_row : 16 + own_row, :]
+                if step < 2:
+                    c[t, z, 8 + own_at : 16 + own_at, :] = c_ref[t, z, 8 + own_row : 16 + own_row, :]
+                elif upper:
+                    c[t, z, 0:16, :] = c_ref[t, z, 8:24, :]
+                else:
+                    c[t, z, 16:32, :] = c_ref[t, z, 8:24, :]
                 c[t, z, 8 + at : 16 + at, :] = value
 
         def move(step, z, sums):
@@ -645,21 +634,26 @@
             return lambda z, sums: move(step, z, sums)
 
         count(0, pipeline([(0, mixing(0)), (1, moving(0)), (3, mixing(1))], none))
-        count(1, pipeline([(0, moving(1)), (2, mixing(2)), (3, moving(2))], none))
+
+        def far_moving(z, sums):
+            near = 0 if upper else 8
+            w = [w_ref[i, z, near : near + 8, :] for i in range(9)]
+            for t in range(9):
+                rows = [c_last[t, z, near + 6 + i : near + 14 + i, :] for i in range(5)]
+                fin_s[1, t, z] = transported(rows, w)
+            return sums
+
+        later = [(0, moving(1)), (2, mixing(2)), (3, moving(2))] + [(3, far_moving)] * far
+        count(1, pipeline(later, none))
         for m in range(3):
             a_s[e, m] = em_s[m, own_at : own_at + 8, :]
 
     def finish(has_upper, has_lower, e_upper, e_lower):
         mine = (iota((16, 128), 1) < 64) == (core == 0)
-        row8 = sub
 
         def rows_of(t, z):
-            low = out_ref[t, z, 0:8, :]
-            high = out_ref[t, z, 8:16, :]
-            if has_upper:
-                high = jnp.where(row8 >= 2, fin_s[e_upper, t, z], high)
-            if has_lower:
-                low = jnp.where(row8 < 6, fin_s[e_lower, t, z], low)
+            low = fin_s[e_lower, t, z]
+            high = fin_s[e_upper, t, z]
             return stack_rows(low, high)
 
         def tracer(t, _):
@@ -684,11 +678,11 @@
 
         def south():
             run(True, 0)
-            finish(True, False, 0, 0)
+            finish(True, False, 0, 1)
 
         def north():
             run(False, 0)
-            finish(False, True, 0, 0)
+            finish(False, True, 1, 0)
 
         pl.when(lat == 0)(south)
         pl.when(lat == 1)(north)
@@ -698,33 +692,39 @@
         finish(True, True, 0, 1)
 
 
-def join_kernel(keep_ref, send_ref, recv_ref, source_ref, out_ref, em_ref):
+def join_kernel(keep_ref, send_ref, recv_ref, source_ref, out_ref, em_ref, part, em_part, sems):
     core = lax.axis_index("lev")
     mine = (iota((16, 128), 1) < 64) == (core == 0)
-
-    def tracer(t, _):
+    source = source_ref[...].astype(F32)
+    for m in range(3):
+        em_part[m] = jnp.where(mine, send_ref[36 + m], recv_ref[36 + m]) * source
+    copies = [pltpu.make_async_copy(em_part, em_ref, sems.at[9])]
+    copies[0].start()
+    for t in range(9):
         for l in range(4):
             got = recv_ref[t * 4 + l]
-            out_ref[t, l] = jnp.where(mine, keep_ref[t, l], got)
-            out_ref[t, l + 4] = jnp.where(mine, keep_ref[t, l + 4], lane_roll(got, 64))
-        return 0
-
-    lax.fori_loop(0, 9, tracer, 0)
-    source = source_ref[...].astype(F32)
-    for m in range(3):
-        em_ref[m] = jnp.where(mine, send_ref[36 + m], recv_ref[36 + m]) * source
+            part[t, l] = jnp.where(mine, keep_ref[t, l], got)
+            part[t, l + 4] = jnp.where(mine, keep_ref[t, l + 4], lane_roll(got, 64))
+        copies.append(pltpu.make_async_copy(part.at[t], out_ref.at[t], sems.at[t]))
+        copies[-1].start()
+    for copy in copies:
+        copy.wait()
+
+
+def corner_kernel(lon_ref, out_ref):
+    out_ref[...] = lon_ref[1 - lax.axis_index("lat")]
 
 
 def shape(*dims, dtype=F32):
     return jax.ShapeDtypeStruct(dims, dtype)
 
 
-def call(kernel, outs, scratch, *args, specs=None, mib=32):
+def call(kernel, outs, scratch, *args, specs=None, out_specs=None, mib=32):
     return pl.pallas_call(
         kernel,
         out_shape=outs,
         in_specs=specs or [VMEM] * len(args),
-        out_specs=[VMEM] * len(outs),
+        out_specs=out_specs or [VMEM] * len(outs),
         scratch_shapes=scratch,
         compiler_params=pltpu.CompilerParams(vmem_limit_bytes=mib * 1024 * 1024),
     )(*args)
@@ -765,7 +765,8 @@
         return run
 
     given = (adjoint_in, trajectory, courant, mixing)
-    other = tuple(over_lev(value) for value in given)
+    wind_other, mix_other = over_lev(courant), over_lev(mixing)
+    other = (over_lev(adjoint_in), over_lev(trajectory), wind_other, mix_other)
     *own, land = call(
         load_kernel,
         [jax.ShapeDtypeStruct(v.shape, v.dtype) for v in given + (land_mask,)],
@@ -775,9 +776,8 @@
         mib=16,
     )
     (lon_out,) = call(
-        bind(lon_pack_kernel), [shape(LON_TILES, 16, 128, dtype=BF16)], [], *own, *other, land, mib=16
-    )
-    *own, lon_out = lax.optimization_barrier((*own, lon_out))
+        bind(lon_pack_kernel), [shape(2, LON_TILES, 16, 128, dtype=BF16)], [], *own, *other, land, mib=16
+    )
     lat_out = call(
         bind(lat_pack_kernel), [shape(LAT_TILES, 16, 128, dtype=BF16)] * edges, [], *own, land, mib=16
     )
@@ -794,7 +794,7 @@
     c_own, emis, traj_own, wind_own, mix_own = call(
         bind(first_kernel),
         [
-            padded,
+            shape(9, 16, 16, 128),
             shape(3, 16, 128),
             shape(2, 9, 16, 16, 128, dtype=BF16),
             shape(2, 16, 16, 128),
@@ -808,7 +808,11 @@
         specs=[VMEM] * 9 + [SMEM] * 5,
     )
     lon_in, c_own = lax.optimization_barrier((lon_in, c_own))
-    corner_in = lat_moves([lon_in])
+    if edges == 1:
+        corner_out = call(corner_kernel, [shape(LON_TILES, 16, 128, dtype=BF16)], [], lon_in, mib=16)
+    else:
+        corner_out = [lon_in[1], lon_in[0]]
+    corner_in = lat_moves(corner_out)
     traj_all, c_first, c_next, north, east, mix, land_all, weight, emis = call(
         bind(second_kernel),
         [
@@ -822,7 +826,7 @@
             shape(9, 16, 16, 128),
             shape(3, 16, 128),
         ],
-        [state, between, pltpu.VMEM((12, 16, 128), F32)],
+        [state, between, pltpu.VMEM((12, 16, 128), F32), pltpu.VMEM((9, 16, 128), BF16)],
         land,
         lon_in,
         c_own,
@@ -834,9 +838,9 @@
         specs=[VMEM] * 7 + [SMEM] * 5,
     )
     c_next, *lat_in = lax.optimization_barrier((c_next, *lat_in))
-    c_last, final, emis = call(
+    c_last, emis = call(
         bind(third_kernel),
-        [padded, shape(9, 16, 16, 128), shape(3, 16, 128)],
+        [padded, shape(3, 16, 128)],
         [state, between],
         traj_all,
         mix,
@@ -847,7 +851,7 @@
         *scalars,
         specs=[VMEM] * 6 + [SMEM] * 5,
     )
-    inner = (traj_all, c_first, c_next, north, east, mix, land_all, c_last, final, emis)
+    inner = (traj_all, c_first, c_next, north, east, mix, land_all, c_last, weight, emis)
     lat_all = []
     for value in lat_in:
         lat_all += [value, over_lev(value)]
@@ -867,7 +871,7 @@
             pltpu.VMEM((16, 128), F32),
             pltpu.VMEM((edges, 3, 8, 128), F32),
             pltpu.VMEM((3, 24, 128), F32),
-            pltpu.VMEM((edges, 9, 16, 8, 128), F32),
+            pltpu.VMEM((2, 9, 16, 8, 128), F32),
         ],
         *inner,
         *lat_all,
@@ -878,7 +882,14 @@
     )
     recv = over_lev(send)
     out, emis = call(
-        join_kernel, [shape(9, 8, 16, 128), shape(3, 16, 128)], [], keep, send, recv, source_mask
+        join_kernel,
+        [shape(9, 8, 16, 128), shape(3, 16, 128)],
+        [pltpu.VMEM((9, 8, 16, 128), F32), pltpu.VMEM((3, 16, 128), F32), pltpu.SemaphoreType.DMA((10,))],
+        keep,
+        send,
+        recv,
+        source_mask,
+        out_specs=[pl.BlockSpec(memory_space=pltpu.HBM)] * 2,
     )
     return (out, emis)
 

time: 39.8 us -> 34.3 us (0.86)
  Pallas kernels: 23.2 us -> 18.5 us
  starting transfers between devices: 9.86 us -> 9.38 us
  waiting for transfers between devices: 5.73 us -> 5.29 us
    pallas_call x8 -> x9, Pallas kernels: 23.2 us -> 18.5 us  [call(): pl.pallas_call(kernel, out_shape=outs, in_specs=specs or [VMEM] * len(arg...]
    ppermute x2, starting transfers between devices: 4.67 us -> 3.58 us  [lat_moves(): return [lax.ppermute(messages[0], 'lat', swap)]]
    ppermute x1, starting transfers between devices: 4.02 us -> 4.55 us  [shards(): lon_in = lax.ppermute(lon_out, ('lon', 'lev'), lon_pairs)]
    ppermute x6, waiting for transfers between devices: 3.01 us -> 2.54 us  [over_lev(): return lax.ppermute(value, 'lev', swap)]
  transfers between devices with their start and end apart: 9 -> 9, of which waited for: 5 -> 4; matrix products, arithmetic and copies ran while one was open for 0% -> 0% of each run, Pallas kernels for 31% -> 33%
where the time goes in v4:
time: 34.3 us; the launch traced here: 34.2 us
  Pallas kernels  18.5 us (54%)
  starting transfers between devices  9.38 us (27%)
  waiting for transfers between devices  5.29 us (15%)
  between operations  0.95 us (3%)
    pallas_call x9, Pallas kernels, call(): pl.pallas_call(kernel, out_shape=outs, in_specs=specs or [VMEM] * len(arg...  18.5 us
    ppermute x1, starting transfers between devices, shards(): lon_in = lax.ppermute(lon_out, ('lon', 'lev'), lon_pairs)  4.55 us
    ppermute x2, starting transfers between devices, lat_moves(): return [lax.ppermute(messages[0], 'lat', swap)]  3.58 us
    ppermute x6, waiting for transfers between devices, over_lev(): return lax.ppermute(value, 'lev', swap)  2.54 us
    ppermute x2, waiting for transfers between devices, lat_moves(): return [lax.ppermute(messages[0], 'lat', swap)]  1.5 us
    ppermute x6, starting transfers between devices, over_lev(): return lax.ppermute(value, 'lev', swap)  1.25 us
    ppermute x1, waiting for transfers between devices, shards(): lon_in = lax.ppermute(lon_out, ('lon', 'lev'), lon_pairs)  1.25 us
  transfers between devices with their start and end apart: 9, of which 4 were waited for; matrix products, arithmetic and copies ran while one was open for 0% of the time, Pallas kernels for 33%

profile of v4, /device:TPU:0, one launch (start us, length us, event | category | flops | bytes accessed | tf_op | source)
XLA Modules:
  0.0 34.2 jit_solution(15277300980706295256)
XLA Ops:
  0.6 0.5 %collective-permute-start.1 = (bf16[3,9,8,16,128]{4,3,2,1,0:T(8,128)(2,1)}, bf16[3,9,8,16,128]{4,3,2,1,0:T(8,128)(2,1)S(1)}, u32[]{:S(2)}, u32[]{:S(2)}) collective-permute-start(bf16[3,9,8,16,128]{4,3,2,1,0:T(8,128)(2,1)} %refs_1_.1), channel_id=1, source_target_pairs={{0,1},{1,0},{2,3},{3,2},{4,5},{5,4},{6,7},{7,6},{8,9},{9,8},{10,11... | collective-permute-start | bytes 2654216 | tf_op jit(solution)/shard_map/ppermute | solution.py:752
  1.1 0.1 collective-permute-start
  1.2 1.4 %shard_map.122 = (f32[9,8,16,128]{3,2,1,0:T(8,128)S(1)}, bf16[3,9,8,16,128]{4,3,2,1,0:T(8,128)(2,1)S(1)}, f32[2,8,16,128]{3,2,1,0:T(8,128)S(1)}, f32[8,16,128]{2,1,0:T(8,128)S(1)}, s32[16,128]{1,0:T(8,128)S(1)}) custom-call(f32[9,8,16,128]{3,2,1,0:T(8,128)} %refs_0_.1, bf16[3,9,8,16,128]{4,3,2,1,0:T(8,128)(2,1)} %refs_1_.1, f32[2,8,16,128]{3,2,1,0:T(8,128)} %refs_2_.1, ...), custom_call_target="tpu_custom_call" | custom-call | tf_op jit(solution)/shard_map/pallas_call | solution.py:723
  2.6 0.0 copy-start.6
  2.6 0.0 copy-start.7
  2.7 0.3 shard_map.126
  2.9 0.0 copy-start
  3.0 0.0 copy-start.1
  3.0 0.0 copy-start.3
  3.0 0.0 copy-start.4
  3.0 0.0 copy-start.5
  3.0 3.0 %collective-permute-start.5 = (bf16[132,16,128]{2,1,0:T(8,128)(2,1)S(1)}, bf16[132,16,128]{2,1,0:T(8,128)(2,1)S(1)}, u32[]{:S(2)}, u32[]{:S(2)}) collective-permute-start(bf16[132,16,128]{2,1,0:T(8,128)(2,1)S(1)} %shard_map.126), channel_id=1, source_target_pairs={{0,2},{2,0},{1,3},{3,1},{4,6},{6,4},{5,7},{7,5},{8,10},{10,8},{9,1... | collective-permute-start | bytes 1622024 | tf_op jit(solution)/shard_map/ppermute | solution.py:756
  6.0 0.0 copy-done.6
  6.0 0.0 collective-permute-start.2
  6.0 0.0 copy-done.7
  6.0 0.5 %collective-permute-start.3 = (f32[8,16,128]{2,1,0:T(8,128)S(1)}, f32[8,16,128]{2,1,0:T(8,128)S(1)}, u32[]{:S(2)}, u32[]{:S(2)}) collective-permute-start(f32[8,16,128]{2,1,0:T(8,128)S(1)} %copy-done.7), channel_id=1, source_target_pairs={{0,1},{1,0},{2,3},{3,2},{4,5},{5,4},{6,7},{7,6},{8,9},{9,8},{10,11... | collective-permute-start | bytes 196616 | tf_op jit(solution)/shard_map/ppermute | solution.py:752
  6.5 0.9 %collective-permute-done.3.refs_7_ = f32[8,16,128]{2,1,0:T(8,128)S(1)} collective-permute-done((f32[8,16,128]{2,1,0:T(8,128)S(1)}, f32[8,16,128]{2,1,0:T(8,128)S(1)}, u32[]{:S(2)}, u32[]{:S(2)}) %collective-permute-start.3) | collective-permute-done | bytes 65568 | tf_op jit(solution)/shard_map/ppermute | solution.py:752
  7.4 0.0 collective-permute-done.2.refs_6_
  7.4 0.0 collective-permute-done.refs_4_
  7.4 0.0 collective-permute-done.1.refs_5_
  7.4 1.3 %shard_map.123 = bf16[2,21,16,128]{3,2,1,0:T(8,128)(2,1)S(1)} custom-call(f32[9,8,16,128]{3,2,1,0:T(8,128)S(1)} %get-tuple-element.30.refs_0_, bf16[3,9,8,16,128]{4,3,2,1,0:T(8,128)(2,1)S(1)} %get-tuple-element.31.refs_1_, f32[2,8,16,128]{3,2,1,0:T(8,128)S(1)} %get-tuple-element.32.refs_2_, f32[8,16,128]{2,1,0:T(8,128)S(1)} %get-tuple-element.33.refs_3_, ...), custom_call_target="tpu_custom_call" | custom-call | tf_op jit(solution)/shard_map/pallas_call | solution.py:723
  8.7 4.6 %collective-permute-start.4 = (bf16[2,21,16,128]{3,2,1,0:T(8,128)(2,1)S(1)}, bf16[2,21,16,128]{3,2,1,0:T(8,128)(2,1)S(1)}, u32[]{:S(2)}, u32[]{:S(2)}) collective-permute-start(bf16[2,21,16,128]{3,2,1,0:T(8,128)(2,1)S(1)} %shard_map.123), channel_id=1, source_target_pairs={{1,4},{0,29},{5,8},{4,1},{9,12},{8,5},{13,16},{12,9},{17,20},{16,1... | collective-permute-start | bytes 516104 | tf_op jit(solution)/shard_map/ppermute | solution.py:789
  13.3 0.0 copy-done
  13.3 0.0 copy-done.1
  13.3 0.0 copy-done.3
  13.3 0.0 copy-done.4
  13.3 0.0 copy-done.5
  13.3 1.8 %shard_map.124 = (f32[9,16,16,128]{3,2,1,0:T(8,128)S(1)}, f32[3,16,128]{2,1,0:T(8,128)S(1)}, bf16[2,9,16,16,128]{4,3,2,1,0:T(8,128)(2,1)S(1)}, f32[2,16,16,128]{3,2,1,0:T(8,128)S(1)}, f32[16,16,128]{2,1,0:T(8,128)S(1)}) custom-call(f32[9,8,16,128]{3,2,1,0:T(8,128)S(1)} %get-tuple-element.30.refs_0_, ...), custom_call_target="tpu_custom_call" | custom-call | tf_op jit(solution)/shard_map/pallas_call | solution.py:723
  15.1 1.2 %collective-permute-done.4.refs_1_.lon_ref = bf16[2,21,16,128]{3,2,1,0:T(8,128)(2,1)S(1)} collective-permute-done((bf16[2,21,16,128]{3,2,1,0:T(8,128)(2,1)S(1)}, bf16[2,21,16,128]{3,2,1,0:T(8,128)(2,1)S(1)}, u32[]{:S(2)}, u32[]{:S(2)}) %collective-permute-start.4) | collective-permute-done | bytes 172064 | tf_op jit(solution)/shard_map/ppermute | solution.py:789
  16.4 3.8 %shard_map.125 = (bf16[2,9,16,16,128]{4,3,2,1,0:T(8,128)(2,1)S(1)}, f32[9,16,32,128]{3,2,1,0:T(8,128)S(1)}, f32[9,16,32,128]{3,2,1,0:T(8,128)S(1)}, f32[16,32,12...) custom-call(s32[16,128]{1,0:T(8,128)S(1)} %get-tuple-element.29.refs, ...), custom_call_target="tpu_custom_call" | custom-call | tf_op jit(solution)/shard_map/pallas_call | solution.py:723
  20.1 0.0 collective-permute-done.5.refs_10_
  20.1 0.1 collective-permute-start.6
  20.2 0.6 %collective-permute-start.7 = (bf16[21,16,128]{2,1,0:T(8,128)(2,1)S(1)}, bf16[21,16,128]{2,1,0:T(8,128)(2,1)S(1)}, u32[]{:S(2)}, u32[]{:S(2)}) collective-permute-start(bf16[21,16,128]{2,1,0:T(8,128)(2,1)S(1)} %shard_map.128), channel_id=1, source_target_pairs={{0,2},{2,0},{1,3},{3,1},{4,6},{6,4},{5,7},{7,5},{8,10},{10,8},{9,1... | collective-permute-start | bytes 258056 | tf_op jit(solution)/shard_map/ppermute | solution.py:756
  20.8 2.8 %shard_map.127 = (f32[9,16,32,128]{3,2,1,0:T(8,128)S(1)}, f32[3,16,128]{2,1,0:T(8,128)S(1)}) custom-call(bf16[2,9,16,16,128]{4,3,2,1,0:T(8,128)(2,1)S(1)} %get-tuple-element.41.refs_0_, f32[17,16,128]{2,1,0:T(8,128)S(1)} %get-tuple-element.47.refs_1_.refs_5_, f32[16,128]{1,0:T(8,128)S(1)} %get-tuple-element.48.refs_2_.refs_6_, ...), custom_call_target="tpu_custom_call" | custom-call | tf_op jit(solution)/shard_map/pallas_call | solution.py:723
  23.7 1.5 %collective-permute-done.7.refs_12_ = bf16[21,16,128]{2,1,0:T(8,128)(2,1)S(1)} collective-permute-done((bf16[21,16,128]{2,1,0:T(8,128)(2,1)S(1)}, bf16[21,16,128]{2,1,0:T(8,128)(2,1)S(1)}, u32[]{:S(2)}, u32[]{:S(2)}) %collective-permute-start.7) | collective-permute-done | bytes 86048 | tf_op jit(solution)/shard_map/ppermute | solution.py:756
  25.2 0.0 collective-permute-done.6.refs_11_
  25.2 0.0 copy-start.2
  25.2 6.2 %shard_map.129 = (f32[9,8,16,128]{3,2,1,0:T(8,128)S(1)}, f32[39,16,128]{2,1,0:T(8,128)S(1)}) custom-call(bf16[2,9,16,16,128]{4,3,2,1,0:T(8,128)(2,1)S(1)} %get-tuple-element.41.refs_0_, f32[9,16,32,128]{3,2,1,0:T(8,128)S(1)} %get-tuple-element.42.refs_1_, f32[9,16,32,128]{3,2,1,0:T(8,128)S(1)} %get-tuple-element.44.refs_4_.refs_2_, ...), custom_call_target="tpu_custom_call" | custom-call | tf_op jit(solution)/shard_map/pallas_call | solution.py:723
  31.3 0.1 collective-permute-start.8
  31.4 1.6 %collective-permute-done.8.recv_ref = f32[39,16,128]{2,1,0:T(8,128)S(1)} collective-permute-done((f32[39,16,128]{2,1,0:T(8,128)S(1)}, f32[39,16,128]{2,1,0:T(8,128)S(1)}, u32[]{:S(2)}, u32[]{:S(2)}) %collective-permute-start.8) | collective-permute-done | bytes 319520 | tf_op jit(solution)/shard_map/ppermute | solution.py:752
  33.0 0.0 copy-done.2
  33.0 1.0 %shard_map.130 = (f32[9,8,16,128]{3,2,1,0:T(8,128)}, f32[3,16,128]{2,1,0:T(8,128)}) custom-call(f32[9,8,16,128]{3,2,1,0:T(8,128)S(1)} %get-tuple-element.54.keep_ref, f32[39,16,128]{2,1,0:T(8,128)S(1)} %get-tuple-element.55.send_ref, f32[39,16,128]{2,1,0:T(8,128)S(1)} %collective-permute-done.8.recv_ref, s32[16,128]{1,0:T(8,128)S(1)} %copy-done.2), custom_call_target="tpu_custom_call" | custom-call | tf_op jit(solution)/shard_map/pallas_call | solution.py:723
  (1 shorter events, 0.0 us)
Async XLA Ops:
  0.6 6.8 %collective-permute-start.1 = (bf16[3,9,8,16,128]{4,3,2,1,0:T(8,128)(2,1)}, bf16[3,9,8,16,128]{4,3,2,1,0:T(8,128)(2,1)S(1)}, u32[]{:S(2)}, u32[]{:S(2)}) collective-permute-start(bf16[3,9,8,16,128]{4,3,2,1,0:T(8,128)(2,1)} %refs_1_.1), channel_id=1, source_target_pairs={{0,1},{1,0},{2,3},{3,2},{4,5},{5,4},{6,7},{7,6},{8,9},{9,8},{10,11... | collective-permute-start | bytes 2654216 | tf_op jit(solution)/shard_map/ppermute | solution.py:752
  1.1 6.3 %collective-permute-start = (f32[9,8,16,128]{3,2,1,0:T(8,128)}, f32[9,8,16,128]{3,2,1,0:T(8,128)S(1)}, u32[]{:S(2)}, u32[]{:S(2)}) collective-permute-start(f32[9,8,16,128]{3,2,1,0:T(8,128)} %refs_0_.1), channel_id=1, source_target_pairs={{0,1},{1,0},{2,3},{3,2},{4,5},{5,4},{6,7},{7,6},{8,9},{9,8},{10,11... | collective-permute-start | bytes 1769480 | tf_op jit(solution)/shard_map/ppermute | solution.py:752
  2.6 3.4 %copy-start.6 = (f32[2,8,16,128]{3,2,1,0:T(8,128)S(1)}, f32[2,8,16,128]{3,2,1,0:T(8,128)}, u32[]{:S(2)}) copy-start(f32[2,8,16,128]{3,2,1,0:T(8,128)} %refs_2_.1) | copy-start | bytes 393220
  2.6 3.3 %copy-start.7 = (f32[8,16,128]{2,1,0:T(8,128)S(1)}, f32[8,16,128]{2,1,0:T(8,128)}, u32[]{:S(2)}) copy-start(f32[8,16,128]{2,1,0:T(8,128)} %refs_3_.1) | copy-start | bytes 196612
  2.9 10.3 %copy-start = (f32[6,16]{1,0:T(8,128)S(1)}, f32[6,16]{1,0:T(8,128)}, u32[]{:S(2)}) copy-start(f32[6,16]{1,0:T(8,128)} %refs_13_.3) | copy-start | bytes 1156
  3.0 10.3 %copy-start.1 = (f32[8,9]{1,0:T(8,128)S(1)}, f32[8,9]{1,0:T(8,128)}, u32[]{:S(2)}) copy-start(f32[8,9]{1,0:T(8,128)} %refs_14_.1) | copy-start | bytes 868
  3.0 10.3 %copy-start.3 = (s32[16]{0:T(128)S(1)}, s32[16]{0:T(128)}, u32[]{:S(2)}) copy-start(s32[16]{0:T(128)} %refs_15_.1) | copy-start | bytes 196
  3.0 10.3 %copy-start.4 = (f32[16]{0:T(128)S(1)}, f32[16]{0:T(128)}, u32[]{:S(2)}) copy-start(f32[16]{0:T(128)} %refs_16_.1) | copy-start | bytes 196
  3.0 10.3 %copy-start.5 = (f32[9]{0:T(128)S(1)}, f32[9]{0:T(128)}, u32[]{:S(2)}) copy-start(f32[9]{0:T(128)} %refs_17_.1) | copy-start | bytes 112
  3.0 17.1 %collective-permute-start.5 = (bf16[132,16,128]{2,1,0:T(8,128)(2,1)S(1)}, bf16[132,16,128]{2,1,0:T(8,128)(2,1)S(1)}, u32[]{:S(2)}, u32[]{:S(2)}) collective-permute-start(bf16[132,16,128]{2,1,0:T(8,128)(2,1)S(1)} %shard_map.126), channel_id=1, source_target_pairs={{0,2},{2,0},{1,3},{3,1},{4,6},{6,4},{5,7},{7,5},{8,10},{10,8},{9,1... | collective-permute-start | bytes 1622024 | tf_op jit(solution)/shard_map/ppermute | solution.py:756
  6.0 1.4 %collective-permute-start.2 = (f32[2,8,16,128]{3,2,1,0:T(8,128)S(1)}, f32[2,8,16,128]{3,2,1,0:T(8,128)S(1)}, u32[]{:S(2)}, u32[]{:S(2)}) collective-permute-start(f32[2,8,16,128]{3,2,1,0:T(8,128)S(1)} %copy-done.6), channel_id=1, source_target_pairs={{0,1},{1,0},{2,3},{3,2},{4,5},{5,4},{6,7},{7,6},{8,9},{9,8},{10,11... | collective-permute-start | bytes 393224 | tf_op jit(solution)/shard_map/ppermute | solution.py:752
  6.0 1.4 %collective-permute-start.3 = (f32[8,16,128]{2,1,0:T(8,128)S(1)}, f32[8,16,128]{2,1,0:T(8,128)S(1)}, u32[]{:S(2)}, u32[]{:S(2)}) collective-permute-start(f32[8,16,128]{2,1,0:T(8,128)S(1)} %copy-done.7), channel_id=1, source_target_pairs={{0,1},{1,0},{2,3},{3,2},{4,5},{5,4},{6,7},{7,6},{8,9},{9,8},{10,11... | collective-permute-start | bytes 196616 | tf_op jit(solution)/shard_map/ppermute | solution.py:752
  8.7 7.6 %collective-permute-start.4 = (bf16[2,21,16,128]{3,2,1,0:T(8,128)(2,1)S(1)}, bf16[2,21,16,128]{3,2,1,0:T(8,128)(2,1)S(1)}, u32[]{:S(2)}, u32[]{:S(2)}) collective-permute-start(bf16[2,21,16,128]{3,2,1,0:T(8,128)(2,1)S(1)} %shard_map.123), channel_id=1, source_target_pairs={{1,4},{0,29},{5,8},{4,1},{9,12},{8,5},{13,16},{12,9},{17,20},{16,1... | collective-permute-start | bytes 516104 | tf_op jit(solution)/shard_map/ppermute | solution.py:789
  20.1 5.0 %collective-permute-start.6 = (bf16[132,16,128]{2,1,0:T(8,128)(2,1)S(1)}, bf16[132,16,128]{2,1,0:T(8,128)(2,1)S(1)}, u32[]{:S(2)}, u32[]{:S(2)}) collective-permute-start(bf16[132,16,128]{2,1,0:T(8,128)(2,1)S(1)} %collective-permute-done.5.refs_10_), channel_id=1, source_target_pairs={{0,1},{1,0},{2,3},{3,2},{4,5},{5,4},{6,7},{7,6},{8,9},{9,8},{10,11... | collective-permute-start | bytes 1622024 | tf_op jit(solution)/shard_map/ppermute | solution.py:752
  20.2 4.9 %collective-permute-start.7 = (bf16[21,16,128]{2,1,0:T(8,128)(2,1)S(1)}, bf16[21,16,128]{2,1,0:T(8,128)(2,1)S(1)}, u32[]{:S(2)}, u32[]{:S(2)}) collective-permute-start(bf16[21,16,128]{2,1,0:T(8,128)(2,1)S(1)} %shard_map.128), channel_id=1, source_target_pairs={{0,2},{2,0},{1,3},{3,1},{4,6},{6,4},{5,7},{7,5},{8,10},{10,8},{9,1... | collective-permute-start | bytes 258056 | tf_op jit(solution)/shard_map/ppermute | solution.py:756
  25.2 7.8 %copy-start.2 = (s32[16,128]{1,0:T(8,128)S(1)}, s32[16,128]{1,0:T(8,128)}, u32[]{:S(2)}) copy-start(s32[16,128]{1,0:T(8,128)} %source_ref.1) | copy-start | bytes 24580
  31.3 1.7 %collective-permute-start.8 = (f32[39,16,128]{2,1,0:T(8,128)S(1)}, f32[39,16,128]{2,1,0:T(8,128)S(1)}, u32[]{:S(2)}, u32[]{:S(2)}) collective-permute-start(f32[39,16,128]{2,1,0:T(8,128)S(1)} %get-tuple-element.55.send_ref), channel_id=1, source_target_pairs={{0,1},{1,0},{2,3},{3,2},{4,5},{5,4},{6,7},{7,6},{8,9},{9,8},{10,11... | collective-permute-start | bytes 958472 | tf_op jit(solution)/shard_map/ppermute | solution.py:752

commit v5 on v4

--- a/solution.py
+++ b/solution.py
@@ -10,7 +10,7 @@
 VMEM = pl.BlockSpec(memory_space=pltpu.VMEM)
 SMEM = pl.BlockSpec(memory_space=pltpu.SMEM)
 PAIRS = ((0, 1, 3), (0, 2, 4), (1, 2, 5))
-LAT_TILES = 132
+LAT_TILES = 124
 LON_TILES = 21
 
 
@@ -105,20 +105,32 @@
     return jnp.where(core == 0, (lane >= 120).astype(jnp.int32), (lane < 8).astype(jnp.int32)) > 0
 
 
-def load_kernel(*refs):
-    given, kept, sems = refs[0:5], refs[5:10], refs[10]
-    copies = [pltpu.make_async_copy(given[i], kept[i], sems.at[i]) for i in range(5)]
+def halo_lanes_16(core):
+    middle = jnp.where(core == 0, 123.5, 3.5).astype(F32)
+    return jnp.abs(iota((16, 128), 1).astype(F32) - middle).astype(BF16) <= jnp.full((16, 128), 3.5, BF16)
+
+
+def load_kernel(adj_ref, traj_ref, wind_ref, mix_ref, land_ref, field_out, traj_out, land_out, sems):
+    pairs = [(adj_ref.at[pl.ds(3 * i, 3)], field_out.at[pl.ds(3 * i, 3)]) for i in range(3)]
+    pairs += [(wind_ref, field_out.at[pl.ds(9, 2)]), (mix_ref, field_out.at[11]), (land_ref, land_out)]
+    pairs += [(traj_ref.at[k], traj_out.at[k]) for k in range(3)]
+    copies = [pltpu.make_async_copy(source, target, sems.at[i]) for i, (source, target) in enumerate(pairs)]
     for copy in copies:
         copy.start()
     for copy in copies:
         copy.wait()
 
 
+def parts_of(field_ref, traj_ref):
+    return field_ref.at[pl.ds(0, 9)], traj_ref, field_ref.at[pl.ds(9, 2)], field_ref.at[11]
+
+
 def marked(mix, land, z):
     return jnp.where((land * (z == 0).astype(jnp.int32)) > 0, -mix, mix)
 
 
-def lat_pack_kernel(lat_count, adj_ref, traj_ref, wind_ref, mix_ref, land_ref, *outs):
+def lat_pack_kernel(lat_count, field_ref, traj_ref, land_ref, *outs):
+    adj_ref, traj_ref, wind_ref, mix_ref = parts_of(field_ref, traj_ref)
     core = lax.axis_index("lev")
     lat = lax.axis_index("lat")
 
@@ -152,13 +164,21 @@
         lax.fori_loop(0, 9, tracer, 0)
 
         def level(l, _):
-            for q in range(3):
-                if q == 2:
-                    value = marked(mix_ref[l, base : base + 8, :], land_ref[base : base + 8, :], l + 8 * core)
-                else:
-                    value = wind_ref[1 - q, l, base : base + 8, :]
+            rows = slice(base, base + 8)
+            z = l + 8 * core
+            north, east = wind_ref[1, l, rows, :], wind_ref[0, l, rows, :]
+            parts = []
+            for value in (north, marked(mix_ref[l, rows, :], land_ref[rows, :], z), east):
                 high = value.astype(BF16).astype(F32)
-                out_ref[108 + q * 8 + l] = stack_rows(high, value - high).astype(BF16)
+                parts += [high, value - high]
+            one, two = (2, 4) if high_rows else (6, 4)
+            north_h, north_l, mix_h, mix_l, east_h, east_l = parts
+            out_ref[108 + l] = stack_rows(
+                jnp.where(keep, north_h, rolled(east_h, one)), jnp.where(keep, north_l, rolled(east_h, two))
+            ).astype(BF16)
+            out_ref[116 + l] = stack_rows(
+                jnp.where(keep, mix_h, rolled(east_l, one)), jnp.where(keep, mix_l, rolled(east_l, two))
+            ).astype(BF16)
             return 0
 
         lax.fori_loop(0, 8, level, 0)
@@ -171,50 +191,75 @@
         fill(outs[1], False)
 
 
-def lon_pack_kernel(lat_count, *refs):
-    own, other = refs[0:4], refs[4:8]
-    land_ref = refs[8]
-    out_ref = refs[9]
+def gather_edges(core, s, blocks, land, f_kind, t_kind, f_done, t_done):
+    edge = jnp.where(core == 0, 0, 120)
+    slot = iota((16, 128), 1) // 8
+    slot_16 = slot.astype(BF16)
+    adj_ref, traj_ref, wind_ref, mix_ref = blocks
+
+    def gather(read, acc, at):
+        for l in range(8):
+            g = 8 * s + l
+            shift = lax.rem(8 * g - edge + 128, 128)
+            acc = jnp.where(at == g, lane_roll(read(l), shift), acc)
+        return acc
+
+    for t in range(9):
+        f_done(t, gather(lambda l: adj_ref[t, l], f_kind(t), slot))
+        t_done(t, [gather(lambda l: traj_ref[k, t, l], t_kind(9 * k + t), slot_16) for k in range(3)])
+    bottom = jnp.bitwise_xor(s, core)
+    f_done(9, gather(lambda l: wind_ref[1, l], f_kind(9), slot))
+    f_done(10, gather(lambda l: wind_ref[0, l], f_kind(10), slot))
+    f_done(11, gather(lambda l: marked(mix_ref[l], land, bottom) if l == 0 else mix_ref[l], f_kind(11), slot))
+
+
+def lon_start_kernel(field_ref, traj_ref, land_ref, f_ref, t_ref):
+    def f_done(f, value):
+        f_ref[f] = value
+
+    def t_done(t, values):
+        for k in range(3):
+            t_ref[9 * k + t] = values[k]
+
+    gather_edges(
+        lax.axis_index("lev"),
+        0,
+        parts_of(field_ref, traj_ref),
+        land_ref[...],
+        lambda f: jnp.zeros((16, 128), F32),
+        lambda f: jnp.zeros((16, 128), BF16),
+        f_done,
+        t_done,
+    )
+
+
+def lon_pack_kernel(field_ref, traj_ref, land_ref, f_ref, t_ref, out_ref):
     core = lax.axis_index("lev")
-    edge = jnp.where(core == 0, 0, 120)
-    lane = iota((16, 128), 1)
-    slot = lane // 8
-    slot_16 = slot.astype(BF16)
-    far = (jnp.bitwise_xor((lane // 4) % 2, core)).astype(F32).astype(BF16)
-    zero_32 = jnp.zeros((16, 128), F32)
-    zero_16 = jnp.zeros((16, 128), BF16)
-
-    def gather(read, zero, at):
-        acc = zero
-        for s in range(2):
-            for l in range(8):
-                g = 8 * s + l
-                shift = lax.rem(8 * g - edge + 128, 128)
-                acc = jnp.where(at == g, lane_roll(read((own, other)[s], l, jnp.bitwise_xor(s, core)), shift), acc)
-        return acc
-
-    def emit(f, value):
-        high, low = split(value)
-        pair(f, high, low)
+    far = (jnp.bitwise_xor((iota((16, 128), 1) // 4) % 2, core)).astype(F32).astype(BF16)
 
     def pair(f, first, second):
         tops, bottoms = halves(first), halves(second)
         for h in range(2):
             out_ref[h, f] = stack_rows(tops[h], bottoms[h]).astype(BF16)
 
-    def tracer(t, _):
-        emit(t, gather(lambda r, l, h: r[0][t, l], zero_32, slot))
-        tr = [gather(lambda r, l, h: r[1][k, t, l], zero_16, slot_16) for k in range(3)]
+    def f_done(f, value):
+        high, low = split(value)
+        pair(f, high, low)
+
+    def t_done(t, tr):
         both = jnp.where(far > 0, lane_roll(tr[0], jnp.where(core == 0, 4, 124)), tr[1])
         pair(12 + t, tr[2], both)
-        return 0
-
-    for t in range(9):
-        tracer(t, 0)
-    emit(9, gather(lambda r, l, h: r[2][1, l], zero_32, slot))
-    emit(10, gather(lambda r, l, h: r[2][0, l], zero_32, slot))
-    land = land_ref[...]
-    emit(11, gather(lambda r, l, h: marked(r[3][l], land, l + 8 * h) if l == 0 else r[3][l], zero_32, slot))
+
+    gather_edges(
+        core,
+        1,
+        parts_of(field_ref, traj_ref),
+        land_ref[...],
+        lambda f: f_ref[f],
+        lambda f: t_ref[f],
+        f_done,
+        t_done,
+    )
 
 
 def put_rows(ref, t, z, value):
@@ -302,11 +347,11 @@
 
 
 def first_kernel(lat_count, *refs):
-    own, other = refs[0:4], refs[4:8]
-    land_ref = refs[8]
-    scalars = refs[9:14]
-    c_out, em_ref, traj_out, wind_out, mix_out = refs[14:19]
-    b_s = refs[19]
+    own, other = parts_of(*refs[0:2]), parts_of(*refs[2:4])
+    land_ref = refs[4]
+    scalars = refs[5:10]
+    c_out, em_ref, traj_out, wind_out, mix_out = refs[10:15]
+    b_s = refs[15]
     core = lax.axis_index("lev")
     zero_ends(b_s)
     deposit = 0.1 + 0.3 * land_ref[...].astype(F32)
@@ -363,14 +408,13 @@
     land_ref, lon_ref, c_own, em_in, traj_own, wind_own, mix_own = refs[0:7]
     scalars = refs[7:12]
     rate_ref, speed_ref, class_ref, prof_ref, coef_ref = scalars
-    traj_out, c_first, c_next, n_out, e_out, d_out, land_out, w_s, em_ref = refs[12:21]
-    a_s, b_s, p_s, q_s = refs[21:]
+    traj_out, c_first, c_next, n_out, e_out, d_out, land_out, w_s, em_ref, q_s = refs[12:22]
+    a_s, b_s, p_s = refs[22:]
     core = lax.axis_index("lev")
     lat = lax.axis_index("lat")
     edge = jnp.where(core == 0, 120, 0)
     halo = halo_lanes(core, 16)
-    edge_f = jnp.where(core == 0, 123.5, 3.5).astype(F32)
-    halo_16 = jnp.abs(iota((16, 128), 1).astype(F32) - edge_f).astype(BF16) <= jnp.full((16, 128), 3.5, BF16)
+    halo_16 = halo_lanes_16(core)
     row = iota((16, 128), 0)
     zero = jnp.zeros((16, 128), F32)
     z_lane = jnp.bitwise_xor(iota((8, 128), 1) // 8, 8 * (1 - core))
@@ -415,11 +459,9 @@
 
     def assemble(z, sums):
         shift = shift_of(z)
-        shift_0 = lax.rem(shift + jnp.where(core == 0, 4, 124), 128)
         for t in range(9):
             put_rows(c_first, t, z, jnp.where(halo, lane_roll(p_s[t], shift), c_own[t, z]))
-            traj_out[1, t, z] = jnp.where(halo_16, lane_roll(q_s[t], shift), traj_own[1, t, z])
-            traj_out[0, t, z] = jnp.where(halo_16, lane_roll(q_s[t], shift_0), traj_own[0, t, z])
+            traj_out[t, z] = jnp.where(halo_16, lane_roll(q_s[t], shift), traj_own[1, t, z])
         north = jnp.where(halo, lane_roll(p_s[9], shift), wind_own[1, z])
         north = jnp.where((row == 15) & last_lat, 0.0, north)
         east = jnp.where(halo, lane_roll(p_s[10], shift), wind_own[0, z])
@@ -437,20 +479,20 @@
             w_s[j, z] = value
         return sums
 
-    steps = stages(scalars, c_first, w_s, a_s, b_s, traj_out, 1, lambda z: d_out[z + 1], land_out[...], c_next, 2)
+    steps = stages(scalars, c_first, w_s, a_s, b_s, traj_out, lambda z: d_out[z + 1], land_out[...], c_next, 2)
     sums = pipeline([(0, assemble), (1, weigh)] + steps, no_sums())
     sums = total(lat_count, 1, sums)
     for m in range(3):
         em_ref[m] = em_in[m] + sums[m]
 
 
-def stages(scalars, c_in, w_ref, a_s, b_s, traj_ref, k, d, deposit, c_out, lag):
+def stages(scalars, c_in, w_ref, a_s, b_s, traj_ref, d, deposit, c_out, lag):
     def move(z, sums):
         moved(c_in, w_ref, a_s, z)
         return sums
 
     def do_react(z, sums):
-        return react(scalars, lambda t: traj_ref[k, t, z], lambda t, rows: a_s[t, z, rows, :], b_s, z, sums)
+        return react(scalars, lambda t: traj_ref[t, z], lambda t, rows: a_s[t, z, rows, :], b_s, z, sums)
 
     def mix(z, sums):
         mixed(scalars, b_s, d, deposit, lambda t, i, value: put_rows(c_out, t, i, value), z)
@@ -460,25 +502,35 @@
 
 
 def third_kernel(lat_count, *refs):
-    traj_ref, d_ref, land_ref, w_ref, c_in, em_in = refs[0:6]
-    scalars = refs[6:11]
-    c_next, em_ref = refs[11:13]
-    a_s, b_s = refs[13:]
+    traj_own, q_ref, d_ref, land_ref, w_ref, c_in, em_in = refs[0:7]
+    scalars = refs[7:12]
+    c_next, em_ref, traj_out = refs[12:15]
+    a_s, b_s = refs[15:]
+    core = lax.axis_index("lev")
+    edge = 124
+    halo_16 = halo_lanes_16(core)
     zero_ends(b_s)
-    steps = stages(scalars, c_in, w_ref, a_s, b_s, traj_ref, 0, lambda z: d_ref[z + 1], land_ref[...], c_next, 0)
-    sums = total(lat_count, 2, pipeline(steps, no_sums()))
+
+    def complete(z, sums):
+        shift = lax.rem(edge + 128 - 8 * jnp.bitwise_xor(z, 8 * (1 - core)), 128)
+        for t in range(9):
+            traj_out[t, z] = jnp.where(halo_16, lane_roll(q_ref[t], shift), traj_own[0, t, z])
+        return sums
+
+    steps = stages(scalars, c_in, w_ref, a_s, b_s, traj_out, lambda z: d_ref[z + 1], land_ref[...], c_next, 0)
+    sums = total(lat_count, 2, pipeline(steps + [(0, complete)], no_sums()))
     for m in range(3):
         em_ref[m] = em_in[m] + sums[m]
 
 
 def edge_kernel(lat_count, *refs):
     edges = 1 if lat_count == 2 else 2
-    traj_ref, c_first, c_next, n_ref, e_ref, d_ref, land_ref, c_last, w_ref, em_ref = refs[0:10]
-    lat_refs = refs[10 : 10 + 2 * edges]
-    corner_refs = refs[10 + 2 * edges : 10 + 3 * edges]
-    rate_ref, speed_ref, class_ref, prof_ref, coef_ref = refs[10 + 3 * edges : 15 + 3 * edges]
-    keep_ref, send_ref = refs[15 + 3 * edges : 17 + 3 * edges]
-    b_0, b_1, c_0, c_1, c_2, t_s, n_s, e_s, d_s, l_s, a_s, em_s, fin_s = refs[17 + 3 * edges :]
+    traj_1, c_first, c_next, n_ref, e_ref, d_ref, land_ref, c_last, w_ref, traj_0, em_ref = refs[0:11]
+    lat_refs = refs[11 : 11 + 2 * edges]
+    corner_refs = refs[11 + 2 * edges : 11 + 3 * edges]
+    rate_ref, speed_ref, class_ref, prof_ref, coef_ref = refs[11 + 3 * edges : 16 + 3 * edges]
+    keep_ref, send_ref = refs[16 + 3 * edges : 18 + 3 * edges]
+    b_0, b_1, c_0, c_1, c_2, t_s, n_s, e_s, d_s, l_s, a_s, em_s, fin_s = refs[18 + 3 * edges :]
     far = 2 - edges
     core = lax.axis_index("lev")
     lat = lax.axis_index("lat")
@@ -488,14 +540,10 @@
     sub = iota((8, 128), 0)
     zero = jnp.zeros((8, 128), F32)
 
-    def rolled(value, shift):
-        return pltpu.roll(value, shift, 0)
-
     def run(upper, e):
         own_at, halo_at = (0, 8) if upper else (8, 0)
         own_row = 8 if upper else 0
         corner_ref = corner_refs[e]
-        keep = (sub < 6) if upper else (sub >= 2)
         starts = (6, 4, 0) if upper else (2, 4, 8)
         b_bufs, c_bufs = (b_0, b_1, b_0), (c_0, c_1, c_2)
 
@@ -509,7 +557,7 @@
             return sum(corner(f, z))
 
         land_c = corner_sum(11, 0)
-        land_l = jnp.where(core == 0, sum(halves(lat_refs[2 * e][124])), sum(halves(lat_refs[2 * e + 1][124])))
+        land_l = jnp.where(core == 0, sum(halves(lat_refs[2 * e][116])), sum(halves(lat_refs[2 * e + 1][116])))
         l_s[pl.ds(halo_at, 8), :] = 0.1 + 0.3 * (jnp.where(halo, land_c, land_l) < 0).astype(F32)
         l_s[pl.ds(own_at, 8), :] = land_ref[pl.ds(own_row, 8), :]
         d_s[0] = jnp.zeros((16, 128), F32)
@@ -529,37 +577,36 @@
                     for t in range(9):
                         v0, v1 = halves(msg[t * 8 + l])
                         v2 = halves(msg[72 + t * 4 + pair])[i]
-                        adj.append(jnp.where(halo, corner_sum(t, z), jnp.where(keep, v0 + v1, 0.0)))
+                        adj.append(jnp.where(halo, corner_sum(t, z), v0 + v1))
                         tr2, tr1 = corner(12 + t, z)
                         tr0 = lane_roll(tr1, jnp.where(core == 0, 4, 124))
                         state.append(jnp.where(halo, tr2, v2))
-                        if upper:
-                            own1 = jnp.where(sub < 2, rolled(v1, 2), rolled(v2, 4))
-                            own0 = rolled(v0, 2)
-                        else:
-                            own1 = jnp.where(sub >= 6, rolled(v1, 6), rolled(v2, 4))
-                            own0 = rolled(v0, 6)
-                        t_s[1, t, z, pl.ds(halo_at, 8), :] = jnp.where(halo, tr1, own1)
-                        t_s[0, t, z, pl.ds(halo_at, 8), :] = jnp.where(halo, tr0, own0)
-                        near = 1 if upper else 0
-                        t_s[1, t, z, pl.ds(own_at, 8), :] = halves(traj_ref[1, t, z])[near]
-                        t_s[0, t, z, pl.ds(own_at, 8), :] = halves(traj_ref[0, t, z])[near]
+                        near, rest = (1, -1) if upper else (0, 1)
+                        t_s[1, t, z, pl.ds(halo_at + 4 * rest, 8), :] = v2
+                        t_s[1, t, z, pl.ds(halo_at + 6 * rest, 8), :] = v1
+                        t_s[0, t, z, pl.ds(halo_at + 6 * rest, 8), :] = v0
+                        t_s[1, t, z, pl.ds(own_at, 8), :] = halves(traj_1[t, z])[near]
+                        t_s[0, t, z, pl.ds(own_at, 8), :] = halves(traj_0[t, z])[near]
+                        pltpu.store(t_s.at[1, t, z, pl.ds(halo_at, 8), :], tr1, mask=halo)
+                        pltpu.store(t_s.at[0, t, z, pl.ds(halo_at, 8), :], tr0, mask=halo)
                     done = coag(adj, state, rate)
                     for t in range(9):
                         b_0[t, z + 1] = done[t]
-                    winds = []
-                    for q in range(3):
-                        high, low = halves(msg[108 + q * 8 + l])
-                        winds.append(jnp.where(halo, corner_sum(9 + q, z), high + low))
+                    north_h, north_l = halves(msg[108 + l])
+                    mix_h, mix_l = halves(msg[116 + l])
+                    north = jnp.where(halo, corner_sum(9, z), north_h + north_l)
+                    mixing = jnp.where(halo, corner_sum(11, z), mix_h + mix_l)
+                    e_s[z, pl.ds(halo_at + 4 * rest, 8), :] = north_l + mix_l
+                    e_s[z, pl.ds(halo_at + 6 * rest, 8), :] = north_h + mix_h
                     if upper:
                         n_s[z, 0:8, :] = n_ref[z, 8:16, :]
                     else:
                         n_s[z, 24:32, :] = n_ref[z, 16:24, :]
-                    n_s[z, pl.ds(8 + halo_at, 8), :] = winds[0]
+                    n_s[z, pl.ds(8 + halo_at, 8), :] = north
                     n_s[z, pl.ds(8 + own_at, 8), :] = n_ref[z, pl.ds(8 + own_row, 8), :]
-                    e_s[z, pl.ds(halo_at, 8), :] = winds[1]
                     e_s[z, pl.ds(own_at, 8), :] = e_ref[z, pl.ds(own_row, 8), :]
-                    d_s[z + 1, pl.ds(halo_at, 8), :] = jnp.where(z == 15, 0.0, jnp.abs(winds[2]))
+                    pltpu.store(e_s.at[z, pl.ds(halo_at, 8), :], corner_sum(10, z), mask=halo)
+                    d_s[z + 1, pl.ds(halo_at, 8), :] = jnp.where(z == 15, 0.0, jnp.abs(mixing))
                     d_s[z + 1, pl.ds(own_at, 8), :] = d_ref[z + 1, pl.ds(own_row, 8), :]
                 return 0
 
@@ -764,19 +811,26 @@
 
         return run
 
-    given = (adjoint_in, trajectory, courant, mixing)
-    wind_other, mix_other = over_lev(courant), over_lev(mixing)
-    other = (over_lev(adjoint_in), over_lev(trajectory), wind_other, mix_other)
-    *own, land = call(
+    given = (adjoint_in, trajectory, courant, mixing, land_mask)
+    field, traj, land = call(
         load_kernel,
-        [jax.ShapeDtypeStruct(v.shape, v.dtype) for v in given + (land_mask,)],
-        [pltpu.SemaphoreType.DMA((5,))],
-        *[pltpu.with_memory_space_constraint(v, pltpu.HBM) for v in given + (land_mask,)],
+        [
+            shape(12, *adjoint_in.shape[1:]),
+            jax.ShapeDtypeStruct(trajectory.shape, trajectory.dtype),
+            jax.ShapeDtypeStruct(land_mask.shape, land_mask.dtype),
+        ],
+        [pltpu.SemaphoreType.DMA((9,))],
+        *[pltpu.with_memory_space_constraint(v, pltpu.HBM) for v in given],
         specs=[pl.BlockSpec(memory_space=pltpu.HBM)] * 5,
         mib=16,
     )
+    own = (field, traj)
+    other = (over_lev(field), over_lev(trajectory))
+    half = call(
+        lon_start_kernel, [shape(12, 16, 128), shape(27, 16, 128, dtype=BF16)], [], *own, land, mib=16
+    )
     (lon_out,) = call(
-        bind(lon_pack_kernel), [shape(2, LON_TILES, 16, 128, dtype=BF16)], [], *own, *other, land, mib=16
+        lon_pack_kernel, [shape(2, LON_TILES, 16, 128, dtype=BF16)], [], *other, land, *half, mib=16
     )
     lat_out = call(
         bind(lat_pack_kernel), [shape(LAT_TILES, 16, 128, dtype=BF16)] * edges, [], *own, land, mib=16
@@ -805,7 +859,7 @@
         *other,
         land,
         *scalars,
-        specs=[VMEM] * 9 + [SMEM] * 5,
+        specs=[VMEM] * 5 + [SMEM] * 5,
     )
     lon_in, c_own = lax.optimization_barrier((lon_in, c_own))
     if edges == 1:
@@ -813,10 +867,10 @@
     else:
         corner_out = [lon_in[1], lon_in[0]]
     corner_in = lat_moves(corner_out)
-    traj_all, c_first, c_next, north, east, mix, land_all, weight, emis = call(
+    traj_1, c_first, c_next, north, east, mix, land_all, weight, emis, strip = call(
         bind(second_kernel),
         [
-            shape(2, 9, 16, 16, 128, dtype=BF16),
+            shape(9, 16, 16, 128, dtype=BF16),
             padded,
             padded,
             shape(16, 32, 128),
@@ -825,8 +879,9 @@
             shape(16, 128),
             shape(9, 16, 16, 128),
             shape(3, 16, 128),
+            shape(9, 16, 128, dtype=BF16),
         ],
-        [state, between, pltpu.VMEM((12, 16, 128), F32), pltpu.VMEM((9, 16, 128), BF16)],
+        [state, between, pltpu.VMEM((12, 16, 128), F32)],
         land,
         lon_in,
         c_own,
@@ -838,20 +893,21 @@
         specs=[VMEM] * 7 + [SMEM] * 5,
     )
     c_next, *lat_in = lax.optimization_barrier((c_next, *lat_in))
-    c_last, emis = call(
+    c_last, emis, traj_0 = call(
         bind(third_kernel),
-        [padded, shape(3, 16, 128)],
+        [padded, shape(3, 16, 128), shape(9, 16, 16, 128, dtype=BF16)],
         [state, between],
-        traj_all,
+        traj_own,
+        strip,
         mix,
         land_all,
         weight,
         c_next,
         emis,
         *scalars,
-        specs=[VMEM] * 6 + [SMEM] * 5,
-    )
-    inner = (traj_all, c_first, c_next, north, east, mix, land_all, c_last, weight, emis)
+        specs=[VMEM] * 7 + [SMEM] * 5,
+    )
+    inner = (traj_1, c_first, c_next, north, east, mix, land_all, c_last, weight, traj_0, emis)
     lat_all = []
     for value in lat_in:
         lat_all += [value, over_lev(value)]
@@ -877,7 +933,7 @@
         *lat_all,
         *corner_in,
         *scalars,
-        specs=[VMEM] * (10 + 3 * edges) + [SMEM] * 5,
+        specs=[VMEM] * (11 + 3 * edges) + [SMEM] * 5,
         mib=40,
     )
     recv = over_lev(send)

time: 34.3 us -> 33 us (0.962)
  waiting for transfers between devices: 5.29 us -> 4.14 us
    ppermute x6 -> x4, waiting for transfers between devices: 2.54 us -> 1.61 us  [over_lev(): return lax.ppermute(value, 'lev', swap)]
    ppermute x2, waiting for transfers between devices: 1.5 us -> 0.86 us  [lat_moves(): return [lax.ppermute(messages[0], 'lat', swap)]]
    ppermute x2, starting transfers between devices: 3.58 us -> 4.16 us  [lat_moves(): return [lax.ppermute(messages[0], 'lat', swap)]]
    ppermute x6 -> x4, starting transfers between devices: 1.25 us -> 0.78 us  [over_lev(): return lax.ppermute(value, 'lev', swap)]
    ppermute x1, starting transfers between devices: 4.55 us -> 4.11 us  [shards(): lon_in = lax.ppermute(lon_out, ('lon', 'lev'), lon_pairs)]
    ppermute x1, waiting for transfers between devices: 1.25 us -> 1.66 us  [shards(): lon_in = lax.ppermute(lon_out, ('lon', 'lev'), lon_pairs)]
    pallas_call x9 -> x10, Pallas kernels: 18.5 us -> 18.7 us  [call(): pl.pallas_call(kernel, out_shape=outs, in_specs=specs or [VMEM] * len(arg...]
  transfers between devices with their start and end apart: 9 -> 7, of which waited for: 4 -> 3; matrix products, arithmetic and copies ran while one was open for 0% -> 0% of each run, Pallas kernels for 33% -> 35%
where the time goes in v5:
time: 33 us; the launch traced here: 32.9 us
  Pallas kernels  18.7 us (57%)
  starting transfers between devices  9.05 us (27%)
  waiting for transfers between devices  4.14 us (13%)
  between operations  0.95 us (3%)
    pallas_call x10, Pallas kernels, call(): pl.pallas_call(kernel, out_shape=outs, in_specs=specs or [VMEM] * len(arg...  18.7 us
    ppermute x2, starting transfers between devices, lat_moves(): return [lax.ppermute(messages[0], 'lat', swap)]  4.16 us
    ppermute x1, starting transfers between devices, shards(): lon_in = lax.ppermute(lon_out, ('lon', 'lev'), lon_pairs)  4.11 us
    ppermute x1, waiting for transfers between devices, shards(): lon_in = lax.ppermute(lon_out, ('lon', 'lev'), lon_pairs)  1.66 us
    ppermute x4, waiting for transfers between devices, over_lev(): return lax.ppermute(value, 'lev', swap)  1.61 us
    ppermute x2, waiting for transfers between devices, lat_moves(): return [lax.ppermute(messages[0], 'lat', swap)]  0.86 us
    ppermute x4, starting transfers between devices, over_lev(): return lax.ppermute(value, 'lev', swap)  0.78 us
  transfers between devices with their start and end apart: 7, of which 3 were waited for; matrix products, arithmetic and copies ran while one was open for 0% of the time, Pallas kernels for 35%

profile of v5, /device:TPU:0, one launch (start us, length us, event | category | flops | bytes accessed | tf_op | source)
XLA Modules:
  0.0 32.9 jit_solution(8855211985135708327)
XLA Ops:
  0.6 0.5 %collective-permute-start.1 = (bf16[3,9,8,16,128]{4,3,2,1,0:T(8,128)(2,1)}, bf16[3,9,8,16,128]{4,3,2,1,0:T(8,128)(2,1)S(1)}, u32[]{:S(2)}, u32[]{:S(2)}) collective-permute-start(bf16[3,9,8,16,128]{4,3,2,1,0:T(8,128)(2,1)} %traj_ref.1), channel_id=1, source_target_pairs={{0,1},{1,0},{2,3},{3,2},{4,5},{5,4},{6,7},{7,6},{8,9},{9,8},{10,11... | collective-permute-start | bytes 2654216 | tf_op jit(solution)/shard_map/ppermute | solution.py:799
  1.1 1.6 %shard_map.122 = (f32[12,8,16,128]{3,2,1,0:T(8,128)S(1)}, bf16[3,9,8,16,128]{4,3,2,1,0:T(8,128)(2,1)S(1)}, s32[16,128]{1,0:T(8,128)S(1)}) custom-call(f32[9,8,16,128]{3,2,1,0:T(8,128)} %adj_ref.1, bf16[3,9,8,16,128]{4,3,2,1,0:T(8,128)(2,1)} %traj_ref.1, f32[2,8,16,128]{3,2,1,0:T(8,128)} %wind_ref.1, f32[8,16,128]{2,1,0:T(8,128)} %mix_ref.1, s32[16,128]{1,0:T(8,128)} %land_ref.1), custom_call_target="tpu_custom_call" | custom-call | tf_op jit(solution)/shard_map/pallas_call | solution.py:770
  2.7 0.1 collective-permute-start
  2.9 0.3 shard_map.127
  3.1 0.0 copy-start
  3.1 0.0 copy-start.1
  3.2 0.0 copy-start.3
  3.2 0.0 copy-start.4
  3.2 0.0 copy-start.5
  3.2 3.0 %collective-permute-start.3 = (bf16[124,16,128]{2,1,0:T(8,128)(2,1)S(1)}, bf16[124,16,128]{2,1,0:T(8,128)(2,1)S(1)}, u32[]{:S(2)}, u32[]{:S(2)}) collective-permute-start(bf16[124,16,128]{2,1,0:T(8,128)(2,1)S(1)} %shard_map.127), channel_id=1, source_target_pairs={{0,2},{2,0},{1,3},{3,1},{4,6},{6,4},{5,7},{7,5},{8,10},{10,8},{9,1... | collective-permute-start | bytes 1523720 | tf_op jit(solution)/shard_map/ppermute | solution.py:803
  6.2 0.5 %shard_map.123 = (f32[12,16,128]{2,1,0:T(8,128)S(1)}, bf16[27,16,128]{2,1,0:T(8,128)(2,1)S(1)}) custom-call(f32[12,8,16,128]{3,2,1,0:T(8,128)S(1)} %get-tuple-element.32.field_ref.refs_0_, bf16[3,9,8,16,128]{4,3,2,1,0:T(8,128)(2,1)S(1)} %get-tuple-element.33.traj_ref.refs_1_, s32[16,128]{1,0:T(8,128)S(1)} %get-tuple-element.31.land_ref.refs_4_.refs_0_.refs_2_), custom_call_target="tpu_custom_call" | custom-call | tf_op jit(solution)/shard_map/pallas_call | solution.py:770
  6.7 0.0 collective-permute-done.field_ref.refs_2_
  6.7 0.0 collective-permute-done.1.traj_ref.refs_3_
  6.7 0.9 %shard_map.124 = bf16[2,21,16,128]{3,2,1,0:T(8,128)(2,1)S(1)} custom-call(f32[12,8,16,128]{3,2,1,0:T(8,128)S(1)} %collective-permute-done.field_ref.refs_2_, bf16[3,9,8,16,128]{4,3,2,1,0:T(8,128)(2,1)S(1)} %collective-permute-done.1.traj_ref.refs_3_, s32[16,128]{1,0:T(8,128)S(1)} %get-tuple-element.31.land_ref.refs_4_.refs_0_.refs_2_, ...), custom_call_target="tpu_custom_call" | custom-call | tf_op jit(solution)/shard_map/pallas_call | solution.py:770
  7.6 4.1 %collective-permute-start.2 = (bf16[2,21,16,128]{3,2,1,0:T(8,128)(2,1)S(1)}, bf16[2,21,16,128]{3,2,1,0:T(8,128)(2,1)S(1)}, u32[]{:S(2)}, u32[]{:S(2)}) collective-permute-start(bf16[2,21,16,128]{3,2,1,0:T(8,128)(2,1)S(1)} %shard_map.124), channel_id=1, source_target_pairs={{1,4},{0,29},{5,8},{4,1},{9,12},{8,5},{13,16},{12,9},{17,20},{16,1... | collective-permute-start | bytes 516104 | tf_op jit(solution)/shard_map/ppermute | solution.py:843
  11.8 0.0 copy-done
  11.8 0.0 copy-done.1
  11.8 0.0 copy-done.3
  11.8 0.0 copy-done.4
  11.8 0.0 copy-done.5
  11.8 1.8 %shard_map.125 = (f32[9,16,16,128]{3,2,1,0:T(8,128)S(1)}, f32[3,16,128]{2,1,0:T(8,128)S(1)}, bf16[2,9,16,16,128]{4,3,2,1,0:T(8,128)(2,1)S(1)}, f32[2,16,16,128]{3,2,1,0:T(8,128)S(1)}, f32[16,16,128]{2,1,0:T(8,128)S(1)}) custom-call(f32[12,8,16,128]{3,2,1,0:T(8,128)S(1)} %get-tuple-element.32.field_ref.refs_0_, ...), custom_call_target="tpu_custom_call" | custom-call | tf_op jit(solution)/shard_map/pallas_call | solution.py:770
  13.6 1.7 %collective-permute-done.2.refs_1_.lon_ref = bf16[2,21,16,128]{3,2,1,0:T(8,128)(2,1)S(1)} collective-permute-done((bf16[2,21,16,128]{3,2,1,0:T(8,128)(2,1)S(1)}, bf16[2,21,16,128]{3,2,1,0:T(8,128)(2,1)S(1)}, u32[]{:S(2)}, u32[]{:S(2)}) %collective-permute-start.2) | collective-permute-done | bytes 172064 | tf_op jit(solution)/shard_map/ppermute | solution.py:843
  15.2 3.6 %shard_map.126 = (bf16[9,16,16,128]{3,2,1,0:T(8,128)(2,1)S(1)}, f32[9,16,32,128]{3,2,1,0:T(8,128)S(1)}, f32[9,16,32,128]{3,2,1,0:T(8,128)S(1)}, f32[16,32,128]{2...) custom-call(s32[16,128]{1,0:T(8,128)S(1)} %get-tuple-element.31.land, ...), custom_call_target="tpu_custom_call" | custom-call | tf_op jit(solution)/shard_map/pallas_call | solution.py:770
  18.9 0.0 collective-permute-done.3.refs_11_
  18.9 0.1 collective-permute-start.4
  19.0 1.2 %collective-permute-start.5 = (bf16[21,16,128]{2,1,0:T(8,128)(2,1)S(1)}, bf16[21,16,128]{2,1,0:T(8,128)(2,1)S(1)}, u32[]{:S(2)}, u32[]{:S(2)}) collective-permute-start(bf16[21,16,128]{2,1,0:T(8,128)(2,1)S(1)} %shard_map.129), channel_id=1, source_target_pairs={{0,2},{2,0},{1,3},{3,1},{4,6},{6,4},{5,7},{7,5},{8,10},{10,8},{9,1... | collective-permute-start | bytes 258056 | tf_op jit(solution)/shard_map/ppermute | solution.py:803
  20.1 2.9 %shard_map.128 = (f32[9,16,32,128]{3,2,1,0:T(8,128)S(1)}, f32[3,16,128]{2,1,0:T(8,128)S(1)}, bf16[9,16,16,128]{3,2,1,0:T(8,128)(2,1)S(1)}) custom-call(bf16[2,9,16,16,128]{4,3,2,1,0:T(8,128)(2,1)S(1)} %get-tuple-element.40.refs_4_.refs_0_, bf16[9,16,128]{2,1,0:T(8,128)(2,1)S(1)} %get-tuple-element.51.refs_1_, ...), custom_call_target="tpu_custom_call" | custom-call | tf_op jit(solution)/shard_map/pallas_call | solution.py:770
  23.0 0.9 %collective-permute-done.5.refs_13_ = bf16[21,16,128]{2,1,0:T(8,128)(2,1)S(1)} collective-permute-done((bf16[21,16,128]{2,1,0:T(8,128)(2,1)S(1)}, bf16[21,16,128]{2,1,0:T(8,128)(2,1)S(1)}, u32[]{:S(2)}, u32[]{:S(2)}) %collective-permute-start.5) | collective-permute-done | bytes 86048 | tf_op jit(solution)/shard_map/ppermute | solution.py:803
  23.9 0.0 collective-permute-done.4.refs_12_
  23.9 0.0 copy-start.2
  23.9 6.2 %shard_map.130 = (f32[9,8,16,128]{3,2,1,0:T(8,128)S(1)}, f32[39,16,128]{2,1,0:T(8,128)S(1)}) custom-call(bf16[9,16,16,128]{3,2,1,0:T(8,128)(2,1)S(1)} %get-tuple-element.43.refs_0_, f32[9,16,32,128]{3,2,1,0:T(8,128)S(1)} %get-tuple-element.44.refs_1_, f32[9,16,32,128]{3,2,1,0:T(8,128)S(1)} %get-tuple-element.46.refs_5_.refs_2_, ...), custom_call_target="tpu_custom_call" | custom-call | tf_op jit(solution)/shard_map/pallas_call | solution.py:770
  30.1 0.1 collective-permute-start.6
  30.2 1.6 %collective-permute-done.6.recv_ref = f32[39,16,128]{2,1,0:T(8,128)S(1)} collective-permute-done((f32[39,16,128]{2,1,0:T(8,128)S(1)}, f32[39,16,128]{2,1,0:T(8,128)S(1)}, u32[]{:S(2)}, u32[]{:S(2)}) %collective-permute-start.6) | collective-permute-done | bytes 319520 | tf_op jit(solution)/shard_map/ppermute | solution.py:799
  31.8 0.0 copy-done.2
  31.8 1.0 %shard_map.131 = (f32[9,8,16,128]{3,2,1,0:T(8,128)}, f32[3,16,128]{2,1,0:T(8,128)}) custom-call(f32[9,8,16,128]{3,2,1,0:T(8,128)S(1)} %get-tuple-element.58.keep_ref, f32[39,16,128]{2,1,0:T(8,128)S(1)} %get-tuple-element.59.send_ref, f32[39,16,128]{2,1,0:T(8,128)S(1)} %collective-permute-done.6.recv_ref, s32[16,128]{1,0:T(8,128)S(1)} %copy-done.2), custom_call_target="tpu_custom_call" | custom-call | tf_op jit(solution)/shard_map/pallas_call | solution.py:770
  (1 shorter events, 0.0 us)
Async XLA Ops:
  0.6 6.1 %collective-permute-start.1 = (bf16[3,9,8,16,128]{4,3,2,1,0:T(8,128)(2,1)}, bf16[3,9,8,16,128]{4,3,2,1,0:T(8,128)(2,1)S(1)}, u32[]{:S(2)}, u32[]{:S(2)}) collective-permute-start(bf16[3,9,8,16,128]{4,3,2,1,0:T(8,128)(2,1)} %traj_ref.1), channel_id=1, source_target_pairs={{0,1},{1,0},{2,3},{3,2},{4,5},{5,4},{6,7},{7,6},{8,9},{9,8},{10,11... | collective-permute-start | bytes 2654216 | tf_op jit(solution)/shard_map/ppermute | solution.py:799
  2.7 4.0 %collective-permute-start = (f32[12,8,16,128]{3,2,1,0:T(8,128)S(1)}, f32[12,8,16,128]{3,2,1,0:T(8,128)S(1)}, u32[]{:S(2)}, u32[]{:S(2)}) collective-permute-start(f32[12,8,16,128]{3,2,1,0:T(8,128)S(1)} %get-tuple-element.32.field_ref.refs_0_), channel_id=1, source_target_pairs={{0,1},{1,0},{2,3},{3,2},{4,5},{5,4},{6,7},{7,6},{8,9},{9,8},{10,11... | collective-permute-start | bytes 2359304 | tf_op jit(solution)/shard_map/ppermute | solution.py:799
  3.1 8.6 %copy-start = (f32[6,16]{1,0:T(8,128)S(1)}, f32[6,16]{1,0:T(8,128)}, u32[]{:S(2)}) copy-start(f32[6,16]{1,0:T(8,128)} %refs_14_.1) | copy-start | bytes 1156
  3.1 8.6 %copy-start.1 = (f32[8,9]{1,0:T(8,128)S(1)}, f32[8,9]{1,0:T(8,128)}, u32[]{:S(2)}) copy-start(f32[8,9]{1,0:T(8,128)} %refs_15_.1) | copy-start | bytes 868
  3.2 8.6 %copy-start.3 = (s32[16]{0:T(128)S(1)}, s32[16]{0:T(128)}, u32[]{:S(2)}) copy-start(s32[16]{0:T(128)} %refs_16_.1) | copy-start | bytes 196
  3.2 8.6 %copy-start.4 = (f32[16]{0:T(128)S(1)}, f32[16]{0:T(128)}, u32[]{:S(2)}) copy-start(f32[16]{0:T(128)} %refs_17_.1) | copy-start | bytes 196
  3.2 8.6 %copy-start.5 = (f32[9]{0:T(128)S(1)}, f32[9]{0:T(128)}, u32[]{:S(2)}) copy-start(f32[9]{0:T(128)} %refs_18_.1) | copy-start | bytes 112
  3.2 15.7 %collective-permute-start.3 = (bf16[124,16,128]{2,1,0:T(8,128)(2,1)S(1)}, bf16[124,16,128]{2,1,0:T(8,128)(2,1)S(1)}, u32[]{:S(2)}, u32[]{:S(2)}) collective-permute-start(bf16[124,16,128]{2,1,0:T(8,128)(2,1)S(1)} %shard_map.127), channel_id=1, source_target_pairs={{0,2},{2,0},{1,3},{3,1},{4,6},{6,4},{5,7},{7,5},{8,10},{10,8},{9,1... | collective-permute-start | bytes 1523720 | tf_op jit(solution)/shard_map/ppermute | solution.py:803
  7.6 7.6 %collective-permute-start.2 = (bf16[2,21,16,128]{3,2,1,0:T(8,128)(2,1)S(1)}, bf16[2,21,16,128]{3,2,1,0:T(8,128)(2,1)S(1)}, u32[]{:S(2)}, u32[]{:S(2)}) collective-permute-start(bf16[2,21,16,128]{3,2,1,0:T(8,128)(2,1)S(1)} %shard_map.124), channel_id=1, source_target_pairs={{1,4},{0,29},{5,8},{4,1},{9,12},{8,5},{13,16},{12,9},{17,20},{16,1... | collective-permute-start | bytes 516104 | tf_op jit(solution)/shard_map/ppermute | solution.py:843
  18.9 5.0 %collective-permute-start.4 = (bf16[124,16,128]{2,1,0:T(8,128)(2,1)S(1)}, bf16[124,16,128]{2,1,0:T(8,128)(2,1)S(1)}, u32[]{:S(2)}, u32[]{:S(2)}) collective-permute-start(bf16[124,16,128]{2,1,0:T(8,128)(2,1)S(1)} %collective-permute-done.3.refs_11_), channel_id=1, source_target_pairs={{0,1},{1,0},{2,3},{3,2},{4,5},{5,4},{6,7},{7,6},{8,9},{9,8},{10,11... | collective-permute-start | bytes 1523720 | tf_op jit(solution)/shard_map/ppermute | solution.py:799
  19.0 4.9 %collective-permute-start.5 = (bf16[21,16,128]{2,1,0:T(8,128)(2,1)S(1)}, bf16[21,16,128]{2,1,0:T(8,128)(2,1)S(1)}, u32[]{:S(2)}, u32[]{:S(2)}) collective-permute-start(bf16[21,16,128]{2,1,0:T(8,128)(2,1)S(1)} %shard_map.129), channel_id=1, source_target_pairs={{0,2},{2,0},{1,3},{3,1},{4,6},{6,4},{5,7},{7,5},{8,10},{10,8},{9,1... | collective-permute-start | bytes 258056 | tf_op jit(solution)/shard_map/ppermute | solution.py:803
  23.9 7.9 %copy-start.2 = (s32[16,128]{1,0:T(8,128)S(1)}, s32[16,128]{1,0:T(8,128)}, u32[]{:S(2)}) copy-start(s32[16,128]{1,0:T(8,128)} %source_ref.1) | copy-start | bytes 24580
  30.1 1.7 %collective-permute-start.6 = (f32[39,16,128]{2,1,0:T(8,128)S(1)}, f32[39,16,128]{2,1,0:T(8,128)S(1)}, u32[]{:S(2)}, u32[]{:S(2)}) collective-permute-start(f32[39,16,128]{2,1,0:T(8,128)S(1)} %get-tuple-element.59.send_ref), channel_id=1, source_target_pairs={{0,1},{1,0},{2,3},{3,2},{4,5},{5,4},{6,7},{7,6},{8,9},{9,8},{10,11... | collective-permute-start | bytes 958472 | tf_op jit(solution)/shard_map/ppermute | solution.py:799

commit v6 on v5

--- a/solution.py
+++ b/solution.py
@@ -111,9 +111,8 @@
 
 
 def load_kernel(adj_ref, traj_ref, wind_ref, mix_ref, land_ref, field_out, traj_out, land_out, sems):
-    pairs = [(adj_ref.at[pl.ds(3 * i, 3)], field_out.at[pl.ds(3 * i, 3)]) for i in range(3)]
-    pairs += [(wind_ref, field_out.at[pl.ds(9, 2)]), (mix_ref, field_out.at[11]), (land_ref, land_out)]
-    pairs += [(traj_ref.at[k], traj_out.at[k]) for k in range(3)]
+    pairs = [(traj_ref, traj_out), (adj_ref, field_out.at[pl.ds(0, 9)]), (wind_ref, field_out.at[pl.ds(9, 2)])]
+    pairs += [(mix_ref, field_out.at[11]), (land_ref, land_out)]
     copies = [pltpu.make_async_copy(source, target, sems.at[i]) for i, (source, target) in enumerate(pairs)]
     for copy in copies:
         copy.start()
@@ -159,9 +158,9 @@
                 out_ref[t * 8 + l] = stack_rows(v0, v1).astype(BF16)
             for j in range(4):
                 out_ref[72 + t * 4 + j] = stack_rows(v2s[2 * j], v2s[2 * j + 1]).astype(BF16)
-            return 0
-
-        lax.fori_loop(0, 9, tracer, 0)
+
+        for t in range(9):
+            tracer(t, 0)
 
         def level(l, _):
             rows = slice(base, base + 8)
@@ -179,9 +178,9 @@
             out_ref[116 + l] = stack_rows(
                 jnp.where(keep, mix_h, rolled(east_l, one)), jnp.where(keep, mix_l, rolled(east_l, two))
             ).astype(BF16)
-            return 0
-
-        lax.fori_loop(0, 8, level, 0)
+
+        for l in range(8):
+            level(l, 0)
 
     if lat_count == 2:
         pl.when(lat == 0)(lambda: fill(outs[0], True))
@@ -568,15 +567,15 @@
         for s in range(2):
             msg = lat_refs[2 * e + s]
 
-            def receive(pair, _):
-                for i in range(2):
-                    l = 2 * pair + i
+            def receive(four, _):
+                for i in range(4):
+                    l = 4 * four + i
                     z = 8 * jnp.bitwise_xor(s, core) + l
                     rate = [rate_ref[q, z] for q in range(6)]
                     adj, state = [], []
                     for t in range(9):
                         v0, v1 = halves(msg[t * 8 + l])
-                        v2 = halves(msg[72 + t * 4 + pair])[i]
+                        v2 = halves(msg[72 + t * 4 + 2 * four + i // 2])[i % 2]
                         adj.append(jnp.where(halo, corner_sum(t, z), v0 + v1))
                         tr2, tr1 = corner(12 + t, z)
                         tr0 = lane_roll(tr1, jnp.where(core == 0, 4, 124))
@@ -610,7 +609,7 @@
                     d_s[z + 1, pl.ds(own_at, 8), :] = d_ref[z + 1, pl.ds(own_row, 8), :]
                 return 0
 
-            lax.fori_loop(0, 4, receive, 0)
+            lax.fori_loop(0, 2, receive, 0)
 
         for m in range(3):
             for part in range(3):
@@ -709,9 +708,9 @@
             for l in range(4):
                 z = 8 * (1 - core) + l
                 send_ref[t * 4 + l] = jnp.where(mine, rows_of(t, z), lane_roll(rows_of(t, z + 4), 64))
-            return 0
-
-        lax.fori_loop(0, 9, tracer, 0)
+
+        for t in range(9):
+            tracer(t, 0)
         for m in range(3):
             low = em_ref[m, 0:8, :]
             high = em_ref[m, 8:16, :]
@@ -819,7 +818,7 @@
             jax.ShapeDtypeStruct(trajectory.shape, trajectory.dtype),
             jax.ShapeDtypeStruct(land_mask.shape, land_mask.dtype),
         ],
-        [pltpu.SemaphoreType.DMA((9,))],
+        [pltpu.SemaphoreType.DMA((5,))],
         *[pltpu.with_memory_space_constraint(v, pltpu.HBM) for v in given],
         specs=[pl.BlockSpec(memory_space=pltpu.HBM)] * 5,
         mib=16,

time: 33 us -> 31.9 us (0.967)
  Pallas kernels: 18.7 us -> 17.5 us
    pallas_call x10, Pallas kernels: 18.7 us -> 17.5 us  [call(): pl.pallas_call(kernel, out_shape=outs, in_specs=specs or [VMEM] * len(arg...]
  transfers between devices with their start and end apart: 7 -> 7, of which waited for: 3 -> 3; matrix products, arithmetic and copies ran while one was open for 0% -> 0% of each run, Pallas kernels for 35% -> 36%
where the time goes in v6:
time: 31.9 us; the launch traced here: 31.7 us
  Pallas kernels  17.5 us (55%)
  starting transfers between devices  9.24 us (29%)
  waiting for transfers between devices  3.96 us (12%)
  between operations  0.95 us (3%)
    pallas_call x10, Pallas kernels, call(): pl.pallas_call(kernel, out_shape=outs, in_specs=specs or [VMEM] * len(arg...  17.5 us
    ppermute x2, starting transfers between devices, lat_moves(): return [lax.ppermute(messages[0], 'lat', swap)]  4.26 us
    ppermute x1, starting transfers between devices, shards(): lon_in = lax.ppermute(lon_out, ('lon', 'lev'), lon_pairs)  4.2 us
    ppermute x4, waiting for transfers between devices, over_lev(): return lax.ppermute(value, 'lev', swap)  1.61 us
    ppermute x1, waiting for transfers between devices, shards(): lon_in = lax.ppermute(lon_out, ('lon', 'lev'), lon_pairs)  1.57 us
    ppermute x4, starting transfers between devices, over_lev(): return lax.ppermute(value, 'lev', swap)  0.78 us
    ppermute x2, waiting for transfers between devices, lat_moves(): return [lax.ppermute(messages[0], 'lat', swap)]  0.77 us
  transfers between devices with their start and end apart: 7, of which 3 were waited for; matrix products, arithmetic and copies ran while one was open for 0% of the time, Pallas kernels for 36%

profile of v6, /device:TPU:0, one launch (start us, length us, event | category | flops | bytes accessed | tf_op | source)
XLA Modules:
  0.0 31.7 jit_solution(3251473935135423402)
XLA Ops:
  0.6 0.5 %collective-permute-start.1 = (bf16[3,9,8,16,128]{4,3,2,1,0:T(8,128)(2,1)}, bf16[3,9,8,16,128]{4,3,2,1,0:T(8,128)(2,1)S(1)}, u32[]{:S(2)}, u32[]{:S(2)}) collective-permute-start(bf16[3,9,8,16,128]{4,3,2,1,0:T(8,128)(2,1)} %traj_ref.1), channel_id=1, source_target_pairs={{0,1},{1,0},{2,3},{3,2},{4,5},{5,4},{6,7},{7,6},{8,9},{9,8},{10,11... | collective-permute-start | bytes 2654216 | tf_op jit(solution)/shard_map/ppermute | solution.py:798
  1.1 1.4 %shard_map.122 = (f32[12,8,16,128]{3,2,1,0:T(8,128)S(1)}, bf16[3,9,8,16,128]{4,3,2,1,0:T(8,128)(2,1)S(1)}, s32[16,128]{1,0:T(8,128)S(1)}) custom-call(f32[9,8,16,128]{3,2,1,0:T(8,128)} %adj_ref.1, bf16[3,9,8,16,128]{4,3,2,1,0:T(8,128)(2,1)} %traj_ref.1, f32[2,8,16,128]{3,2,1,0:T(8,128)} %wind_ref.1, f32[8,16,128]{2,1,0:T(8,128)} %mix_ref.1, s32[16,128]{1,0:T(8,128)} %land_ref.1), custom_call_target="tpu_custom_call" | custom-call | tf_op jit(solution)/shard_map/pallas_call | solution.py:769
  2.6 0.1 collective-permute-start
  2.7 0.2 shard_map.127
  2.8 0.0 copy-start
  2.9 0.0 copy-start.1
  2.9 0.0 copy-start.3
  2.9 0.0 copy-start.4
  2.9 0.0 copy-start.5
  2.9 3.0 %collective-permute-start.3 = (bf16[124,16,128]{2,1,0:T(8,128)(2,1)S(1)}, bf16[124,16,128]{2,1,0:T(8,128)(2,1)S(1)}, u32[]{:S(2)}, u32[]{:S(2)}) collective-permute-start(bf16[124,16,128]{2,1,0:T(8,128)(2,1)S(1)} %shard_map.127), channel_id=1, source_target_pairs={{0,2},{2,0},{1,3},{3,1},{4,6},{6,4},{5,7},{7,5},{8,10},{10,8},{9,1... | collective-permute-start | bytes 1523720 | tf_op jit(solution)/shard_map/ppermute | solution.py:802
  5.9 0.5 %shard_map.123 = (f32[12,16,128]{2,1,0:T(8,128)S(1)}, bf16[27,16,128]{2,1,0:T(8,128)(2,1)S(1)}) custom-call(f32[12,8,16,128]{3,2,1,0:T(8,128)S(1)} %get-tuple-element.32.field_ref.refs_0_, bf16[3,9,8,16,128]{4,3,2,1,0:T(8,128)(2,1)S(1)} %get-tuple-element.33.traj_ref.refs_1_, s32[16,128]{1,0:T(8,128)S(1)} %get-tuple-element.31.land_ref.refs_4_.refs_0_.refs_2_), custom_call_target="tpu_custom_call" | custom-call | tf_op jit(solution)/shard_map/pallas_call | solution.py:769
  6.4 0.0 collective-permute-done.field_ref.refs_2_
  6.4 0.0 collective-permute-done.1.traj_ref.refs_3_
  6.4 0.9 %shard_map.124 = bf16[2,21,16,128]{3,2,1,0:T(8,128)(2,1)S(1)} custom-call(f32[12,8,16,128]{3,2,1,0:T(8,128)S(1)} %collective-permute-done.field_ref.refs_2_, bf16[3,9,8,16,128]{4,3,2,1,0:T(8,128)(2,1)S(1)} %collective-permute-done.1.traj_ref.refs_3_, s32[16,128]{1,0:T(8,128)S(1)} %get-tuple-element.31.land_ref.refs_4_.refs_0_.refs_2_, ...), custom_call_target="tpu_custom_call" | custom-call | tf_op jit(solution)/shard_map/pallas_call | solution.py:769
  7.4 4.2 %collective-permute-start.2 = (bf16[2,21,16,128]{3,2,1,0:T(8,128)(2,1)S(1)}, bf16[2,21,16,128]{3,2,1,0:T(8,128)(2,1)S(1)}, u32[]{:S(2)}, u32[]{:S(2)}) collective-permute-start(bf16[2,21,16,128]{3,2,1,0:T(8,128)(2,1)S(1)} %shard_map.124), channel_id=1, source_target_pairs={{1,4},{0,29},{5,8},{4,1},{9,12},{8,5},{13,16},{12,9},{17,20},{16,1... | collective-permute-start | bytes 516104 | tf_op jit(solution)/shard_map/ppermute | solution.py:842
  11.6 0.0 copy-done
  11.6 0.0 copy-done.1
  11.6 0.0 copy-done.3
  11.6 0.0 copy-done.4
  11.6 0.0 copy-done.5
  11.6 1.8 %shard_map.125 = (f32[9,16,16,128]{3,2,1,0:T(8,128)S(1)}, f32[3,16,128]{2,1,0:T(8,128)S(1)}, bf16[2,9,16,16,128]{4,3,2,1,0:T(8,128)(2,1)S(1)}, f32[2,16,16,128]{3,2,1,0:T(8,128)S(1)}, f32[16,16,128]{2,1,0:T(8,128)S(1)}) custom-call(f32[12,8,16,128]{3,2,1,0:T(8,128)S(1)} %get-tuple-element.32.field_ref.refs_0_, ...), custom_call_target="tpu_custom_call" | custom-call | tf_op jit(solution)/shard_map/pallas_call | solution.py:769
  13.4 1.6 %collective-permute-done.2.refs_1_.lon_ref = bf16[2,21,16,128]{3,2,1,0:T(8,128)(2,1)S(1)} collective-permute-done((bf16[2,21,16,128]{3,2,1,0:T(8,128)(2,1)S(1)}, bf16[2,21,16,128]{3,2,1,0:T(8,128)(2,1)S(1)}, u32[]{:S(2)}, u32[]{:S(2)}) %collective-permute-start.2) | collective-permute-done | bytes 172064 | tf_op jit(solution)/shard_map/ppermute | solution.py:842
  15.0 3.6 %shard_map.126 = (bf16[9,16,16,128]{3,2,1,0:T(8,128)(2,1)S(1)}, f32[9,16,32,128]{3,2,1,0:T(8,128)S(1)}, f32[9,16,32,128]{3,2,1,0:T(8,128)S(1)}, f32[16,32,128]{2...) custom-call(s32[16,128]{1,0:T(8,128)S(1)} %get-tuple-element.31.land, ...), custom_call_target="tpu_custom_call" | custom-call | tf_op jit(solution)/shard_map/pallas_call | solution.py:769
  18.6 0.0 collective-permute-done.3.refs_11_
  18.6 0.1 collective-permute-start.4
  18.7 1.3 %collective-permute-start.5 = (bf16[21,16,128]{2,1,0:T(8,128)(2,1)S(1)}, bf16[21,16,128]{2,1,0:T(8,128)(2,1)S(1)}, u32[]{:S(2)}, u32[]{:S(2)}) collective-permute-start(bf16[21,16,128]{2,1,0:T(8,128)(2,1)S(1)} %shard_map.129), channel_id=1, source_target_pairs={{0,2},{2,0},{1,3},{3,1},{4,6},{6,4},{5,7},{7,5},{8,10},{10,8},{9,1... | collective-permute-start | bytes 258056 | tf_op jit(solution)/shard_map/ppermute | solution.py:802
  19.9 2.9 %shard_map.128 = (f32[9,16,32,128]{3,2,1,0:T(8,128)S(1)}, f32[3,16,128]{2,1,0:T(8,128)S(1)}, bf16[9,16,16,128]{3,2,1,0:T(8,128)(2,1)S(1)}) custom-call(bf16[2,9,16,16,128]{4,3,2,1,0:T(8,128)(2,1)S(1)} %get-tuple-element.40.refs_4_.refs_0_, bf16[9,16,128]{2,1,0:T(8,128)(2,1)S(1)} %get-tuple-element.51.refs_1_, ...), custom_call_target="tpu_custom_call" | custom-call | tf_op jit(solution)/shard_map/pallas_call | solution.py:769
  22.8 0.8 %collective-permute-done.5.refs_13_ = bf16[21,16,128]{2,1,0:T(8,128)(2,1)S(1)} collective-permute-done((bf16[21,16,128]{2,1,0:T(8,128)(2,1)S(1)}, bf16[21,16,128]{2,1,0:T(8,128)(2,1)S(1)}, u32[]{:S(2)}, u32[]{:S(2)}) %collective-permute-start.5) | collective-permute-done | bytes 86048 | tf_op jit(solution)/shard_map/ppermute | solution.py:802
  23.6 0.0 collective-permute-done.4.refs_12_
  23.6 0.0 copy-start.2
  23.6 5.3 %shard_map.130 = (f32[9,8,16,128]{3,2,1,0:T(8,128)S(1)}, f32[39,16,128]{2,1,0:T(8,128)S(1)}) custom-call(bf16[9,16,16,128]{3,2,1,0:T(8,128)(2,1)S(1)} %get-tuple-element.43.refs_0_, f32[9,16,32,128]{3,2,1,0:T(8,128)S(1)} %get-tuple-element.44.refs_1_, f32[9,16,32,128]{3,2,1,0:T(8,128)S(1)} %get-tuple-element.46.refs_5_.refs_2_, ...), custom_call_target="tpu_custom_call" | custom-call | tf_op jit(solution)/shard_map/pallas_call | solution.py:769
  28.9 0.1 collective-permute-start.6
  29.0 1.6 %collective-permute-done.6.recv_ref = f32[39,16,128]{2,1,0:T(8,128)S(1)} collective-permute-done((f32[39,16,128]{2,1,0:T(8,128)S(1)}, f32[39,16,128]{2,1,0:T(8,128)S(1)}, u32[]{:S(2)}, u32[]{:S(2)}) %collective-permute-start.6) | collective-permute-done | bytes 319520 | tf_op jit(solution)/shard_map/ppermute | solution.py:798
  30.6 0.0 copy-done.2
  30.6 1.0 %shard_map.131 = (f32[9,8,16,128]{3,2,1,0:T(8,128)}, f32[3,16,128]{2,1,0:T(8,128)}) custom-call(f32[9,8,16,128]{3,2,1,0:T(8,128)S(1)} %get-tuple-element.58.keep_ref, f32[39,16,128]{2,1,0:T(8,128)S(1)} %get-tuple-element.59.send_ref, f32[39,16,128]{2,1,0:T(8,128)S(1)} %collective-permute-done.6.recv_ref, s32[16,128]{1,0:T(8,128)S(1)} %copy-done.2), custom_call_target="tpu_custom_call" | custom-call | tf_op jit(solution)/shard_map/pallas_call | solution.py:769
  (1 shorter events, 0.0 us)
Async XLA Ops:
  0.6 5.8 %collective-permute-start.1 = (bf16[3,9,8,16,128]{4,3,2,1,0:T(8,128)(2,1)}, bf16[3,9,8,16,128]{4,3,2,1,0:T(8,128)(2,1)S(1)}, u32[]{:S(2)}, u32[]{:S(2)}) collective-permute-start(bf16[3,9,8,16,128]{4,3,2,1,0:T(8,128)(2,1)} %traj_ref.1), channel_id=1, source_target_pairs={{0,1},{1,0},{2,3},{3,2},{4,5},{5,4},{6,7},{7,6},{8,9},{9,8},{10,11... | collective-permute-start | bytes 2654216 | tf_op jit(solution)/shard_map/ppermute | solution.py:798
  2.6 3.9 %collective-permute-start = (f32[12,8,16,128]{3,2,1,0:T(8,128)S(1)}, f32[12,8,16,128]{3,2,1,0:T(8,128)S(1)}, u32[]{:S(2)}, u32[]{:S(2)}) collective-permute-start(f32[12,8,16,128]{3,2,1,0:T(8,128)S(1)} %get-tuple-element.32.field_ref.refs_0_), channel_id=1, source_target_pairs={{0,1},{1,0},{2,3},{3,2},{4,5},{5,4},{6,7},{7,6},{8,9},{9,8},{10,11... | collective-permute-start | bytes 2359304 | tf_op jit(solution)/shard_map/ppermute | solution.py:798
  2.8 8.7 %copy-start = (f32[6,16]{1,0:T(8,128)S(1)}, f32[6,16]{1,0:T(8,128)}, u32[]{:S(2)}) copy-start(f32[6,16]{1,0:T(8,128)} %refs_14_.1) | copy-start | bytes 1156
  2.9 8.7 %copy-start.1 = (f32[8,9]{1,0:T(8,128)S(1)}, f32[8,9]{1,0:T(8,128)}, u32[]{:S(2)}) copy-start(f32[8,9]{1,0:T(8,128)} %refs_15_.1) | copy-start | bytes 868
  2.9 8.7 %copy-start.3 = (s32[16]{0:T(128)S(1)}, s32[16]{0:T(128)}, u32[]{:S(2)}) copy-start(s32[16]{0:T(128)} %refs_16_.1) | copy-start | bytes 196
  2.9 8.7 %copy-start.4 = (f32[16]{0:T(128)S(1)}, f32[16]{0:T(128)}, u32[]{:S(2)}) copy-start(f32[16]{0:T(128)} %refs_17_.1) | copy-start | bytes 196
  2.9 8.7 %copy-start.5 = (f32[9]{0:T(128)S(1)}, f32[9]{0:T(128)}, u32[]{:S(2)}) copy-start(f32[9]{0:T(128)} %refs_18_.1) | copy-start | bytes 112
  2.9 15.7 %collective-permute-start.3 = (bf16[124,16,128]{2,1,0:T(8,128)(2,1)S(1)}, bf16[124,16,128]{2,1,0:T(8,128)(2,1)S(1)}, u32[]{:S(2)}, u32[]{:S(2)}) collective-permute-start(bf16[124,16,128]{2,1,0:T(8,128)(2,1)S(1)} %shard_map.127), channel_id=1, source_target_pairs={{0,2},{2,0},{1,3},{3,1},{4,6},{6,4},{5,7},{7,5},{8,10},{10,8},{9,1... | collective-permute-start | bytes 1523720 | tf_op jit(solution)/shard_map/ppermute | solution.py:802
  7.4 7.6 %collective-permute-start.2 = (bf16[2,21,16,128]{3,2,1,0:T(8,128)(2,1)S(1)}, bf16[2,21,16,128]{3,2,1,0:T(8,128)(2,1)S(1)}, u32[]{:S(2)}, u32[]{:S(2)}) collective-permute-start(bf16[2,21,16,128]{3,2,1,0:T(8,128)(2,1)S(1)} %shard_map.124), channel_id=1, source_target_pairs={{1,4},{0,29},{5,8},{4,1},{9,12},{8,5},{13,16},{12,9},{17,20},{16,1... | collective-permute-start | bytes 516104 | tf_op jit(solution)/shard_map/ppermute | solution.py:842
  18.6 5.0 %collective-permute-start.4 = (bf16[124,16,128]{2,1,0:T(8,128)(2,1)S(1)}, bf16[124,16,128]{2,1,0:T(8,128)(2,1)S(1)}, u32[]{:S(2)}, u32[]{:S(2)}) collective-permute-start(bf16[124,16,128]{2,1,0:T(8,128)(2,1)S(1)} %collective-permute-done.3.refs_11_), channel_id=1, source_target_pairs={{0,1},{1,0},{2,3},{3,2},{4,5},{5,4},{6,7},{7,6},{8,9},{9,8},{10,11... | collective-permute-start | bytes 1523720 | tf_op jit(solution)/shard_map/ppermute | solution.py:798
  18.7 4.9 %collective-permute-start.5 = (bf16[21,16,128]{2,1,0:T(8,128)(2,1)S(1)}, bf16[21,16,128]{2,1,0:T(8,128)(2,1)S(1)}, u32[]{:S(2)}, u32[]{:S(2)}) collective-permute-start(bf16[21,16,128]{2,1,0:T(8,128)(2,1)S(1)} %shard_map.129), channel_id=1, source_target_pairs={{0,2},{2,0},{1,3},{3,1},{4,6},{6,4},{5,7},{7,5},{8,10},{10,8},{9,1... | collective-permute-start | bytes 258056 | tf_op jit(solution)/shard_map/ppermute | solution.py:802
  23.6 7.0 %copy-start.2 = (s32[16,128]{1,0:T(8,128)S(1)}, s32[16,128]{1,0:T(8,128)}, u32[]{:S(2)}) copy-start(s32[16,128]{1,0:T(8,128)} %source_ref.1) | copy-start | bytes 24580
  28.9 1.7 %collective-permute-start.6 = (f32[39,16,128]{2,1,0:T(8,128)S(1)}, f32[39,16,128]{2,1,0:T(8,128)S(1)}, u32[]{:S(2)}, u32[]{:S(2)}) collective-permute-start(f32[39,16,128]{2,1,0:T(8,128)S(1)} %get-tuple-element.59.send_ref), channel_id=1, source_target_pairs={{0,1},{1,0},{2,3},{3,2},{4,5},{5,4},{6,7},{7,6},{8,9},{9,8},{10,11... | collective-permute-start | bytes 958472 | tf_op jit(solution)/shard_map/ppermute | solution.py:798

commit v7 on v6

--- a/solution.py
+++ b/solution.py
@@ -497,7 +497,7 @@
         mixed(scalars, b_s, d, deposit, lambda t, i, value: put_rows(c_out, t, i, value), z)
         return sums
 
-    return [(lag, move), (lag + 1, do_react), (lag + 3, mix)]
+    return [(lag, move), (lag + 2, do_react), (lag + 5, mix)]
 
 
 def third_kernel(lat_count, *refs):
@@ -679,7 +679,7 @@
         def moving(step):
             return lambda z, sums: move(step, z, sums)
 
-        count(0, pipeline([(0, mixing(0)), (1, moving(0)), (3, mixing(1))], none))
+        count(0, pipeline([(0, mixing(0)), (2, moving(0)), (5, mixing(1))], none))
 
         def far_moving(z, sums):
             near = 0 if upper else 8
@@ -689,7 +689,7 @@
                 fin_s[1, t, z] = transported(rows, w)
             return sums
 
-        later = [(0, moving(1)), (2, mixing(2)), (3, moving(2))] + [(3, far_moving)] * far
+        later = [(0, moving(1)), (3, mixing(2)), (5, moving(2))] + [(4, far_moving)] * far
         count(1, pipeline(later, none))
         for m in range(3):
             a_s[e, m] = em_s[m, own_at : own_at + 8, :]

time: 31.9 us -> 31.9 us (level)
  no operation moved by 1% of the time
where the time goes in v7:
time: 31.9 us; the launch traced here: 31.7 us
  Pallas kernels  17.5 us (55%)
  starting transfers between devices  9.24 us (29%)
  waiting for transfers between devices  3.96 us (12%)
  between operations  0.95 us (3%)
    pallas_call x10, Pallas kernels, call(): pl.pallas_call(kernel, out_shape=outs, in_specs=specs or [VMEM] * len(arg...  17.5 us
    ppermute x2, starting transfers between devices, lat_moves(): return [lax.ppermute(messages[0], 'lat', swap)]  4.26 us
    ppermute x1, starting transfers between devices, shards(): lon_in = lax.ppermute(lon_out, ('lon', 'lev'), lon_pairs)  4.2 us
    ppermute x4, waiting for transfers between devices, over_lev(): return lax.ppermute(value, 'lev', swap)  1.61 us
    ppermute x1, waiting for transfers between devices, shards(): lon_in = lax.ppermute(lon_out, ('lon', 'lev'), lon_pairs)  1.57 us
    ppermute x4, starting transfers between devices, over_lev(): return lax.ppermute(value, 'lev', swap)  0.78 us
    ppermute x2, waiting for transfers between devices, lat_moves(): return [lax.ppermute(messages[0], 'lat', swap)]  0.77 us
  transfers between devices with their start and end apart: 7, of which 3 were waited for; matrix products, arithmetic and copies ran while one was open for 0% of the time, Pallas kernels for 36%

profile of v7, /device:TPU:0, one launch (start us, length us, event | category | flops | bytes accessed | tf_op | source)
XLA Modules:
  0.0 31.7 jit_solution(9468076552446996305)
XLA Ops:
  0.6 0.5 %collective-permute-start.1 = (bf16[3,9,8,16,128]{4,3,2,1,0:T(8,128)(2,1)}, bf16[3,9,8,16,128]{4,3,2,1,0:T(8,128)(2,1)S(1)}, u32[]{:S(2)}, u32[]{:S(2)}) collective-permute-start(bf16[3,9,8,16,128]{4,3,2,1,0:T(8,128)(2,1)} %traj_ref.1), channel_id=1, source_target_pairs={{0,1},{1,0},{2,3},{3,2},{4,5},{5,4},{6,7},{7,6},{8,9},{9,8},{10,11... | collective-permute-start | bytes 2654216 | tf_op jit(solution)/shard_map/ppermute | solution.py:798
  1.1 1.4 %shard_map.122 = (f32[12,8,16,128]{3,2,1,0:T(8,128)S(1)}, bf16[3,9,8,16,128]{4,3,2,1,0:T(8,128)(2,1)S(1)}, s32[16,128]{1,0:T(8,128)S(1)}) custom-call(f32[9,8,16,128]{3,2,1,0:T(8,128)} %adj_ref.1, bf16[3,9,8,16,128]{4,3,2,1,0:T(8,128)(2,1)} %traj_ref.1, f32[2,8,16,128]{3,2,1,0:T(8,128)} %wind_ref.1, f32[8,16,128]{2,1,0:T(8,128)} %mix_ref.1, s32[16,128]{1,0:T(8,128)} %land_ref.1), custom_call_target="tpu_custom_call" | custom-call | tf_op jit(solution)/shard_map/pallas_call | solution.py:769
  2.6 0.1 collective-permute-start
  2.7 0.2 shard_map.127
  2.8 0.0 copy-start
  2.9 0.0 copy-start.1
  2.9 0.0 copy-start.3
  2.9 0.0 copy-start.4
  2.9 0.0 copy-start.5
  2.9 3.0 %collective-permute-start.3 = (bf16[124,16,128]{2,1,0:T(8,128)(2,1)S(1)}, bf16[124,16,128]{2,1,0:T(8,128)(2,1)S(1)}, u32[]{:S(2)}, u32[]{:S(2)}) collective-permute-start(bf16[124,16,128]{2,1,0:T(8,128)(2,1)S(1)} %shard_map.127), channel_id=1, source_target_pairs={{0,2},{2,0},{1,3},{3,1},{4,6},{6,4},{5,7},{7,5},{8,10},{10,8},{9,1... | collective-permute-start | bytes 1523720 | tf_op jit(solution)/shard_map/ppermute | solution.py:802
  5.9 0.5 %shard_map.123 = (f32[12,16,128]{2,1,0:T(8,128)S(1)}, bf16[27,16,128]{2,1,0:T(8,128)(2,1)S(1)}) custom-call(f32[12,8,16,128]{3,2,1,0:T(8,128)S(1)} %get-tuple-element.32.field_ref.refs_0_, bf16[3,9,8,16,128]{4,3,2,1,0:T(8,128)(2,1)S(1)} %get-tuple-element.33.traj_ref.refs_1_, s32[16,128]{1,0:T(8,128)S(1)} %get-tuple-element.31.land_ref.refs_4_.refs_0_.refs_2_), custom_call_target="tpu_custom_call" | custom-call | tf_op jit(solution)/shard_map/pallas_call | solution.py:769
  6.4 0.0 collective-permute-done.field_ref.refs_2_
  6.4 0.0 collective-permute-done.1.traj_ref.refs_3_
  6.4 0.9 %shard_map.124 = bf16[2,21,16,128]{3,2,1,0:T(8,128)(2,1)S(1)} custom-call(f32[12,8,16,128]{3,2,1,0:T(8,128)S(1)} %collective-permute-done.field_ref.refs_2_, bf16[3,9,8,16,128]{4,3,2,1,0:T(8,128)(2,1)S(1)} %collective-permute-done.1.traj_ref.refs_3_, s32[16,128]{1,0:T(8,128)S(1)} %get-tuple-element.31.land_ref.refs_4_.refs_0_.refs_2_, ...), custom_call_target="tpu_custom_call" | custom-call | tf_op jit(solution)/shard_map/pallas_call | solution.py:769
  7.4 4.2 %collective-permute-start.2 = (bf16[2,21,16,128]{3,2,1,0:T(8,128)(2,1)S(1)}, bf16[2,21,16,128]{3,2,1,0:T(8,128)(2,1)S(1)}, u32[]{:S(2)}, u32[]{:S(2)}) collective-permute-start(bf16[2,21,16,128]{3,2,1,0:T(8,128)(2,1)S(1)} %shard_map.124), channel_id=1, source_target_pairs={{1,4},{0,29},{5,8},{4,1},{9,12},{8,5},{13,16},{12,9},{17,20},{16,1... | collective-permute-start | bytes 516104 | tf_op jit(solution)/shard_map/ppermute | solution.py:842
  11.6 0.0 copy-done
  11.6 0.0 copy-done.1
  11.6 0.0 copy-done.3
  11.6 0.0 copy-done.4
  11.6 0.0 copy-done.5
  11.6 1.8 %shard_map.125 = (f32[9,16,16,128]{3,2,1,0:T(8,128)S(1)}, f32[3,16,128]{2,1,0:T(8,128)S(1)}, bf16[2,9,16,16,128]{4,3,2,1,0:T(8,128)(2,1)S(1)}, f32[2,16,16,128]{3,2,1,0:T(8,128)S(1)}, f32[16,16,128]{2,1,0:T(8,128)S(1)}) custom-call(f32[12,8,16,128]{3,2,1,0:T(8,128)S(1)} %get-tuple-element.32.field_ref.refs_0_, ...), custom_call_target="tpu_custom_call" | custom-call | tf_op jit(solution)/shard_map/pallas_call | solution.py:769
  13.4 1.6 %collective-permute-done.2.refs_1_.lon_ref = bf16[2,21,16,128]{3,2,1,0:T(8,128)(2,1)S(1)} collective-permute-done((bf16[2,21,16,128]{3,2,1,0:T(8,128)(2,1)S(1)}, bf16[2,21,16,128]{3,2,1,0:T(8,128)(2,1)S(1)}, u32[]{:S(2)}, u32[]{:S(2)}) %collective-permute-start.2) | collective-permute-done | bytes 172064 | tf_op jit(solution)/shard_map/ppermute | solution.py:842
  15.0 3.6 %shard_map.126 = (bf16[9,16,16,128]{3,2,1,0:T(8,128)(2,1)S(1)}, f32[9,16,32,128]{3,2,1,0:T(8,128)S(1)}, f32[9,16,32,128]{3,2,1,0:T(8,128)S(1)}, f32[16,32,128]{2...) custom-call(s32[16,128]{1,0:T(8,128)S(1)} %get-tuple-element.31.land, ...), custom_call_target="tpu_custom_call" | custom-call | tf_op jit(solution)/shard_map/pallas_call | solution.py:769
  18.6 0.0 collective-permute-done.3.refs_11_
  18.6 0.1 collective-permute-start.4
  18.7 1.3 %collective-permute-start.5 = (bf16[21,16,128]{2,1,0:T(8,128)(2,1)S(1)}, bf16[21,16,128]{2,1,0:T(8,128)(2,1)S(1)}, u32[]{:S(2)}, u32[]{:S(2)}) collective-permute-start(bf16[21,16,128]{2,1,0:T(8,128)(2,1)S(1)} %shard_map.129), channel_id=1, source_target_pairs={{0,2},{2,0},{1,3},{3,1},{4,6},{6,4},{5,7},{7,5},{8,10},{10,8},{9,1... | collective-permute-start | bytes 258056 | tf_op jit(solution)/shard_map/ppermute | solution.py:802
  19.9 2.9 %shard_map.128 = (f32[9,16,32,128]{3,2,1,0:T(8,128)S(1)}, f32[3,16,128]{2,1,0:T(8,128)S(1)}, bf16[9,16,16,128]{3,2,1,0:T(8,128)(2,1)S(1)}) custom-call(bf16[2,9,16,16,128]{4,3,2,1,0:T(8,128)(2,1)S(1)} %get-tuple-element.40.refs_4_.refs_0_, bf16[9,16,128]{2,1,0:T(8,128)(2,1)S(1)} %get-tuple-element.51.refs_1_, ...), custom_call_target="tpu_custom_call" | custom-call | tf_op jit(solution)/shard_map/pallas_call | solution.py:769
  22.8 0.8 %collective-permute-done.5.refs_13_ = bf16[21,16,128]{2,1,0:T(8,128)(2,1)S(1)} collective-permute-done((bf16[21,16,128]{2,1,0:T(8,128)(2,1)S(1)}, bf16[21,16,128]{2,1,0:T(8,128)(2,1)S(1)}, u32[]{:S(2)}, u32[]{:S(2)}) %collective-permute-start.5) | collective-permute-done | bytes 86048 | tf_op jit(solution)/shard_map/ppermute | solution.py:802
  23.6 0.0 collective-permute-done.4.refs_12_
  23.6 0.0 copy-start.2
  23.6 5.3 %shard_map.130 = (f32[9,8,16,128]{3,2,1,0:T(8,128)S(1)}, f32[39,16,128]{2,1,0:T(8,128)S(1)}) custom-call(bf16[9,16,16,128]{3,2,1,0:T(8,128)(2,1)S(1)} %get-tuple-element.43.refs_0_, f32[9,16,32,128]{3,2,1,0:T(8,128)S(1)} %get-tuple-element.44.refs_1_, f32[9,16,32,128]{3,2,1,0:T(8,128)S(1)} %get-tuple-element.46.refs_5_.refs_2_, ...), custom_call_target="tpu_custom_call" | custom-call | tf_op jit(solution)/shard_map/pallas_call | solution.py:769
  28.9 0.1 collective-permute-start.6
  29.0 1.6 %collective-permute-done.6.recv_ref = f32[39,16,128]{2,1,0:T(8,128)S(1)} collective-permute-done((f32[39,16,128]{2,1,0:T(8,128)S(1)}, f32[39,16,128]{2,1,0:T(8,128)S(1)}, u32[]{:S(2)}, u32[]{:S(2)}) %collective-permute-start.6) | collective-permute-done | bytes 319520 | tf_op jit(solution)/shard_map/ppermute | solution.py:798
  30.6 0.0 copy-done.2
  30.6 1.0 %shard_map.131 = (f32[9,8,16,128]{3,2,1,0:T(8,128)}, f32[3,16,128]{2,1,0:T(8,128)}) custom-call(f32[9,8,16,128]{3,2,1,0:T(8,128)S(1)} %get-tuple-element.58.keep_ref, f32[39,16,128]{2,1,0:T(8,128)S(1)} %get-tuple-element.59.send_ref, f32[39,16,128]{2,1,0:T(8,128)S(1)} %collective-permute-done.6.recv_ref, s32[16,128]{1,0:T(8,128)S(1)} %copy-done.2), custom_call_target="tpu_custom_call" | custom-call | tf_op jit(solution)/shard_map/pallas_call | solution.py:769
  (1 shorter events, 0.0 us)
Async XLA Ops:
  0.6 5.8 %collective-permute-start.1 = (bf16[3,9,8,16,128]{4,3,2,1,0:T(8,128)(2,1)}, bf16[3,9,8,16,128]{4,3,2,1,0:T(8,128)(2,1)S(1)}, u32[]{:S(2)}, u32[]{:S(2)}) collective-permute-start(bf16[3,9,8,16,128]{4,3,2,1,0:T(8,128)(2,1)} %traj_ref.1), channel_id=1, source_target_pairs={{0,1},{1,0},{2,3},{3,2},{4,5},{5,4},{6,7},{7,6},{8,9},{9,8},{10,11... | collective-permute-start | bytes 2654216 | tf_op jit(solution)/shard_map/ppermute | solution.py:798
  2.6 3.9 %collective-permute-start = (f32[12,8,16,128]{3,2,1,0:T(8,128)S(1)}, f32[12,8,16,128]{3,2,1,0:T(8,128)S(1)}, u32[]{:S(2)}, u32[]{:S(2)}) collective-permute-start(f32[12,8,16,128]{3,2,1,0:T(8,128)S(1)} %get-tuple-element.32.field_ref.refs_0_), channel_id=1, source_target_pairs={{0,1},{1,0},{2,3},{3,2},{4,5},{5,4},{6,7},{7,6},{8,9},{9,8},{10,11... | collective-permute-start | bytes 2359304 | tf_op jit(solution)/shard_map/ppermute | solution.py:798
  2.8 8.7 %copy-start = (f32[6,16]{1,0:T(8,128)S(1)}, f32[6,16]{1,0:T(8,128)}, u32[]{:S(2)}) copy-start(f32[6,16]{1,0:T(8,128)} %refs_14_.1) | copy-start | bytes 1156
  2.9 8.7 %copy-start.1 = (f32[8,9]{1,0:T(8,128)S(1)}, f32[8,9]{1,0:T(8,128)}, u32[]{:S(2)}) copy-start(f32[8,9]{1,0:T(8,128)} %refs_15_.1) | copy-start | bytes 868
  2.9 8.7 %copy-start.3 = (s32[16]{0:T(128)S(1)}, s32[16]{0:T(128)}, u32[]{:S(2)}) copy-start(s32[16]{0:T(128)} %refs_16_.1) | copy-start | bytes 196
  2.9 8.7 %copy-start.4 = (f32[16]{0:T(128)S(1)}, f32[16]{0:T(128)}, u32[]{:S(2)}) copy-start(f32[16]{0:T(128)} %refs_17_.1) | copy-start | bytes 196
  2.9 8.7 %copy-start.5 = (f32[9]{0:T(128)S(1)}, f32[9]{0:T(128)}, u32[]{:S(2)}) copy-start(f32[9]{0:T(128)} %refs_18_.1) | copy-start | bytes 112
  2.9 15.7 %collective-permute-start.3 = (bf16[124,16,128]{2,1,0:T(8,128)(2,1)S(1)}, bf16[124,16,128]{2,1,0:T(8,128)(2,1)S(1)}, u32[]{:S(2)}, u32[]{:S(2)}) collective-permute-start(bf16[124,16,128]{2,1,0:T(8,128)(2,1)S(1)} %shard_map.127), channel_id=1, source_target_pairs={{0,2},{2,0},{1,3},{3,1},{4,6},{6,4},{5,7},{7,5},{8,10},{10,8},{9,1... | collective-permute-start | bytes 1523720 | tf_op jit(solution)/shard_map/ppermute | solution.py:802
  7.4 7.6 %collective-permute-start.2 = (bf16[2,21,16,128]{3,2,1,0:T(8,128)(2,1)S(1)}, bf16[2,21,16,128]{3,2,1,0:T(8,128)(2,1)S(1)}, u32[]{:S(2)}, u32[]{:S(2)}) collective-permute-start(bf16[2,21,16,128]{3,2,1,0:T(8,128)(2,1)S(1)} %shard_map.124), channel_id=1, source_target_pairs={{1,4},{0,29},{5,8},{4,1},{9,12},{8,5},{13,16},{12,9},{17,20},{16,1... | collective-permute-start | bytes 516104 | tf_op jit(solution)/shard_map/ppermute | solution.py:842
  18.6 5.0 %collective-permute-start.4 = (bf16[124,16,128]{2,1,0:T(8,128)(2,1)S(1)}, bf16[124,16,128]{2,1,0:T(8,128)(2,1)S(1)}, u32[]{:S(2)}, u32[]{:S(2)}) collective-permute-start(bf16[124,16,128]{2,1,0:T(8,128)(2,1)S(1)} %collective-permute-done.3.refs_11_), channel_id=1, source_target_pairs={{0,1},{1,0},{2,3},{3,2},{4,5},{5,4},{6,7},{7,6},{8,9},{9,8},{10,11... | collective-permute-start | bytes 1523720 | tf_op jit(solution)/shard_map/ppermute | solution.py:798
  18.7 4.9 %collective-permute-start.5 = (bf16[21,16,128]{2,1,0:T(8,128)(2,1)S(1)}, bf16[21,16,128]{2,1,0:T(8,128)(2,1)S(1)}, u32[]{:S(2)}, u32[]{:S(2)}) collective-permute-start(bf16[21,16,128]{2,1,0:T(8,128)(2,1)S(1)} %shard_map.129), channel_id=1, source_target_pairs={{0,2},{2,0},{1,3},{3,1},{4,6},{6,4},{5,7},{7,5},{8,10},{10,8},{9,1... | collective-permute-start | bytes 258056 | tf_op jit(solution)/shard_map/ppermute | solution.py:802
  23.6 7.0 %copy-start.2 = (s32[16,128]{1,0:T(8,128)S(1)}, s32[16,128]{1,0:T(8,128)}, u32[]{:S(2)}) copy-start(s32[16,128]{1,0:T(8,128)} %source_ref.1) | copy-start | bytes 24580
  28.9 1.7 %collective-permute-start.6 = (f32[39,16,128]{2,1,0:T(8,128)S(1)}, f32[39,16,128]{2,1,0:T(8,128)S(1)}, u32[]{:S(2)}, u32[]{:S(2)}) collective-permute-start(f32[39,16,128]{2,1,0:T(8,128)S(1)} %get-tuple-element.59.send_ref), channel_id=1, source_target_pairs={{0,1},{1,0},{2,3},{3,2},{4,5},{5,4},{6,7},{7,6},{8,9},{9,8},{10,11... | collective-permute-start | bytes 958472 | tf_op jit(solution)/shard_map/ppermute | solution.py:798
